TPU v7x, 128 devices: a whole 4x4x4 slice. The times are simulated.
128 devices in a mesh: rows: 16 (over y_hi, x, core), inner: 8 (over z, y_lo).
Axes of the slice: x: 4, y: 4 (y_hi: 2, y_lo: 2; y = y_hi * 2 + y_lo), z: 4, core: 2. Of those that a mesh axis runs over, the one named last changes fastest.
Arguments:
- h_blocks: bfloat16 [64, 8, 128, 128], P('rows'), may hold values from -6 to 6
- h_cols: int32 [64, 8], P('rows'), may hold values from 0 to 63, as said below
- h_count: int32 [64], P('rows'), may hold values from 1 to 8, as said below
- z_blocks: bfloat16 [64, 8, 128, 128], P('rows'), may hold values from -0.1875 to 0.1875
- z_cols: int32 [64, 8], P('rows'), may hold values from 0 to 63, as said below
- z_count: int32 [64], P('rows'), may hold values from 1 to 8, as said below
- x_perp: bfloat16 [8192, 8192], P('rows', 'inner'), may hold values from -6 to 6
Outputs:
- h_perp: bfloat16 [8192, 8192], P('rows', 'inner')
- x_out: bfloat16 [8192, 8192], P('rows', 'inner')
Inputs may be any that keep to these rules, and one draw needn't show every extreme that they name: `h_cols`: slot s of every block row, live or padded, names a block column of stripe s, that is from (s) * 8 to (s + 1) * 8 - 1; a row may name a column twice. `z_cols`: slot s of every block row, live or padded, names a block column of stripe s, that is from (s) * 8 to (s + 1) * 8 - 1; a row may name a column twice. The live slots of block row i are slots 0 to h_count[i] - 1. The live slots of block row k are slots 0 to z_count[k] - 1.
All inputs are finite; a program needn't handle non-finite values.
Results may differ from a plain program's by a relative error of at most 0.0049.
Values may be sent and summed in bfloat16 or wider, within the bound.
No kernel may reach another device: no remote copies, remote signals or barrier semaphores. Data moves between devices by JAX's collectives and lax.ppermute only.
A program may use at most 192 MiB of HBM per device.

v0:
```python
import jax
import jax.numpy as jnp
from jax import lax
from jax.sharding import PartitionSpec as P


def masked(blocks, counts):
    live = jnp.arange(blocks.shape[1])[None, :] < counts[:, None]
    return jnp.where(live[:, :, None, None], blocks, jnp.zeros((), blocks.dtype))


def body(h_blocks, h_cols, h_count, z_blocks, z_cols, z_count, x_perp):
    rows_here = h_blocks.shape[0]
    slot_count = h_blocks.shape[1]
    edge = h_blocks.shape[2]
    inner_size = lax.axis_size("inner")
    slot_group = slot_count // inner_size
    stripe = x_perp.shape[1] // edge
    stripe_pos = lax.axis_index("inner")
    row_pos = lax.axis_index("rows")
    h_mask = masked(h_blocks, h_count)
    z_mask = masked(z_blocks, z_count)
    everything, every_col = (
        lax.all_gather(z_mask, "rows", axis=0, tiled=True),
        lax.all_gather(z_cols, "rows", axis=0, tiled=True),
    )
    shared = lax.dynamic_slice_in_dim(everything, stripe_pos * slot_group, slot_group, 1)
    shared_cols = lax.dynamic_slice_in_dim(every_col, stripe_pos * slot_group, slot_group, 1)
    local_cols = shared_cols - stripe_pos * stripe
    picked = jnp.take(shared, h_cols.reshape(-1), axis=0).reshape(
        rows_here, slot_count, slot_group, edge, edge
    )
    picked_cols = jnp.take(local_cols, h_cols.reshape(-1), axis=0).reshape(
        rows_here, slot_count, slot_group
    )
    products = jnp.einsum("ispq,istqr->istpr", h_mask, picked, preferred_element_type=jnp.float32)
    placing = (picked_cols[..., None] == jnp.arange(stripe)[None, None, None, :]).astype(
        jnp.float32
    )
    m_tile = jnp.einsum("istj,istpr->ipjr", placing, products, precision=lax.Precision.HIGHEST)
    m_tile = m_tile.reshape(rows_here * edge, stripe * edge).astype(jnp.bfloat16)
    owner_stripe = row_pos * rows_here // stripe
    stripe_blocks = lax.dynamic_slice_in_dim(everything, owner_stripe * slot_group, slot_group, 1)
    stripe_names = lax.dynamic_slice_in_dim(every_col, owner_stripe * slot_group, slot_group, 1)
    targets = row_pos * rows_here + jnp.arange(rows_here)
    portion = lax.all_gather(m_tile, "rows", axis=0, tiled=True)
    blocks = portion.shape[0] // edge
    segment = stripe_blocks
    segment_cols = stripe_names
    pieces = jnp.einsum(
        "ktpq,kpj->ktqj",
        segment,
        portion.reshape(blocks, edge, stripe * edge),
        preferred_element_type=jnp.float32,
    )
    matches = (segment_cols[:, :, None] == targets[None, None, :]).astype(jnp.float32)
    h_total = jnp.einsum("kti,ktqj->iqj", matches, pieces, precision=lax.Precision.HIGHEST).reshape(
        rows_here * edge, stripe * edge
    )
    h_perp = h_total.astype(jnp.bfloat16)
    panel_rows = rows_here * edge
    x_three = x_perp.reshape(panel_rows, stripe, edge)
    blocks = stripe * edge * lax.axis_size("inner") // edge
    segment = shared
    segment_cols = local_cols
    columns = jnp.take(x_three, segment_cols.reshape(-1), axis=1).reshape(
        panel_rows, blocks, slot_group, edge
    )
    result = jnp.einsum("ktqp,aktp->kqa", segment, columns, preferred_element_type=jnp.float32)
    coupled_sum = lax.psum_scatter(
        result.reshape(stripe * edge * lax.axis_size("inner"), panel_rows),
        "inner",
        scatter_dimension=0,
        tiled=True,
    )
    coupled_t = coupled_sum.astype(jnp.bfloat16)
    portion = lax.all_gather(coupled_t, "rows", axis=1, tiled=True)
    blocks = portion.shape[1] // edge
    matches = (z_cols[:, :, None] == jnp.arange(blocks)[None, None, :]).astype(jnp.bfloat16)
    chosen = jnp.einsum(
        "itb,kbp->itkp",
        matches,
        portion.reshape(portion.shape[0], blocks, edge),
        preferred_element_type=jnp.float32,
    )
    gathered = chosen.astype(jnp.bfloat16)
    x_tile = jnp.einsum("itqp,itkp->iqk", z_mask, gathered, preferred_element_type=jnp.float32)
    x_tile = x_tile.reshape(rows_here * edge, stripe * edge).astype(jnp.bfloat16)
    return (h_perp, x_tile)


def solution(mesh):
    in_specs = (
        P("rows", None, None, None),
        P("rows", None),
        P("rows"),
        P("rows", None, None, None),
        P("rows", None),
        P("rows"),
        P("rows", "inner"),
    )
    out_specs = (P("rows", "inner"), P("rows", "inner"))
    return jax.shard_map(body, mesh=mesh, in_specs=in_specs, out_specs=out_specs, check_vma=False)
```

profile of v0, /device:TPU:1, one launch (start us, length us, event | category | flops | bytes accessed | tf_op | source)
XLA Modules:
  0.0 733.8 jit_solution(8927628435772185918)
XLA Ops:
  7.2 0.7 iota_compare_fusion.3
  7.9 2.3 broadcast_select_fusion
  10.4 26.2 %all-gather = s32[16,4,8]{2,1,0:T(4,128)S(1)} all-gather(s32[1,4,8]{2,1,0:T(4,128)} %bitcast.73), channel_id=1, replica_groups=mesh['rows'=16,'inner'=8] {'rows'}, dimensions={0}, use_global_device_ids=true | all-gather | bytes 2176 | tf_op jit(solution)/shard_map/all_gather | solution.py:25
  36.7 1.5 copy.35
  38.9 5.6 gather_fusion.2
  44.5 80.4 %all-gather.5.cloned.1.call-done = bf16[64,8,128,128]{3,2,1,0:T(8,128)(2,1)} async-done(((bf16[4,8,128,128]{3,2,1,0:T(8,128)(2,1)}), bf16[64,8,128,128]{3,2,1,0:T(8,128)(2,1)}) %all-gather.5.cloned.1.call-update) | async-done | bytes 16777232 | tf_op jit(solution)/shard_map/all_gather | solution.py:24
  124.9 1.7 dynamic-slice_bitcast_fusion
  126.7 11.6 %fusion.2 = f32[64,128,512]{2,1,0:T(8,128)} fusion(bf16[64,128,128]{2,1,0:T(8,128)(2,1)S(1)} %dynamic-slice_bitcast_fusion, bf16[64,512,128]{2,1,0:T(8,128)(2,1)} %gather_fusion.2, pred[64]{0:T(512)(128)(4,1)S(1)} %get-tuple-element.2), kind=kOutput, calls=%fused_computation.5 | convolution fusion | flops 1077936128 | bytes 27263040 | tf_op jit(solution)/shard_map/ktqp,aktp->kqa/dot_general | solution.py:69
  139.9 1.7 gather_fusion
  141.5 1.6 copy.30
  143.1 2.1 convolution_bitcast_fusion
  145.3 1.9 copy.32
  147.2 2.7 convolution_convert_fusion.1
  149.8 1.2 copy.54
  151.3 310.9 %reduce-scatter.2.cloned.1.call-done = f32[1024,512]{1,0:T(8,128)} async-done(((f32[8192,512]{1,0:T(8,128)}), f32[1024,512]{1,0:T(8,128)}) %reduce-scatter.2.cloned.1.call-update) | async-done | bytes 2097168 | tf_op jit(solution)/shard_map/reduce_scatter | solution.py:70
  462.3 2.7 convert_element_type.35
  465.1 111.9 %all-gather.7.cloned.1.call-done = bf16[8192,1024]{1,0:T(8,128)(2,1)} async-done(((bf16[512,1024]{1,0:T(8,128)(2,1)}), bf16[8192,1024]{1,0:T(8,128)(2,1)}) %all-gather.7.cloned.1.call-update) | async-done | bytes 16777232 | tf_op jit(solution)/shard_map/all_gather | solution.py:46
  576.9 22.5 %fusion.9 = f32[64,128,1024]{2,1,0:T(8,128)} fusion(bf16[64,128,1024]{2,1,0:T(8,128)(2,1)} %bitcast.63, bf16[64,8,128,128]{3,2,1,0:T(8,128)(2,1)} %all-gather.5.cloned.1.call-done, s32[]{:T(128)S(6)} %select_n.73), kind=kOutput, calls=%fused_computation.13 | convolution fusion | flops 2147483648 | bytes 52428804 | tf_op jit(solution)/shard_map/ktpq,kpj->ktqj/dot_general | solution.py:50
  599.4 36.3 %fusion.14 = bf16[4,128,1024]{2,0,1:T(4,128)(2,1)S(1)} fusion(f32[64,128,1024]{2,1,0:T(8,128)} %fusion.9, s32[64]{0:T(128)S(1)} %bitcast.72, s32[4]{0:T(128)S(1)} %iota_add_fusion), kind=kOutput, calls=%fused_computation.20 | convolution fusion | flops 403177728 | bytes 34603280 | tf_op jit(solution)/shard_map/kti,ktqj->iqj/dot_general | solution.py:57
  635.7 1.3 copy.34
  637.0 63.1 %all-gather.9.cloned.1.call-done = bf16[1024,8192]{1,0:T(8,128)(2,1)} async-done(((bf16[1024,512]{1,0:T(8,128)(2,1)}), bf16[1024,8192]{1,0:T(8,128)(2,1)}) %all-gather.9.cloned.1.call-update) | async-done | bytes 16777232 | tf_op jit(solution)/shard_map/all_gather | solution.py:77
  700.1 15.1 %copy.44 = bf16[128,8,64,128]{3,2,1,0:T(8,128)(2,1)} copy(bf16[128,8,64,128]{3,1,2,0:T(8,128)(2,1)} %bitcast.64) | data formatting | bytes 33554432
  715.2 8.2 %convolution_convert_fusion = bf16[4,8,1024,128]{3,1,2,0:T(8,128)(2,1)S(1)} fusion(bf16[1024,64,128,1]{2,1,0,3:T(8,128)(2,1)} %bitcast.65, s32[4,8]{1,0:T(4,128)S(1)} %copy-done.2), kind=kOutput, calls=%fused_computation.11 | convolution fusion | flops 541067264 | bytes 25165952 | tf_op jit(solution)/shard_map/itb,kbp->itkp/dot_general | solution.py:80
  723.4 3.9 bitcast_convert_fusion
  (31 shorter events, 2.9 us)
Async XLA Ops:
  7.2 117.8 %all-gather.5.cloned.1.call-start = ((), (), s32[]{:S(2)}) async-start(), calls=%async_computation.1 | async-start | bytes 17825792 | tf_op jit(solution)/shard_map/all_gather | solution.py:24
  10.3 452.0 %reduce-scatter.2.cloned.1.call-start = ((), (), s32[]{:S(2)}) async-start(), calls=%async_computation.3 | async-start | bytes 18874368 | tf_op jit(solution)/shard_map/reduce_scatter | solution.py:70
  138.2 0.7 copy-start.1
  138.2 1.6 copy-start.3
  138.2 438.7 %all-gather.7.cloned.1.call-start = ((), (), s32[]{:S(2)}) async-start(), calls=%async_computation.2 | async-start | bytes 17825792 | tf_op jit(solution)/shard_map/all_gather | solution.py:46
  151.1 549.0 %all-gather.9.cloned.1.call-start = ((), (), s32[]{:S(2)}) async-start(), calls=%async_computation.4 | async-start | bytes 17825792 | tf_op jit(solution)/shard_map/all_gather | solution.py:77
  700.1 15.1 %copy-start.2 = (s32[4,8]{1,0:T(4,128)S(1)}, s32[4,8]{1,0:T(4,128)}, u32[]{:S(2)}) copy-start(s32[4,8]{1,0:T(4,128)} %param.11) | copy-start | bytes 388
  715.2 8.2 %copy-start = (bf16[4,8,128,128]{3,2,1,0:T(8,128)(2,1)S(1)}, bf16[4,8,128,128]{3,2,1,0:T(8,128)(2,1)}, u32[]{:S(2)}) copy-start(bf16[4,8,128,128]{3,2,1,0:T(8,128)(2,1)} %broadcast_select_fusion) | copy-start | bytes 3145732
Sparse Core Ops, SparseCore 0:
  11.0 113.8 all-gather.4
  138.4 323.8 reduce-scatter.1
  465.3 111.5 all-gather.6
  579.0 120.9 all-gather.8
where the time goes:
time: 734 us
  waiting for transfers between devices  566 us (77%)
  matrix products  87.2 us (12%)
  local copies, waits for them, and re-layouts  33.9 us (5%)
  blocking collectives  26.2 us (4%)
  between operations  13.9 us (2%)
    reduce_scatter x1, waiting for transfers between devices, body(): lax.psum_scatter(result.reshape(stripe * edge * lax.axis_size('inner'), p...  311 us
    all_gather x1, waiting for transfers between devices, body(): portion = lax.all_gather(m_tile, 'rows', axis=0, tiled=True)  112 us
    all_gather x1, waiting for transfers between devices, body(): lax.all_gather(z_mask, 'rows', axis=0, tiled=True)  80.4 us
    all_gather x1, waiting for transfers between devices, body(): portion = lax.all_gather(coupled_t, 'rows', axis=1, tiled=True)  63.1 us
    dot_general x1, matrix products, body(): jnp.einsum('kti,ktqj->iqj', matches, pieces, precision=lax.Precision.HIGH...  36.3 us
    all_gather x1, blocking collectives, body(): lax.all_gather(z_cols, 'rows', axis=0, tiled=True)  26.2 us
    dot_general x1, matrix products, body(): jnp.einsum('ktpq,kpj->ktqj', segment, portion.reshape(blocks, edge, strip...  22.5 us
    unnamed x13, local copies, waits for them, and re-layouts  18.6 us
  transfers between devices with their start and end apart: 4, of which 4 were waited for; matrix products, arithmetic and copies ran while one was open for 11% of the time, Pallas kernels for 0%

commit v1 on v0

v1 whole, which is shorter than its diff:
```python
import functools

import jax
import jax.numpy as jnp
from jax import lax
from jax.experimental import pallas as pl
from jax.experimental.pallas import tpu as pltpu
from jax.sharding import PartitionSpec as P

AXES = ("rows", "inner")
B = 128
BF = jnp.bfloat16
F32 = jnp.float32
VMEM_LIMIT = 48 * 1024 * 1024
ZC, HC, ZN, HN = 0, 8, 16, 17
PX, PYH, PP, PZ, PYL, PM, PC, PR = range(8)


def places():
    for yh in range(2):
        for x in range(4):
            for p in range(2):
                for z in range(4):
                    for yl in range(2):
                        yield yh, x, p, z, yl


def number(yh, x, p, z, yl):
    return (((yh * 4 + x % 4) * 2 + p) * 4 + z % 4) * 2 + yl


def send(value, to):
    return lax.ppermute(value, AXES, [(number(*at), number(*to(*at))) for at in places()])


def along_x(d):
    return lambda yh, x, p, z, yl: (yh, (x + d) % 4, p, z, yl)


def along_z(d):
    return lambda yh, x, p, z, yl: (yh, x, p, (z + d) % 4, yl)


def other_yh(yh, x, p, z, yl):
    return 1 - yh, x, p, z, yl


def other_yl(yh, x, p, z, yl):
    return yh, x, p, z, 1 - yl


def other_core(yh, x, p, z, yl):
    return yh, x, 1 - p, z, yl


def to_chip(dy, dx):
    return lambda yh, x, p, z, yl: ((yh + dy) % 2, (x + dx) % 4, p, z, yl)


def transposed(yh, x, p, z, yl):
    m, c = yh * 4 + x, z * 2 + yl
    return c // 4, c % 4, p, m // 2, m % 2


def pieces_of(rows):
    half = rows // 2
    out = []
    for pair in (0, 1):
        out += [(0, pair, 0, rows), (-1, pair, 0, rows), (1, pair, 0, rows), (2, pair, 0, half), (2, pair, half, half)]
    return out


def gather_chips(v, ring, pair):
    half = v.shape[0] // 2
    y = send(v, pair)
    out = []
    for w in (v, y):
        a = send(w, ring(1))
        b = send(w, ring(-1))
        a2 = send(a[:half], ring(1))
        b2 = send(b[half:], ring(-1))
        out += [w, a, b, a2, b2]
    return out


def vmem_call(kernel, scalars, arrays, out_shape, scratch, flops):
    whole = pl.BlockSpec(memory_space=pltpu.VMEM)
    many = isinstance(out_shape, (list, tuple))
    outs = list(out_shape) if many else [out_shape]
    size = sum(a.size * a.dtype.itemsize for a in list(arrays) + outs)
    return pl.pallas_call(
        kernel,
        out_shape=out_shape,
        grid_spec=pltpu.PrefetchScalarGridSpec(
            num_scalar_prefetch=len(scalars),
            grid=(),
            in_specs=[whole] * len(arrays),
            out_specs=[whole] * len(outs) if many else whole,
            scratch_shapes=scratch,
        ),
        compiler_params=pltpu.CompilerParams(vmem_limit_bytes=VMEM_LIMIT),
        cost_estimate=pl.CostEstimate(flops=flops, bytes_accessed=size, transcendentals=0),
    )(*scalars, *arrays)


def inner_stripe(pos, dz, dyl):
    return lax.rem(pos[PZ] + dz + 4, 4) * 2 + lax.rem(pos[PYL] + dyl, 2)


def chip_of(pos, dx, dyh):
    return lax.rem(pos[PYH] + dyh, 2) * 4 + lax.rem(pos[PX] + dx + 4, 4)


def coupled_kernel(pieces, table, pos, *refs):
    n = len(pieces)
    xs, (z_own, z_sib, out, lhs, rhs) = refs[:n], refs[n:]
    c, p = pos[PC], pos[PP]

    def one(source, core, j):
        row = c * 8 + core * 4 + j
        live = table[row, ZN]
        for ref, (dz, dyl, lo, size) in zip(xs, pieces):
            t = inner_stripe(pos, dz, dyl)
            col = table[row, ZC + t] - t * 8
            spot = (dz % 4) * 2 + dyl
            lhs[lo : lo + size, spot * B : spot * B + B] = ref[:, pl.ds(pl.multiple_of(col * B, B), B)]
            if lo == 0:
                block = source[j, t]
                rhs[:, spot * B : spot * B + B] = jnp.where(t < live, block, jnp.zeros_like(block))
        total = lax.dot_general(lhs[...], rhs[...], (((1,), (1,)), ((), ())), preferred_element_type=F32)
        out[:, pl.ds(pl.multiple_of((core * 4 + j) * B, B), B)] = total.astype(BF)

    @pl.loop(0, 4)
    def _(j):
        one(z_own, p, j)
        one(z_sib, 1 - p, j)


def x_out_kernel(pieces, table, pos, *refs):
    n = len(pieces)
    blocks, (z_own, z_sib, mine, theirs) = refs[:n], refs[n:]
    p, r = pos[PP], pos[PR]
    for source, acc, core_row in ((z_own, mine, r), (z_sib, theirs, r + 1 - 2 * p)):
        acc[...] = jnp.zeros_like(acc)

        @pl.loop(0, 4)
        def _(i):
            row = core_row * 4 + i
            live = table[row, ZN]
            here = pl.ds(pl.multiple_of(i * B, B), B)
            for ref, (dx, dyh, lo, size) in zip(blocks, pieces):
                t = chip_of(pos, dx, dyh)
                q = table[row, ZC + t] - t * 8 - p * 4 - lo // B

                @pl.when((t < live) & (q >= 0) & (q < size // B))
                def _():
                    rows = pl.ds(pl.multiple_of(q * B, B), B)
                    acc[here, :] += jnp.dot(source[i, t], ref[rows, :], preferred_element_type=F32)


def w_kernel(table, pos, z_own, z_sib, shared, out, acc):
    p, m, c = pos[PP], pos[PM], pos[PC]
    acc[...] = jnp.zeros_like(acc)
    for source, core in ((z_own, p), (z_sib, 1 - p)):
        for d in range(8):
            chip = chip_of(pos, -(d % 4), d // 4)

            @pl.loop(0, 4)
            def _(j):
                k = chip * 8 + core * 4 + j
                i = table[k, ZC + m] - m * 8 - p * 4
                col = table[k, HC + c] - c * 8

                @pl.when((m < table[k, ZN]) & (c < table[k, HN]) & (i >= 0) & (i < 4))
                def _():
                    term = lax.dot_general(
                        source[d, j],
                        shared[chip * 2 + core, 4 + j],
                        (((0,), (0,)), ((), ())),
                        preferred_element_type=F32,
                    )
                    acc[pl.ds(pl.multiple_of(i * B, B), B), pl.ds(pl.multiple_of(col * B, B), B)] += term

    out[...] = acc[...].astype(BF)


def h_perp_kernel(pieces, table, pos, *refs):
    n = len(pieces)
    blocks, (shared, out, acc) = refs[:n], refs[n:]
    c = pos[PC]
    acc[...] = jnp.zeros_like(acc)

    @pl.loop(0, 8)
    def _(j):
        for ref, (dz, dyl, lo, size) in zip(blocks, pieces):
            t = inner_stripe(pos, dz, dyl)
            row = t * 8 + j
            col = table[row, ZC + c] - c * 8

            @pl.when(c < table[row, ZN])
            def _():
                term = jnp.dot(
                    ref[:, pl.ds(pl.multiple_of(j * B, B), B)],
                    shared[row // 4, lax.rem(row, 4)],
                    preferred_element_type=F32,
                )
                acc[lo : lo + size, pl.ds(pl.multiple_of(col * B, B), B)] += term

    out[...] = acc[...].astype(BF)


def body(h_blocks, h_cols, h_count, z_blocks, z_cols, z_count, x_perp):
    r, c = lax.axis_index("rows"), lax.axis_index("inner")
    m, p = r // 2, r % 2
    yh, x, z, yl = m // 4, m % 4, c // 2, c % 2
    pos = jnp.stack([x, yh, p, z, yl, m, c, r]).astype(jnp.int32)

    mine = jnp.concatenate([z_cols, h_cols, z_count[:, None], h_count[:, None]], axis=1)
    table = lax.dynamic_update_slice(jnp.zeros((64, 18), jnp.int32), mine, (r * 4, 0))
    table = table + send(table, other_core)
    table = table + send(table, other_yh)
    table = table + (send(table, along_x(1)) + send(table, along_x(-1)) + send(table, along_x(2)))

    x_pieces = gather_chips(x_perp, along_z, other_yl)
    z_stripe = send(z_blocks, transposed)
    z_stripe_sib = send(z_stripe, other_core)
    z_sib = send(z_blocks, other_core)

    slot_c = jnp.concatenate(
        [lax.dynamic_index_in_dim(v, c, 1, keepdims=False) for v in (z_blocks, h_blocks)], axis=0
    )
    shared = lax.all_gather(slot_c[None], "rows", axis=0, tiled=True)
    named = []
    for d in range(8):
        dy, dx = d // 4, d % 4
        slot = (yh + dy) % 2 * 4 + (x + dx) % 4
        block = lax.dynamic_index_in_dim(z_blocks, slot, 1, keepdims=False)
        named.append(send(block, to_chip(dy, dx)) if d else block)
    named = jnp.stack(named)
    named_sib = send(named, other_core)

    tile = jax.ShapeDtypeStruct((512, 1024), BF)
    wide = jax.ShapeDtypeStruct((512, 1024), F32)
    pieces = pieces_of(512)
    dense = 2 * 64 * 512 * B * B
    w_tile = vmem_call(
        w_kernel, (table, pos), (named, named_sib, shared), tile, [pltpu.VMEM((512, 1024), F32)], dense // 4
    )
    coupled = vmem_call(
        functools.partial(coupled_kernel, pieces),
        (table, pos),
        (*x_pieces, z_stripe, z_stripe_sib),
        tile,
        [pltpu.VMEM((512, 1024), BF), pltpu.VMEM((B, 1024), BF)],
        dense,
    )
    c_pieces = gather_chips(coupled, along_x, other_yh)
    w_pieces = gather_chips(w_tile, along_z, other_yl)
    x_mine, x_theirs = vmem_call(
        functools.partial(x_out_kernel, pieces), (table, pos), (*c_pieces, z_blocks, z_sib), [wide, wide], [], dense
    )
    x_tile = (x_mine + send(x_theirs, other_core)).astype(BF)
    h_tile = vmem_call(
        functools.partial(h_perp_kernel, pieces),
        (table, pos),
        (*w_pieces, shared),
        tile,
        [pltpu.VMEM((512, 1024), F32)],
        dense,
    )
    return h_tile, x_tile


def solution(mesh):
    in_specs = (
        P("rows", None, None, None),
        P("rows", None),
        P("rows"),
        P("rows", None, None, None),
        P("rows", None),
        P("rows"),
        P("rows", "inner"),
    )
    out_specs = (P("rows", "inner"), P("rows", "inner"))
    return jax.shard_map(body, mesh=mesh, in_specs=in_specs, out_specs=out_specs, check_vma=False)
```

time: 734 us -> 339 us (0.46)
  waiting for transfers between devices: 566 us -> 175 us
  matrix products: 87.2 us -> 0 us
  starting transfers between devices: 0.34 us -> 78.3 us
  Pallas kernels: 0 us -> 49.9 us
  blocking collectives: 26.2 us -> 0 us
  local copies, waits for them, and re-layouts: 33.9 us -> 17.8 us
    reduce_scatter x1 -> x0, waiting for transfers between devices: 311 us -> none  [body(): lax.psum_scatter(result.reshape(stripe * edge * lax.axis_size('inner'), p...]
    all_gather x3 -> x1, waiting for transfers between devices: 255 us -> 0.01 us  [body(): shared = lax.all_gather(slot_c[None], 'rows', axis=0, tiled=True)]
    ppermute x0 -> x44, waiting for transfers between devices: none -> 175 us  [send(): lax.ppermute(value, AXES, [(number(*at), number(*to(*at))) for at in plac...]
    dot_general x7 -> x0, matrix products: 87.2 us -> none  [the longest x1 36.3 us: body(): jnp.einsum('kti,ktqj->iqj', matches, pieces, precision=lax.Precision.HIGH...]
    ppermute x0 -> x44, starting transfers between devices: none -> 78.3 us  [send(): lax.ppermute(value, AXES, [(number(*at), number(*to(*at))) for at in plac...]
    pallas_call x0 -> x4, Pallas kernels: none -> 49.9 us  [vmem_call(): pl.pallas_call(kernel, out_shape=out_shape, grid_spec=pltpu.PrefetchScala...]
    all_gather x1 -> x0, blocking collectives: 26.2 us -> none  [body(): lax.all_gather(z_cols, 'rows', axis=0, tiled=True)]
    unnamed x13 -> x47, local copies, waits for them, and re-layouts: 18.6 us -> 7.69 us
  transfers between devices with their start and end apart: 4 -> 45, of which waited for: 4 -> 13; matrix products, arithmetic and copies ran while one was open for 11% -> 3% of each run, Pallas kernels for 0% -> 9%
where the time goes in v1:
time: 339 us; the launch traced here: 337 us
  waiting for transfers between devices  175 us (52%)
  starting transfers between devices  78.3 us (23%)
  Pallas kernels  49.9 us (15%)
  local copies, waits for them, and re-layouts  17.8 us (5%)
  between operations  14.6 us (4%)
    ppermute x44, waiting for transfers between devices, send(): lax.ppermute(value, AXES, [(number(*at), number(*to(*at))) for at in plac...  175 us
    ppermute x44, starting transfers between devices, send(): lax.ppermute(value, AXES, [(number(*at), number(*to(*at))) for at in plac...  78.3 us
    pallas_call x4, Pallas kernels, vmem_call(): pl.pallas_call(kernel, out_shape=out_shape, grid_spec=pltpu.PrefetchScala...  49.9 us
    unnamed x47, local copies, waits for them, and re-layouts  7.69 us
  transfers between devices with their start and end apart: 45, of which 13 were waited for; matrix products, arithmetic and copies ran while one was open for 3% of the time, Pallas kernels for 9%

profile of v1, /device:TPU:1, one launch (start us, length us, event | category | flops | bytes accessed | tf_op | source)
XLA Modules:
  0.0 337.4 jit_solution(13654291931122520801)
XLA Ops:
  13.5 9.5 %collective-permute-start.31 = (bf16[4,8,128,128]{3,2,1,0:T(8,128)(2,1)}, bf16[4,8,128,128]{3,2,1,0:T(8,128)(2,1)}, u32[]{:S(2)}, u32[]{:S(2)}) collective-permute-start(bf16[4,8,128,128]{3,2,1,0:T(8,128)(2,1)} %refs_10_.1), channel_id=1, source_target_pairs={{0,0},{1,16},{2,32},{3,48},{4,64},{5,80},{6,96},{7,112},{8,8},{9,2... | collective-permute-start | bytes 3145736 | tf_op jit(solution)/shard_map/ppermute | solution.py:33
  27.0 56.1 %collective-permute-done.26.refs_5_ = bf16[512,1024]{1,0:T(8,128)(2,1)} collective-permute-done((bf16[512,1024]{1,0:T(8,128)(2,1)S(1)}, bf16[512,1024]{1,0:T(8,128)(2,1)}, u32[]{:S(2)}, u32[]{:S(2)}) %collective-permute-start.26) | collective-permute-done | bytes 1048608 | tf_op jit(solution)/shard_map/ppermute | solution.py:33
  83.1 3.8 %collective-permute-done.1 = s32[64,18]{1,0:T(8,128)S(1)} collective-permute-done((s32[64,18]{1,0:T(8,128)S(1)}, s32[64,18]{1,0:T(8,128)S(1)}, u32[]{:S(2)}, u32[]{:S(2)}) %collective-permute-start.1) | collective-permute-done | bytes 4640 | tf_op jit(solution)/shard_map/ppermute | solution.py:33
  86.9 3.6 %collective-permute-start.32 = (bf16[4,8,128,128]{3,2,1,0:T(8,128)(2,1)}, bf16[4,8,128,128]{3,2,1,0:T(8,128)(2,1)}, u32[]{:S(2)}, u32[]{:S(2)}) collective-permute-start(bf16[4,8,128,128]{3,2,1,0:T(8,128)(2,1)} %collective-permute-done.31.refs_10_), channel_id=1, source_target_pairs={{0,8},{1,9},{2,10},{3,11},{4,12},{5,13},{6,14},{7,15},{8,0},{9,1},... | collective-permute-start | bytes 3145736 | tf_op jit(solution)/shard_map/ppermute | solution.py:33
  91.4 3.5 %collective-permute-done.2 = s32[64,18]{1,0:T(8,128)S(1)} collective-permute-done((s32[64,18]{1,0:T(8,128)S(1)}, s32[64,18]{1,0:T(8,128)S(1)}, u32[]{:S(2)}, u32[]{:S(2)}) %collective-permute-start.2) | collective-permute-done | bytes 4640 | tf_op jit(solution)/shard_map/ppermute | solution.py:33
  99.4 10.9 %collective-permute-done.27.refs_6_ = bf16[512,1024]{1,0:T(8,128)(2,1)} collective-permute-done((bf16[512,1024]{1,0:T(8,128)(2,1)}, bf16[512,1024]{1,0:T(8,128)(2,1)}, u32[]{:S(2)}, u32[]{:S(2)}) %collective-permute-start.27) | collective-permute-done | bytes 1048608 | tf_op jit(solution)/shard_map/ppermute | solution.py:33
  110.2 3.4 collective-permute-start.4
  116.9 3.5 %collective-permute-start.25 = (bf16[256,1024]{1,0:T(8,128)(2,1)S(1)}, bf16[256,1024]{1,0:T(8,128)(2,1)S(1)}, u32[]{:S(2)}, u32[]{:S(2)}) collective-permute-start(bf16[256,1024]{1,0:T(8,128)(2,1)S(1)} %slice.53), channel_id=1, source_target_pairs={{0,6},{1,7},{2,0},{3,1},{4,2},{5,3},{6,4},{7,5},{8,14},{9,15},{10,... | collective-permute-start | bytes 1572872 | tf_op jit(solution)/shard_map/ppermute | solution.py:33
  131.5 6.4 %collective-permute-done.30.refs_9_ = bf16[256,1024]{1,0:T(8,128)(2,1)S(1)} collective-permute-done((bf16[256,1024]{1,0:T(8,128)(2,1)S(1)}, bf16[256,1024]{1,0:T(8,128)(2,1)S(1)}, u32[]{:S(2)}, u32[]{:S(2)}) %collective-permute-start.30) | collective-permute-done | bytes 524320 | tf_op jit(solution)/shard_map/ppermute | solution.py:33
  139.2 8.6 %shard_map.88.refs_0_ = bf16[512,1024]{1,0:T(8,128)(2,1)S(1)} custom-call(s32[64,18]{1,0:T(8,128)S(1)} %add_add_fusion.table, s32[8]{0:T(128)S(1)} %stack.62.pos, bf16[512,1024]{1,0:T(8,128)(2,1)S(1)} %copy-done.6, bf16[512,1024]{1,0:T(8,128)(2,1)S(1)} %collective-permute-done.22.refs_1_, bf16[512,1024]{1,0:T(8,128)(2,1)} %collective-permute-done.23.refs_2_, ...), custom_call_target="tpu_custom_call" | custom-call | flops 1073741824 | bytes 11534336 | tf_op jit(solution)/shard_map/pallas_call | solution.py:91
  150.9 4.0 %collective-permute-start.11 = (bf16[4,128,128]{2,1,0:T(8,128)(2,1)S(1)}, bf16[4,128,128]{2,1,0:T(8,128)(2,1)S(1)}, u32[]{:S(2)}, u32[]{:S(2)}) collective-permute-start(bf16[4,128,128]{2,1,0:T(8,128)(2,1)S(1)} %get-tuple-element.9), channel_id=1, source_target_pairs={{0,112},{1,113},{2,114},{3,115},{4,116},{5,117},{6,118},{7,119},{8... | collective-permute-start | bytes 393224 | tf_op jit(solution)/shard_map/ppermute | solution.py:33
  157.8 13.8 %collective-permute-done.37.refs_5_ = bf16[512,1024]{1,0:T(8,128)(2,1)S(1)} collective-permute-done((bf16[512,1024]{1,0:T(8,128)(2,1)S(1)}, bf16[512,1024]{1,0:T(8,128)(2,1)S(1)}, u32[]{:S(2)}, u32[]{:S(2)}) %collective-permute-start.37) | collective-permute-done | bytes 1048608 | tf_op jit(solution)/shard_map/ppermute | solution.py:33
  171.6 4.3 %collective-permute-start.38 = (bf16[512,1024]{1,0:T(8,128)(2,1)S(1)}, bf16[512,1024]{1,0:T(8,128)(2,1)S(1)}, u32[]{:S(2)}, u32[]{:S(2)}) collective-permute-start(bf16[512,1024]{1,0:T(8,128)(2,1)S(1)} %collective-permute-done.37.refs_5_), channel_id=1, source_target_pairs={{0,16},{1,17},{2,18},{3,19},{4,20},{5,21},{6,22},{7,23},{8,24},{9,... | collective-permute-start | bytes 3145736 | tf_op jit(solution)/shard_map/ppermute | solution.py:33
  177.9 4.5 %collective-permute-start.12 = (bf16[8,4,128,128]{3,2,1,0:T(8,128)(2,1)S(1)}, bf16[8,4,128,128]{3,2,1,0:T(8,128)(2,1)S(1)}, u32[]{:S(2)}, u32[]{:S(2)}) collective-permute-start(bf16[8,4,128,128]{3,2,1,0:T(8,128)(2,1)S(1)} %bitcast_dynamic-update-slice_fusion.z_own), channel_id=1, source_target_pairs={{0,8},{1,9},{2,10},{3,11},{4,12},{5,13},{6,14},{7,15},{8,0},{9,1},... | collective-permute-start | bytes 3145736 | tf_op jit(solution)/shard_map/ppermute | solution.py:33
  186.8 14.8 %collective-permute-done.38.refs_6_ = bf16[512,1024]{1,0:T(8,128)(2,1)S(1)} collective-permute-done((bf16[512,1024]{1,0:T(8,128)(2,1)S(1)}, bf16[512,1024]{1,0:T(8,128)(2,1)S(1)}, u32[]{:S(2)}, u32[]{:S(2)}) %collective-permute-start.38) | collective-permute-done | bytes 1048608 | tf_op jit(solution)/shard_map/ppermute | solution.py:33
  209.6 10.1 %shard_map.86.refs_0_ = bf16[512,1024]{1,0:T(8,128)(2,1)S(1)} custom-call(s32[64,18]{1,0:T(8,128)S(1)} %add_add_fusion.table, s32[8]{0:T(128)S(1)} %stack.62.pos, bf16[8,4,128,128]{3,2,1,0:T(8,128)(2,1)S(1)} %copy-done.4, bf16[8,4,128,128]{3,2,1,0:T(8,128)(2,1)S(1)} %copy-done.8, bf16[16,8,128,128]{3,2,1,0:T(8,128)(2,1)} %bitcast.45), custom_call_target="tpu_custom_call" | custom-call | flops 268435456 | bytes 7340032 | tf_op jit(solution)/shard_map/pallas_call | solution.py:91
  219.8 4.4 %collective-permute-done.40.refs_8_ = bf16[256,1024]{1,0:T(8,128)(2,1)} collective-permute-done((bf16[256,1024]{1,0:T(8,128)(2,1)}, bf16[256,1024]{1,0:T(8,128)(2,1)}, u32[]{:S(2)}, u32[]{:S(2)}) %collective-permute-start.40) | collective-permute-done | bytes 524320 | tf_op jit(solution)/shard_map/ppermute | solution.py:33
  224.2 10.9 %shard_map.89 = (f32[512,1024]{1,0:T(8,128)}, f32[512,1024]{1,0:T(8,128)}) custom-call(s32[64,18]{1,0:T(8,128)S(1)} %add_add_fusion.table, s32[8]{0:T(128)S(1)} %stack.62.pos, bf16[512,1024]{1,0:T(8,128)(2,1)S(1)} %shard_map.88.refs_0_, bf16[512,1024]{1,0:T(8,128)(2,1)S(1)} %collective-permute-done.33.refs_1_, bf16[512,1024]{1,0:T(8,128)(2,1)S(1)} %copy-done.2, ...), custom_call_target="tpu_custom_call" | custom-call | flops 1073741824 | bytes 14680064 | tf_op jit(solution)/shard_map/pallas_call | solution.py:91
  235.1 4.2 %collective-permute-start.43 = (f32[512,1024]{1,0:T(8,128)}, f32[512,1024]{1,0:T(8,128)S(1)}, u32[]{:S(2)}, u32[]{:S(2)}) collective-permute-start(f32[512,1024]{1,0:T(8,128)} %get-tuple-element.5), channel_id=1, source_target_pairs={{0,8},{1,9},{2,10},{3,11},{4,12},{5,13},{6,14},{7,15},{8,0},{9,1},... | collective-permute-start | bytes 6291464 | tf_op jit(solution)/shard_map/ppermute | solution.py:33
  244.7 20.6 %collective-permute-done.13.refs_1_ = bf16[512,1024]{1,0:T(8,128)(2,1)S(1)} collective-permute-done((bf16[512,1024]{1,0:T(8,128)(2,1)S(1)}, bf16[512,1024]{1,0:T(8,128)(2,1)S(1)}, u32[]{:S(2)}, u32[]{:S(2)}) %collective-permute-start.13) | collective-permute-done | bytes 1048608 | tf_op jit(solution)/shard_map/ppermute | solution.py:33
  268.2 19.6 %collective-permute-done.18.refs_6_ = bf16[512,1024]{1,0:T(8,128)(2,1)S(1)} collective-permute-done((bf16[512,1024]{1,0:T(8,128)(2,1)S(1)}, bf16[512,1024]{1,0:T(8,128)(2,1)S(1)}, u32[]{:S(2)}, u32[]{:S(2)}) %collective-permute-start.18) | collective-permute-done | bytes 1048608 | tf_op jit(solution)/shard_map/ppermute | solution.py:33
  292.0 7.0 %collective-permute-done.15.refs_3_ = bf16[256,1024]{1,0:T(8,128)(2,1)S(1)} collective-permute-done((bf16[256,1024]{1,0:T(8,128)(2,1)S(1)}, bf16[256,1024]{1,0:T(8,128)(2,1)S(1)}, u32[]{:S(2)}, u32[]{:S(2)}) %collective-permute-start.15) | collective-permute-done | bytes 524320 | tf_op jit(solution)/shard_map/ppermute | solution.py:33
  299.0 11.2 %collective-permute-done.20.refs_8_ = bf16[256,1024]{1,0:T(8,128)(2,1)S(1)} collective-permute-done((bf16[256,1024]{1,0:T(8,128)(2,1)S(1)}, bf16[256,1024]{1,0:T(8,128)(2,1)S(1)}, u32[]{:S(2)}, u32[]{:S(2)}) %collective-permute-start.20) | collective-permute-done | bytes 524320 | tf_op jit(solution)/shard_map/ppermute | solution.py:33
  310.2 20.3 %shard_map.87 = bf16[512,1024]{1,0:T(8,128)(2,1)} custom-call(s32[64,18]{1,0:T(8,128)S(1)} %add_add_fusion.table, s32[8]{0:T(128)S(1)} %stack.62.pos, bf16[512,1024]{1,0:T(8,128)(2,1)S(1)} %shard_map.86.refs_0_, bf16[512,1024]{1,0:T(8,128)(2,1)S(1)} %collective-permute-done.13.refs_1_, bf16[512,1024]{1,0:T(8,128)(2,1)S(1)} %collective-permute-done.14.refs_2_, ...), custom_call_target="tpu_custom_call" | custom-call | flops 1073741824 | bytes 13631488 | tf_op jit(solution)/shard_map/pallas_call | solution.py:91
  (143 shorter events, 63.8 us)
Async XLA Ops:
  7.2 199.9 %all-gather.3.cloned.1.call-start = ((), (), s32[]{:S(2)}) async-start(), calls=%async_computation | async-start | bytes 4456448 | tf_op jit(solution)/shard_map/all_gather | solution.py:232
  11.3 71.8 %collective-permute-start.26 = (bf16[512,1024]{1,0:T(8,128)(2,1)S(1)}, bf16[512,1024]{1,0:T(8,128)(2,1)}, u32[]{:S(2)}, u32[]{:S(2)}) collective-permute-start(bf16[512,1024]{1,0:T(8,128)(2,1)S(1)} %copy-done.5), channel_id=1, source_target_pairs={{0,1},{1,0},{2,3},{3,2},{4,5},{5,4},{6,7},{7,6},{8,9},{9,8},{10,11... | collective-permute-start | bytes 3145736 | tf_op jit(solution)/shard_map/ppermute | solution.py:33
  13.5 73.4 %collective-permute-start.31 = (bf16[4,8,128,128]{3,2,1,0:T(8,128)(2,1)}, bf16[4,8,128,128]{3,2,1,0:T(8,128)(2,1)}, u32[]{:S(2)}, u32[]{:S(2)}) collective-permute-start(bf16[4,8,128,128]{3,2,1,0:T(8,128)(2,1)} %refs_10_.1), channel_id=1, source_target_pairs={{0,0},{1,16},{2,32},{3,48},{4,64},{5,80},{6,96},{7,112},{8,8},{9,2... | collective-permute-start | bytes 3145736 | tf_op jit(solution)/shard_map/ppermute | solution.py:33
  24.2 66.3 %collective-permute-start.22 = (bf16[512,1024]{1,0:T(8,128)(2,1)S(1)}, bf16[512,1024]{1,0:T(8,128)(2,1)S(1)}, u32[]{:S(2)}, u32[]{:S(2)}) collective-permute-start(bf16[512,1024]{1,0:T(8,128)(2,1)S(1)} %copy-done.5), channel_id=1, source_target_pairs={{0,2},{1,3},{2,4},{3,5},{4,6},{5,7},{6,0},{7,1},{8,10},{9,11},{10,... | collective-permute-start | bytes 3145736 | tf_op jit(solution)/shard_map/ppermute | solution.py:33
  24.2 73.0 %collective-permute-start.23 = (bf16[512,1024]{1,0:T(8,128)(2,1)S(1)}, bf16[512,1024]{1,0:T(8,128)(2,1)}, u32[]{:S(2)}, u32[]{:S(2)}) collective-permute-start(bf16[512,1024]{1,0:T(8,128)(2,1)S(1)} %copy-done.5), channel_id=1, source_target_pairs={{0,6},{1,7},{2,0},{3,1},{4,2},{5,3},{6,4},{7,5},{8,14},{9,15},{10,... | collective-permute-start | bytes 3145736 | tf_op jit(solution)/shard_map/ppermute | solution.py:33
  26.9 60.0 %collective-permute-start.1 = (s32[64,18]{1,0:T(8,128)S(1)}, s32[64,18]{1,0:T(8,128)S(1)}, u32[]{:S(2)}, u32[]{:S(2)}) collective-permute-start(s32[64,18]{1,0:T(8,128)S(1)} %constant_dynamic-update-slice_fusion), channel_id=1, source_target_pairs={{0,64},{1,65},{2,66},{3,67},{4,68},{5,69},{6,70},{7,71},{8,72},{9,... | collective-permute-start | bytes 13832 | tf_op jit(solution)/shard_map/ppermute | solution.py:33
  83.1 27.1 %collective-permute-start.27 = (bf16[512,1024]{1,0:T(8,128)(2,1)}, bf16[512,1024]{1,0:T(8,128)(2,1)}, u32[]{:S(2)}, u32[]{:S(2)}) collective-permute-start(bf16[512,1024]{1,0:T(8,128)(2,1)} %collective-permute-done.26.refs_5_), channel_id=1, source_target_pairs={{0,2},{1,3},{2,4},{3,5},{4,6},{5,7},{6,0},{7,1},{8,10},{9,11},{10,... | collective-permute-start | bytes 3145736 | tf_op jit(solution)/shard_map/ppermute | solution.py:33
  86.9 41.0 %collective-permute-start.32 = (bf16[4,8,128,128]{3,2,1,0:T(8,128)(2,1)}, bf16[4,8,128,128]{3,2,1,0:T(8,128)(2,1)}, u32[]{:S(2)}, u32[]{:S(2)}) collective-permute-start(bf16[4,8,128,128]{3,2,1,0:T(8,128)(2,1)} %collective-permute-done.31.refs_10_), channel_id=1, source_target_pairs={{0,8},{1,9},{2,10},{3,11},{4,12},{5,13},{6,14},{7,15},{8,0},{9,1},... | collective-permute-start | bytes 3145736 | tf_op jit(solution)/shard_map/ppermute | solution.py:33
  95.0 29.1 %collective-permute-start.24 = (bf16[256,1024]{1,0:T(8,128)(2,1)}, bf16[256,1024]{1,0:T(8,128)(2,1)}, u32[]{:S(2)}, u32[]{:S(2)}) collective-permute-start(bf16[256,1024]{1,0:T(8,128)(2,1)} %slice.52), channel_id=1, source_target_pairs={{0,2},{1,3},{2,4},{3,5},{4,6},{5,7},{6,0},{7,1},{8,10},{9,11},{10,... | collective-permute-start | bytes 1572872 | tf_op jit(solution)/shard_map/ppermute | solution.py:33
  127.9 27.0 %collective-permute-start.8 = (bf16[4,128,128]{2,1,0:T(8,128)(2,1)}, bf16[4,128,128]{2,1,0:T(8,128)(2,1)S(1)}, u32[]{:S(2)}, u32[]{:S(2)}) collective-permute-start(bf16[4,128,128]{2,1,0:T(8,128)(2,1)} %get-tuple-element.12), channel_id=1, source_target_pairs={{0,64},{1,65},{2,66},{3,67},{4,68},{5,69},{6,70},{7,71},{8,72},{9,... | collective-permute-start | bytes 393224 | tf_op jit(solution)/shard_map/ppermute | solution.py:33
  150.9 27.0 %collective-permute-start.11 = (bf16[4,128,128]{2,1,0:T(8,128)(2,1)S(1)}, bf16[4,128,128]{2,1,0:T(8,128)(2,1)S(1)}, u32[]{:S(2)}, u32[]{:S(2)}) collective-permute-start(bf16[4,128,128]{2,1,0:T(8,128)(2,1)S(1)} %get-tuple-element.9), channel_id=1, source_target_pairs={{0,112},{1,113},{2,114},{3,115},{4,116},{5,117},{6,118},{7,119},{8... | collective-permute-start | bytes 393224 | tf_op jit(solution)/shard_map/ppermute | solution.py:33
  154.9 27.4 %collective-permute-start.33 = (bf16[512,1024]{1,0:T(8,128)(2,1)S(1)}, bf16[512,1024]{1,0:T(8,128)(2,1)S(1)}, u32[]{:S(2)}, u32[]{:S(2)}) collective-permute-start(bf16[512,1024]{1,0:T(8,128)(2,1)S(1)} %shard_map.88.refs_0_), channel_id=1, source_target_pairs={{0,16},{1,17},{2,18},{3,19},{4,20},{5,21},{6,22},{7,23},{8,24},{9,... | collective-permute-start | bytes 3145736 | tf_op jit(solution)/shard_map/ppermute | solution.py:33
  155.1 29.8 %collective-permute-start.34 = (bf16[512,1024]{1,0:T(8,128)(2,1)S(1)}, bf16[512,1024]{1,0:T(8,128)(2,1)S(1)}, u32[]{:S(2)}, u32[]{:S(2)}) collective-permute-start(bf16[512,1024]{1,0:T(8,128)(2,1)S(1)} %shard_map.88.refs_0_), channel_id=1, source_target_pairs={{0,48},{1,49},{2,50},{3,51},{4,52},{5,53},{6,54},{7,55},{8,56},{9,... | collective-permute-start | bytes 3145736 | tf_op jit(solution)/shard_map/ppermute | solution.py:33
  171.6 30.0 %collective-permute-start.38 = (bf16[512,1024]{1,0:T(8,128)(2,1)S(1)}, bf16[512,1024]{1,0:T(8,128)(2,1)S(1)}, u32[]{:S(2)}, u32[]{:S(2)}) collective-permute-start(bf16[512,1024]{1,0:T(8,128)(2,1)S(1)} %collective-permute-done.37.refs_5_), channel_id=1, source_target_pairs={{0,16},{1,17},{2,18},{3,19},{4,20},{5,21},{6,22},{7,23},{8,24},{9,... | collective-permute-start | bytes 3145736 | tf_op jit(solution)/shard_map/ppermute | solution.py:33
  175.9 26.6 %collective-permute-start.39 = (bf16[512,1024]{1,0:T(8,128)(2,1)S(1)}, bf16[512,1024]{1,0:T(8,128)(2,1)S(1)}, u32[]{:S(2)}, u32[]{:S(2)}) collective-permute-start(bf16[512,1024]{1,0:T(8,128)(2,1)S(1)} %collective-permute-done.37.refs_5_), channel_id=1, source_target_pairs={{0,48},{1,49},{2,50},{3,51},{4,52},{5,53},{6,54},{7,55},{8,56},{9,... | collective-permute-start | bytes 3145736 | tf_op jit(solution)/shard_map/ppermute | solution.py:33
  177.9 26.9 %collective-permute-start.12 = (bf16[8,4,128,128]{3,2,1,0:T(8,128)(2,1)S(1)}, bf16[8,4,128,128]{3,2,1,0:T(8,128)(2,1)S(1)}, u32[]{:S(2)}, u32[]{:S(2)}) collective-permute-start(bf16[8,4,128,128]{3,2,1,0:T(8,128)(2,1)S(1)} %bitcast_dynamic-update-slice_fusion.z_own), channel_id=1, source_target_pairs={{0,8},{1,9},{2,10},{3,11},{4,12},{5,13},{6,14},{7,15},{8,0},{9,1},... | collective-permute-start | bytes 3145736 | tf_op jit(solution)/shard_map/ppermute | solution.py:33
  182.4 37.3 %collective-permute-start.42 = (bf16[4,8,128,128]{3,2,1,0:T(8,128)(2,1)}, bf16[4,8,128,128]{3,2,1,0:T(8,128)(2,1)}, u32[]{:S(2)}, u32[]{:S(2)}) collective-permute-start(bf16[4,8,128,128]{3,2,1,0:T(8,128)(2,1)} %refs_10_.1), channel_id=1, source_target_pairs={{0,8},{1,9},{2,10},{3,11},{4,12},{5,13},{6,14},{7,15},{8,0},{9,1},... | collective-permute-start | bytes 3145736 | tf_op jit(solution)/shard_map/ppermute | solution.py:33
  184.9 34.9 %collective-permute-start.35 = (bf16[256,1024]{1,0:T(8,128)(2,1)}, bf16[256,1024]{1,0:T(8,128)(2,1)}, u32[]{:S(2)}, u32[]{:S(2)}) collective-permute-start(bf16[256,1024]{1,0:T(8,128)(2,1)} %slice.56), channel_id=1, source_target_pairs={{0,16},{1,17},{2,18},{3,19},{4,20},{5,21},{6,22},{7,23},{8,24},{9,... | collective-permute-start | bytes 1572872 | tf_op jit(solution)/shard_map/ppermute | solution.py:33
  235.1 55.5 %collective-permute-start.43 = (f32[512,1024]{1,0:T(8,128)}, f32[512,1024]{1,0:T(8,128)S(1)}, u32[]{:S(2)}, u32[]{:S(2)}) collective-permute-start(f32[512,1024]{1,0:T(8,128)} %get-tuple-element.5), channel_id=1, source_target_pairs={{0,8},{1,9},{2,10},{3,11},{4,12},{5,13},{6,14},{7,15},{8,0},{9,1},... | collective-permute-start | bytes 6291464 | tf_op jit(solution)/shard_map/ppermute | solution.py:33
  239.4 26.0 %collective-permute-start.14 = (bf16[512,1024]{1,0:T(8,128)(2,1)S(1)}, bf16[512,1024]{1,0:T(8,128)(2,1)S(1)}, u32[]{:S(2)}, u32[]{:S(2)}) collective-permute-start(bf16[512,1024]{1,0:T(8,128)(2,1)S(1)} %shard_map.86.refs_0_), channel_id=1, source_target_pairs={{0,6},{1,7},{2,0},{3,1},{4,2},{5,3},{6,4},{7,5},{8,14},{9,15},{10,... | collective-permute-start | bytes 3145736 | tf_op jit(solution)/shard_map/ppermute | solution.py:33
  242.0 45.7 %collective-permute-start.18 = (bf16[512,1024]{1,0:T(8,128)(2,1)S(1)}, bf16[512,1024]{1,0:T(8,128)(2,1)S(1)}, u32[]{:S(2)}, u32[]{:S(2)}) collective-permute-start(bf16[512,1024]{1,0:T(8,128)(2,1)S(1)} %collective-permute-done.17.refs_5_), channel_id=1, source_target_pairs={{0,2},{1,3},{2,4},{3,5},{4,6},{5,7},{6,0},{7,1},{8,10},{9,11},{10,... | collective-permute-start | bytes 3145736 | tf_op jit(solution)/shard_map/ppermute | solution.py:33
  242.1 45.8 %collective-permute-start.19 = (bf16[512,1024]{1,0:T(8,128)(2,1)S(1)}, bf16[512,1024]{1,0:T(8,128)(2,1)S(1)}, u32[]{:S(2)}, u32[]{:S(2)}) collective-permute-start(bf16[512,1024]{1,0:T(8,128)(2,1)S(1)} %collective-permute-done.17.refs_5_), channel_id=1, source_target_pairs={{0,6},{1,7},{2,0},{3,1},{4,2},{5,3},{6,4},{7,5},{8,14},{9,15},{10,... | collective-permute-start | bytes 3145736 | tf_op jit(solution)/shard_map/ppermute | solution.py:33
  265.3 33.7 %collective-permute-start.15 = (bf16[256,1024]{1,0:T(8,128)(2,1)S(1)}, bf16[256,1024]{1,0:T(8,128)(2,1)S(1)}, u32[]{:S(2)}, u32[]{:S(2)}) collective-permute-start(bf16[256,1024]{1,0:T(8,128)(2,1)S(1)} %slice.48), channel_id=1, source_target_pairs={{0,2},{1,3},{2,4},{3,5},{4,6},{5,7},{6,0},{7,1},{8,10},{9,11},{10,... | collective-permute-start | bytes 1572872 | tf_op jit(solution)/shard_map/ppermute | solution.py:33
  265.5 33.5 %collective-permute-start.16 = (bf16[256,1024]{1,0:T(8,128)(2,1)S(1)}, bf16[256,1024]{1,0:T(8,128)(2,1)S(1)}, u32[]{:S(2)}, u32[]{:S(2)}) collective-permute-start(bf16[256,1024]{1,0:T(8,128)(2,1)S(1)} %slice.49), channel_id=1, source_target_pairs={{0,6},{1,7},{2,0},{3,1},{4,2},{5,3},{6,4},{7,5},{8,14},{9,15},{10,... | collective-permute-start | bytes 1572872 | tf_op jit(solution)/shard_map/ppermute | solution.py:33
  (41 other events, 638.0 us)
Sparse Core Ops, SparseCore 0:
  11.4 99.0 all-gather.2

commit v2 on v1

v2 whole, which is shorter than its diff:
```python
import functools

import jax
import jax.numpy as jnp
from jax import lax
from jax.experimental import pallas as pl
from jax.experimental.pallas import tpu as pltpu
from jax.sharding import PartitionSpec as P

AXES = ("rows", "inner")
B = 128
BF = jnp.bfloat16
F32 = jnp.float32
VMEM_LIMIT = 48 * 1024 * 1024
ZC, HC, ZN, HN = 0, 8, 16, 17
PX, PYH, PP, PZ, PYL, PM, PC, PR = range(8)


def places():
    for yh in range(2):
        for x in range(4):
            for p in range(2):
                for z in range(4):
                    for yl in range(2):
                        yield yh, x, p, z, yl


def number(yh, x, p, z, yl):
    return (((yh * 4 + x % 4) * 2 + p) * 4 + z % 4) * 2 + yl


def send(value, to):
    return lax.ppermute(value, AXES, [(number(*at), number(*to(*at))) for at in places()])


def along_x(d):
    return lambda yh, x, p, z, yl: (yh, (x + d) % 4, p, z, yl)


def along_z(d):
    return lambda yh, x, p, z, yl: (yh, x, p, (z + d) % 4, yl)


def other_yh(yh, x, p, z, yl):
    return 1 - yh, x, p, z, yl


def other_yl(yh, x, p, z, yl):
    return yh, x, p, z, 1 - yl


def other_core(yh, x, p, z, yl):
    return yh, x, 1 - p, z, yl


OWN, UP, DOWN, FAR = (0, 0), (-1, 0), (1, 0), (2, 0)
PAIR, PAIR_UP, PAIR_DOWN, PAIR_FAR = (0, 1), (-1, 1), (1, 1), (2, 1)
GATHERED = (OWN, DOWN, FAR, UP, PAIR, PAIR_DOWN, PAIR_FAR, PAIR_UP)
LZ, LH, LN, LETTER = 0, 4096, 4608, 4624


def after(values, others):
    n = len(values)
    return lax.optimization_barrier((*values, *others))[:n]


def vmem_call(kernel, scalars, arrays, out_shape, scratch, flops, space=pltpu.VMEM, out_space=pltpu.VMEM):
    whole, whole_out = pl.BlockSpec(memory_space=space), pl.BlockSpec(memory_space=out_space)
    many = isinstance(out_shape, (list, tuple))
    outs = list(out_shape) if many else [out_shape]
    size = sum(a.size * a.dtype.itemsize for a in list(arrays) + outs)
    return pl.pallas_call(
        kernel,
        out_shape=out_shape,
        grid_spec=pltpu.PrefetchScalarGridSpec(
            num_scalar_prefetch=len(scalars),
            grid=(),
            in_specs=[whole] * len(arrays),
            out_specs=[whole_out] * len(outs) if many else whole_out,
            scratch_shapes=scratch,
        ),
        compiler_params=pltpu.CompilerParams(vmem_limit_bytes=VMEM_LIMIT),
        cost_estimate=pl.CostEstimate(flops=flops, bytes_accessed=size, transcendentals=0),
    )(*scalars, *arrays)


def inner_stripe(pos, dz, dyl):
    return lax.rem(pos[PZ] + dz + 4, 4) * 2 + lax.rem(pos[PYL] + dyl, 2)


def chip_of(pos, dx, dyh):
    return lax.rem(pos[PYH] + dyh, 2) * 4 + lax.rem(pos[PX] + dx + 4, 4)


def spot_of(pos, chip):
    return lax.rem(chip // 4 + pos[PYH], 2) * 4 + lax.rem(lax.rem(chip, 4) - pos[PX] + 4, 4)


def table_row(pos, chip, core, j):
    return lax.rem(core + pos[PP], 2) * 32 + spot_of(pos, chip) * 4 + j


def rows_at(start, size=B):
    return pl.ds(pl.multiple_of(start, size), size)


def coupled_kernel(pieces, first, last, table, pos, *refs):
    n = len(pieces)
    xs, rest = refs[:n], refs[n:]
    z_own, z_sib = rest[:2]
    before = None if first else rest[2]
    out, lhs, rhs = rest[-3:]
    c, p = pos[PC], pos[PP]

    def one(source, core, j):
        row = table_row(pos, c, core, j)
        live = table[row, ZN]
        for spot, (ref, (dz, dyl)) in enumerate(zip(xs, pieces)):
            t = inner_stripe(pos, dz, dyl)
            col = table[row, ZC + t] - t * 8
            lhs[:, spot * B : spot * B + B] = ref[:, rows_at(col * B)]
            block = source[t, rows_at(j * B), :]
            rhs[:, spot * B : spot * B + B] = jnp.where(t < live, block, jnp.zeros_like(block))
        total = lax.dot_general(lhs[...], rhs[...], (((1,), (1,)), ((), ())), preferred_element_type=F32)
        here = rows_at((core * 4 + j) * B)
        if not first:
            total += before[:, here]
        out[:, here] = total.astype(out.dtype)

    @pl.loop(0, 4)
    def _(j):
        one(z_own, p, j)
        one(z_sib, 1 - p, j)


def x_out_kernel(pieces, first, last, table, pos, *refs):
    n = len(pieces)
    blocks, rest = refs[:n], refs[n:]
    sources, outs = rest[:2], rest[-3:-1]
    befores = (None, None) if first else rest[2:4]
    acc = rest[-1]
    p, m = pos[PP], pos[PM]
    for source, out, before, core in zip(sources, outs, befores, (p, 1 - p)):
        acc[...] = jnp.zeros_like(acc) if first else before[...]

        @pl.loop(0, 4)
        def _(i):
            row = table_row(pos, m, core, i)
            live = table[row, ZN]
            for ref, (dx, dyh) in zip(blocks, pieces):
                t = chip_of(pos, dx, dyh)
                q = table[row, ZC + t] - t * 8 - p * 4

                @pl.when((t < live) & (q >= 0) & (q < 4))
                def _():
                    acc[rows_at(i * B), :] += jnp.dot(source[i, t], ref[rows_at(q * B), :], preferred_element_type=F32)

        out[...] = acc[...].astype(out.dtype)


def pick_kernel(pos, *refs):
    letters, (stripe, slots, sems) = refs[:8], refs[8:]
    c = pos[PC]
    row = pl.ds(pl.multiple_of(c * 512, 512), 512)
    copies = [pltpu.make_async_copy(v.at[row], slots.at[n], sems.at[n]) for n, v in enumerate(letters)]
    for copy in copies:
        copy.start()
    for v, (dx, dyh) in zip(letters, GATHERED):

        @pl.when(chip_of(pos, dx, dyh) == c)
        def _():
            copy = pltpu.make_async_copy(v.at[pl.ds(0, 4096)], stripe, sems.at[8])
            copy.start()
            copy.wait()

    for copy in copies:
        copy.wait()


def w_kernel(table, pos, *refs):
    letters, (mine, theirs, z_m, h_c, acc, sems) = refs[:8], refs[8:]
    p, m, c = pos[PP], pos[PM], pos[PC]
    row = pl.ds(pl.multiple_of(m * 512, 512), 512)
    copies = []
    for n, v in enumerate(letters):
        copies.append(pltpu.make_async_copy(v.at[row], z_m.at[n], sems.at[0, n]))
        copies.append(pltpu.make_async_copy(v.at[pl.ds(LH, 512)], h_c.at[n], sems.at[1, n]))
    for copy in copies:
        copy.start()
    acc[...] = jnp.zeros_like(acc)
    for n in range(8):
        copies[2 * n].wait()
        copies[2 * n + 1].wait()

        @pl.loop(0, 4)
        def _(j):
            row = n * 4 + j
            i = table[row, ZC + m] - m * 8
            col = table[row, HC + c] - c * 8

            @pl.when((m < table[row, ZN]) & (c < table[row, HN]))
            def _():
                term = lax.dot_general(
                    z_m[n, rows_at(j * B), :],
                    h_c[n, rows_at(j * B), :],
                    (((0,), (0,)), ((), ())),
                    preferred_element_type=F32,
                )
                acc[rows_at(i * B), rows_at(col * B)] += term

    mine[...] = acc[rows_at(p * 512, 512), :]
    theirs[...] = acc[rows_at(512 - p * 512, 512), :].astype(BF)


def h_perp_kernel(pieces, first, last, table, pos, *refs):
    n = len(pieces)
    blocks, rest = refs[:n], refs[n:]
    own, sib = rest[:2]
    out, acc = rest[-2:]
    c, p = pos[PC], pos[PP]
    acc[...] = jnp.zeros_like(acc) if first else rest[2][...]

    @pl.loop(0, 4)
    def _(j):
        for source, core in ((own, p), (sib, 1 - p)):
            for ref, (dz, dyl) in zip(blocks, pieces):
                t = inner_stripe(pos, dz, dyl)
                row = table_row(pos, t, core, j)
                col = table[row, ZC + c] - c * 8

                @pl.when(c < table[row, ZN])
                def _():
                    term = jnp.dot(
                        ref[:, rows_at((core * 4 + j) * B)],
                        source[spot_of(pos, t), rows_at(j * B), :],
                        preferred_element_type=F32,
                    )
                    acc[:, rows_at(col * B)] += term

    out[...] = acc[...].astype(out.dtype)


def part(kernel, scalars, blocks, fixed, before, last, outs, scratch):
    pieces = tuple(blocks)
    shapes = [jax.ShapeDtypeStruct((512, 1024), t) for t in outs]
    got = vmem_call(
        functools.partial(kernel, pieces, not before, last),
        scalars,
        (*blocks.values(), *fixed, *before),
        shapes,
        scratch,
        2 * 8 * len(pieces) * 512 * B * B,
    )
    return list(got)


def body(h_blocks, h_cols, h_count, z_blocks, z_cols, z_count, x_perp):
    r, c = lax.axis_index("rows"), lax.axis_index("inner")
    m, p = r // 2, r % 2
    yh, x, z, yl = m // 4, m % 4, c // 2, c % 2
    pos = jnp.stack([x, yh, p, z, yl, m, c, r]).astype(jnp.int32)
    up_z, down_z, up_x, down_x = along_z(1), along_z(-1), along_x(1), along_x(-1)

    names = jnp.concatenate([z_cols, h_cols, z_count[:, None], h_count[:, None]], axis=1)
    names = jnp.pad(names.astype(BF), ((0, 12), (0, 110)))
    h_c = lax.dynamic_index_in_dim(h_blocks, c, 1, keepdims=False).reshape(512, B)
    l = jnp.concatenate([z_blocks.transpose(1, 0, 2, 3).reshape(4096, B), h_c, names], axis=0)

    xa, xb = send(x_perp, up_z), send(x_perp, down_z)
    la, lb, ly = send(l, up_x), send(l, down_x), send(l, other_yh)
    la_, ly_, x_, xa_ = after((la, ly, x_perp, xa), (lb, xb))
    la2, lyb = send(la_, up_x), send(ly_, down_x)
    xy, xa2 = send(x_, other_yl), send(xa_, up_z)
    ly_, lyb_, xy_, xa2_ = after((ly, lyb, xy, xa2), (la2,))
    lya, lyb2 = send(ly_, up_x), send(lyb_, down_x)
    xya, xyb, xya2 = send(xy_, up_z), send(xy_, down_z), send(xa2_, other_yl)

    lya, lyb2 = after((lya, lyb2), (xya, xyb, xya2))
    came = {OWN: l, UP: la, DOWN: lb, PAIR: ly, FAR: la2, PAIR_UP: lya, PAIR_DOWN: lyb, PAIR_FAR: lyb2}
    letters = [came[at] for at in GATHERED]
    table = jnp.concatenate([v[LN : LN + 4, :18] for v in letters], axis=0).astype(jnp.int32)
    table = jnp.concatenate([table, send(table, other_core)], axis=0)
    at = (table, pos)
    tile = jax.ShapeDtypeStruct((512, 1024), BF)
    wide = pltpu.VMEM((512, 1024), F32)
    slot = jax.ShapeDtypeStruct((8, 512, B), BF)
    z_stripe, slots_zc = vmem_call(
        pick_kernel,
        (pos,),
        letters,
        [jax.ShapeDtypeStruct((4096, B), BF), slot],
        [pltpu.SemaphoreType.DMA((9,))],
        0,
        pl.ANY,
        pl.ANY,
    )
    z_stripe = z_stripe.reshape(8, 512, B)
    z_stripe_sib = send(z_stripe, other_core)
    slots_zc_sib = send(slots_zc, other_core)
    z_sib = send(z_blocks, other_core)
    w_mine, w_theirs = vmem_call(
        w_kernel,
        at,
        letters,
        [jax.ShapeDtypeStruct((512, 1024), F32), tile],
        [pltpu.VMEM((8, 512, B), BF)] * 2 + [pltpu.VMEM((1024, 1024), F32), pltpu.SemaphoreType.DMA((2, 8))],
        64 * 2 * B**3,
        pl.ANY,
    )
    w = (w_mine + send(w_theirs, other_core).astype(F32)).astype(BF)
    z_c_rows = (z_stripe, z_stripe_sib)

    def coupled_part(blocks, before, last):
        n = len(blocks) * B
        scratch = [pltpu.VMEM((512, n), BF), pltpu.VMEM((B, n), BF)]
        return part(coupled_kernel, at, blocks, z_c_rows, before, last, [BF if last else F32], scratch)

    x_all = {OWN: x_perp, UP: xa, DOWN: xb, PAIR: xy, FAR: xa2, PAIR_UP: xya, PAIR_DOWN: xyb, PAIR_FAR: xya2}
    (v,) = coupled_part(x_all, [], True)

    v_, w_ = after((v, w), (slots_zc_sib, z_sib))
    va, vb, vy = send(v_, up_x), send(v_, down_x), send(v_, other_yh)
    wa, wb = send(w_, up_z), send(w_, down_z)
    va_, vy_, w_, wa_ = after((va, vy, w, wa), (vb, wb))
    va2, vyb = send(va_, up_x), send(vy_, down_x)
    wy, wa2 = send(w_, other_yl), send(wa_, up_z)
    def x_part(blocks, before, last):
        return part(
            x_out_kernel, at, blocks, (z_blocks, z_sib), before, last, [F32, BF] if last else [F32, F32], [wide]
        )

    def h_part(blocks, before, last):
        return part(h_perp_kernel, at, blocks, (slots_zc, slots_zc_sib), before, last, [BF if last else F32], [wide])

    vy_, vyb_, wy_, wa2_ = after((vy, vyb, wy, wa2), (va2,))
    vya, vyb2 = send(vy_, up_x), send(vyb_, down_x)
    wya, wyb, wya2 = send(wy_, up_z), send(wy_, down_z), send(wa2_, other_yl)
    xs = x_part({OWN: v, UP: va, DOWN: vb, PAIR: vy, FAR: va2, PAIR_DOWN: vyb}, [], False)
    hs = h_part({OWN: w, UP: wa, DOWN: wb, PAIR: wy, FAR: wa2}, [], False)
    mine, theirs = x_part({PAIR_UP: vya, PAIR_FAR: vyb2}, xs, True)
    x_tile = (mine + send(theirs, other_core).astype(F32)).astype(BF)
    (h_tile,) = h_part({PAIR_UP: wya, PAIR_DOWN: wyb, PAIR_FAR: wya2}, hs, True)
    return h_tile, x_tile


def solution(mesh):
    in_specs = (
        P("rows", None, None, None),
        P("rows", None),
        P("rows"),
        P("rows", None, None, None),
        P("rows", None),
        P("rows"),
        P("rows", "inner"),
    )
    out_specs = (P("rows", "inner"), P("rows", "inner"))
    return jax.shard_map(body, mesh=mesh, in_specs=in_specs, out_specs=out_specs, check_vma=False)
```

time: 339 us -> 238 us (0.70)
  waiting for transfers between devices: 175 us -> 115 us
  starting transfers between devices: 78.3 us -> 42 us
  between operations: 14.6 us -> 0.94 us
  Pallas kernels: 49.9 us -> 62.2 us
  local copies, waits for them, and re-layouts: 17.8 us -> 12.4 us
    ppermute x44 -> x34, waiting for transfers between devices: 175 us -> 115 us  [send(): lax.ppermute(value, AXES, [(number(*at), number(*to(*at))) for at in plac...]
    ppermute x44 -> x34, starting transfers between devices: 78.3 us -> 42 us  [send(): lax.ppermute(value, AXES, [(number(*at), number(*to(*at))) for at in plac...]
    pallas_call x4 -> x7, Pallas kernels: 49.9 us -> 62.2 us  [vmem_call(): pl.pallas_call(kernel, out_shape=out_shape, grid_spec=pltpu.PrefetchScala...]
    slice x12 -> x7, local copies, waits for them, and re-layouts: 7.64 us -> 3.95 us  [body(): v[LN:LN + 4, :18]]
    unnamed x47 -> x38, local copies, waits for them, and re-layouts: 7.69 us -> 6.74 us
  transfers between devices with their start and end apart: 45 -> 34, of which waited for: 13 -> 12; matrix products, arithmetic and copies ran while one was open for 3% -> 1% of each run, Pallas kernels for 9% -> 26%
where the time goes in v2:
time: 238 us; the launch traced here: 237 us
  waiting for transfers between devices  115 us (48%)
  Pallas kernels  62.2 us (26%)
  starting transfers between devices  42 us (18%)
  local copies, waits for them, and re-layouts  12.4 us (5%)
  other arithmetic  4.68 us (2%)
    ppermute x34, waiting for transfers between devices, send(): lax.ppermute(value, AXES, [(number(*at), number(*to(*at))) for at in plac...  115 us
    pallas_call x7, Pallas kernels, vmem_call(): pl.pallas_call(kernel, out_shape=out_shape, grid_spec=pltpu.PrefetchScala...  62.2 us
    ppermute x34, starting transfers between devices, send(): lax.ppermute(value, AXES, [(number(*at), number(*to(*at))) for at in plac...  42 us
    unnamed x38, local copies, waits for them, and re-layouts  6.74 us
  transfers between devices with their start and end apart: 34, of which 12 were waited for; matrix products, arithmetic and copies ran while one was open for 1% of the time, Pallas kernels for 26%

profile of v2, /device:TPU:1, one launch (start us, length us, event | category | flops | bytes accessed | tf_op | source)
XLA Modules:
  0.0 236.8 jit_solution(2203505887606381797)
XLA Ops:
  5.2 3.4 %collective-permute-start = (bf16[4624,128]{1,0:T(8,128)(2,1)S(1)}, bf16[4624,128]{1,0:T(8,128)(2,1)S(1)}, u32[]{:S(2)}, u32[]{:S(2)}) collective-permute-start(bf16[4624,128]{1,0:T(8,128)(2,1)S(1)} %fusion.1.refs_0_), channel_id=1, source_target_pairs={{0,48},{1,49},{2,50},{3,51},{4,52},{5,53},{6,54},{7,55},{8,56},{9,... | collective-permute-start | bytes 3551240 | tf_op jit(solution)/shard_map/ppermute | solution.py:33
  8.5 2.9 %collective-permute-start.2 = (bf16[4624,128]{1,0:T(8,128)(2,1)S(1)}, bf16[4624,128]{1,0:T(8,128)(2,1)}, u32[]{:S(2)}, u32[]{:S(2)}) collective-permute-start(bf16[4624,128]{1,0:T(8,128)(2,1)S(1)} %fusion.1.refs_0_), channel_id=1, source_target_pairs={{0,64},{1,65},{2,66},{3,67},{4,68},{5,69},{6,70},{7,71},{8,72},{9,... | collective-permute-start | bytes 3551240 | tf_op jit(solution)/shard_map/ppermute | solution.py:33
  13.1 2.1 collective-permute-start.4
  15.2 22.6 %collective-permute-done.3.refs_1_ = bf16[512,1024]{1,0:T(8,128)(2,1)S(1)} collective-permute-done((bf16[512,1024]{1,0:T(8,128)(2,1)}, bf16[512,1024]{1,0:T(8,128)(2,1)S(1)}, u32[]{:S(2)}, u32[]{:S(2)}) %collective-permute-start.3) | collective-permute-done | bytes 1048608 | tf_op jit(solution)/shard_map/ppermute | solution.py:33
  39.9 2.7 %collective-permute-start.6 = (bf16[4624,128]{1,0:T(8,128)(2,1)}, bf16[4624,128]{1,0:T(8,128)(2,1)}, u32[]{:S(2)}, u32[]{:S(2)}) collective-permute-start(bf16[4624,128]{1,0:T(8,128)(2,1)} %collective-permute-done.2.refs_4_), channel_id=1, source_target_pairs={{0,48},{1,49},{2,50},{3,51},{4,52},{5,53},{6,54},{7,55},{8,56},{9,... | collective-permute-start | bytes 3551240 | tf_op jit(solution)/shard_map/ppermute | solution.py:33
  44.3 20.9 %collective-permute-done.7.refs_3_ = bf16[512,1024]{1,0:T(8,128)(2,1)} collective-permute-done((bf16[512,1024]{1,0:T(8,128)(2,1)}, bf16[512,1024]{1,0:T(8,128)(2,1)}, u32[]{:S(2)}, u32[]{:S(2)}) %collective-permute-start.7) | collective-permute-done | bytes 1048608 | tf_op jit(solution)/shard_map/ppermute | solution.py:33
  68.1 2.7 %collective-permute-start.10 = (bf16[4624,128]{1,0:T(8,128)(2,1)}, bf16[4624,128]{1,0:T(8,128)(2,1)}, u32[]{:S(2)}, u32[]{:S(2)}) collective-permute-start(bf16[4624,128]{1,0:T(8,128)(2,1)} %collective-permute-done.6.refs_5_), channel_id=1, source_target_pairs={{0,48},{1,49},{2,50},{3,51},{4,52},{5,53},{6,54},{7,55},{8,56},{9,... | collective-permute-start | bytes 3551240 | tf_op jit(solution)/shard_map/ppermute | solution.py:33
  70.8 2.7 %collective-permute-start.12 = (bf16[512,1024]{1,0:T(8,128)(2,1)}, bf16[512,1024]{1,0:T(8,128)(2,1)}, u32[]{:S(2)}, u32[]{:S(2)}) collective-permute-start(bf16[512,1024]{1,0:T(8,128)(2,1)} %collective-permute-done.7.refs_3_), channel_id=1, source_target_pairs={{0,6},{1,7},{2,0},{3,1},{4,2},{5,3},{6,4},{7,5},{8,14},{9,15},{10,... | collective-permute-start | bytes 3145736 | tf_op jit(solution)/shard_map/ppermute | solution.py:33
  76.5 17.1 %collective-permute-done.11.refs_5_ = bf16[512,1024]{1,0:T(8,128)(2,1)} collective-permute-done((bf16[512,1024]{1,0:T(8,128)(2,1)}, bf16[512,1024]{1,0:T(8,128)(2,1)}, u32[]{:S(2)}, u32[]{:S(2)}) %collective-permute-start.11) | collective-permute-done | bytes 1048608 | tf_op jit(solution)/shard_map/ppermute | solution.py:33
  96.0 4.9 %collective-permute-start.14 = (s32[32,18]{1,0:T(8,128)S(1)}, s32[32,18]{1,0:T(8,128)S(1)}, u32[]{:S(2)}, u32[]{:S(2)}) collective-permute-start(s32[32,18]{1,0:T(8,128)S(1)} %convert_element_type.18), channel_id=1, source_target_pairs={{0,8},{1,9},{2,10},{3,11},{4,12},{5,13},{6,14},{7,15},{8,0},{9,1},... | collective-permute-start | bytes 6920 | tf_op jit(solution)/shard_map/ppermute | solution.py:33
  102.2 2.3 shard_map.86
  104.8 10.7 %shard_map.88 = (f32[512,1024]{1,0:T(8,128)}, bf16[512,1024]{1,0:T(8,128)(2,1)S(1)}) custom-call(s32[64,18]{1,0:T(8,128)S(1)} %pad_add_fusion.table, s32[8]{0:T(128)S(1)} %stack.35.pos, bf16[4624,128]{1,0:T(8,128)(2,1)S(1)} %fusion.1.refs_0_, bf16[4624,128]{1,0:T(8,128)(2,1)S(1)} %collective-permute-done.refs_1_, bf16[4624,128]{1,0:T(8,128)(2,1)S(1)} %copy-done.4, ...), custom_call_target="tpu_custom_call" | custom-call | flops 268435456 | bytes 12615680 | tf_op jit(solution)/shard_map/pallas_call | solution.py:72
  116.5 8.7 %shard_map.87.refs_0_ = bf16[512,1024]{1,0:T(8,128)(2,1)S(1)} custom-call(s32[64,18]{1,0:T(8,128)S(1)} %pad_add_fusion.table, s32[8]{0:T(128)S(1)} %stack.35.pos, bf16[512,1024]{1,0:T(8,128)(2,1)S(1)} %copy-done.11, bf16[512,1024]{1,0:T(8,128)(2,1)S(1)} %copy-done.13, bf16[512,1024]{1,0:T(8,128)(2,1)S(1)} %copy-done.15, ...), custom_call_target="tpu_custom_call" | custom-call | flops 1073741824 | bytes 11534336 | tf_op jit(solution)/shard_map/pallas_call | solution.py:72
  126.0 2.6 %collective-permute-start.22 = (bf16[512,1024]{1,0:T(8,128)(2,1)S(1)}, bf16[512,1024]{1,0:T(8,128)(2,1)S(1)}, u32[]{:S(2)}, u32[]{:S(2)}) collective-permute-start(bf16[512,1024]{1,0:T(8,128)(2,1)S(1)} %shard_map.87.refs_0_), channel_id=1, source_target_pairs={{0,48},{1,49},{2,50},{3,51},{4,52},{5,53},{6,54},{7,55},{8,56},{9,... | collective-permute-start | bytes 3145736 | tf_op jit(solution)/shard_map/ppermute | solution.py:33
  128.6 2.7 %collective-permute-start.23 = (bf16[512,1024]{1,0:T(8,128)(2,1)S(1)}, bf16[512,1024]{1,0:T(8,128)(2,1)S(1)}, u32[]{:S(2)}, u32[]{:S(2)}) collective-permute-start(bf16[512,1024]{1,0:T(8,128)(2,1)S(1)} %add_convert_fusion.1.refs_0_), channel_id=1, source_target_pairs={{0,6},{1,7},{2,0},{3,1},{4,2},{5,3},{6,4},{7,5},{8,14},{9,15},{10,... | collective-permute-start | bytes 3145736 | tf_op jit(solution)/shard_map/ppermute | solution.py:33
  131.3 20.8 %collective-permute-done.19.refs_3_ = bf16[512,1024]{1,0:T(8,128)(2,1)S(1)} collective-permute-done((bf16[512,1024]{1,0:T(8,128)(2,1)S(1)}, bf16[512,1024]{1,0:T(8,128)(2,1)S(1)}, u32[]{:S(2)}, u32[]{:S(2)}) %collective-permute-start.19) | collective-permute-done | bytes 1048608 | tf_op jit(solution)/shard_map/ppermute | solution.py:33
  154.3 21.5 %collective-permute-done.24.refs_5_ = bf16[512,1024]{1,0:T(8,128)(2,1)} collective-permute-done((bf16[512,1024]{1,0:T(8,128)(2,1)S(1)}, bf16[512,1024]{1,0:T(8,128)(2,1)}, u32[]{:S(2)}, u32[]{:S(2)}) %collective-permute-start.24) | collective-permute-done | bytes 1048608 | tf_op jit(solution)/shard_map/ppermute | solution.py:33
  179.1 2.2 collective-permute-start.32
  185.1 11.5 %shard_map.91 = (f32[512,1024]{1,0:T(8,128)}, f32[512,1024]{1,0:T(8,128)}) custom-call(s32[64,18]{1,0:T(8,128)S(1)} %pad_add_fusion.table, s32[8]{0:T(128)S(1)} %stack.35.pos, bf16[512,1024]{1,0:T(8,128)(2,1)S(1)} %shard_map.87.refs_0_, bf16[512,1024]{1,0:T(8,128)(2,1)S(1)} %collective-permute-done.20.refs_1_, ...), custom_call_target="tpu_custom_call" | custom-call | flops 805306368 | bytes 12582912 | tf_op jit(solution)/shard_map/pallas_call | solution.py:72
  196.6 5.4 %collective-permute-done.31.refs_0_ = bf16[512,1024]{1,0:T(8,128)(2,1)S(1)} collective-permute-done((bf16[512,1024]{1,0:T(8,128)(2,1)S(1)}, bf16[512,1024]{1,0:T(8,128)(2,1)S(1)}, u32[]{:S(2)}, u32[]{:S(2)}) %collective-permute-start.31) | collective-permute-done | bytes 1048608 | tf_op jit(solution)/shard_map/ppermute | solution.py:33
  203.3 6.6 %shard_map.92 = (f32[512,1024]{1,0:T(8,128)}, bf16[512,1024]{1,0:T(8,128)(2,1)S(1)}) custom-call(s32[64,18]{1,0:T(8,128)S(1)} %pad_add_fusion.table, s32[8]{0:T(128)S(1)} %stack.35.pos, bf16[512,1024]{1,0:T(8,128)(2,1)S(1)} %collective-permute-done.31.refs_0_, bf16[512,1024]{1,0:T(8,128)(2,1)} %collective-permute-done.32.refs_1_, ...), custom_call_target="tpu_custom_call" | custom-call | flops 268435456 | bytes 11534336 | tf_op jit(solution)/shard_map/pallas_call | solution.py:72
  209.9 3.1 %collective-permute-start.33 = (bf16[512,1024]{1,0:T(8,128)(2,1)S(1)}, bf16[512,1024]{1,0:T(8,128)(2,1)S(1)}, u32[]{:S(2)}, u32[]{:S(2)}) collective-permute-start(bf16[512,1024]{1,0:T(8,128)(2,1)S(1)} %get-tuple-element.57), channel_id=1, source_target_pairs={{0,8},{1,9},{2,10},{3,11},{4,12},{5,13},{6,14},{7,15},{8,0},{9,1},... | collective-permute-start | bytes 3145736 | tf_op jit(solution)/shard_map/ppermute | solution.py:33
  213.0 12.8 %shard_map.89.refs_5_ = f32[512,1024]{1,0:T(8,128)} custom-call(s32[64,18]{1,0:T(8,128)S(1)} %pad_add_fusion.table, s32[8]{0:T(128)S(1)} %stack.35.pos, bf16[512,1024]{1,0:T(8,128)(2,1)S(1)} %add_convert_fusion.1.refs_0_, bf16[512,1024]{1,0:T(8,128)(2,1)S(1)} %collective-permute-done.21.refs_1_, bf16[512,1024]{1,0:T(8,128)(2,1)S(1)} %collective-permute-done.23.refs_2_, ...), custom_call_target="tpu_custom_call" | custom-call | flops 671088640 | bytes 9437184 | tf_op jit(solution)/shard_map/pallas_call | solution.py:72
  225.8 9.7 %shard_map.90 = bf16[512,1024]{1,0:T(8,128)(2,1)} custom-call(s32[64,18]{1,0:T(8,128)S(1)} %pad_add_fusion.table, s32[8]{0:T(128)S(1)} %stack.35.pos, bf16[512,1024]{1,0:T(8,128)(2,1)S(1)} %collective-permute-done.28.refs_0_, bf16[512,1024]{1,0:T(8,128)(2,1)} %collective-permute-done.29.refs_1_, bf16[512,1024]{1,0:T(8,128)(2,1)} %collective-permute-done.30.refs_2_, ...), custom_call_target="tpu_custom_call" | custom-call | flops 402653184 | bytes 8388608 | tf_op jit(solution)/shard_map/pallas_call | solution.py:72
  (112 shorter events, 33.5 us)
Async XLA Ops:
  5.2 33.6 %collective-permute-start = (bf16[4624,128]{1,0:T(8,128)(2,1)S(1)}, bf16[4624,128]{1,0:T(8,128)(2,1)S(1)}, u32[]{:S(2)}, u32[]{:S(2)}) collective-permute-start(bf16[4624,128]{1,0:T(8,128)(2,1)S(1)} %fusion.1.refs_0_), channel_id=1, source_target_pairs={{0,48},{1,49},{2,50},{3,51},{4,52},{5,53},{6,54},{7,55},{8,56},{9,... | collective-permute-start | bytes 3551240 | tf_op jit(solution)/shard_map/ppermute | solution.py:33
  8.5 30.3 %collective-permute-start.1 = (bf16[4624,128]{1,0:T(8,128)(2,1)S(1)}, bf16[4624,128]{1,0:T(8,128)(2,1)S(1)}, u32[]{:S(2)}, u32[]{:S(2)}) collective-permute-start(bf16[4624,128]{1,0:T(8,128)(2,1)S(1)} %fusion.1.refs_0_), channel_id=1, source_target_pairs={{0,16},{1,17},{2,18},{3,19},{4,20},{5,21},{6,22},{7,23},{8,24},{9,... | collective-permute-start | bytes 3551240 | tf_op jit(solution)/shard_map/ppermute | solution.py:33
  8.5 30.3 %collective-permute-start.2 = (bf16[4624,128]{1,0:T(8,128)(2,1)S(1)}, bf16[4624,128]{1,0:T(8,128)(2,1)}, u32[]{:S(2)}, u32[]{:S(2)}) collective-permute-start(bf16[4624,128]{1,0:T(8,128)(2,1)S(1)} %fusion.1.refs_0_), channel_id=1, source_target_pairs={{0,64},{1,65},{2,66},{3,67},{4,68},{5,69},{6,70},{7,71},{8,72},{9,... | collective-permute-start | bytes 3551240 | tf_op jit(solution)/shard_map/ppermute | solution.py:33
  11.5 26.3 %collective-permute-start.3 = (bf16[512,1024]{1,0:T(8,128)(2,1)}, bf16[512,1024]{1,0:T(8,128)(2,1)S(1)}, u32[]{:S(2)}, u32[]{:S(2)}) collective-permute-start(bf16[512,1024]{1,0:T(8,128)(2,1)} %refs_0_.1), channel_id=1, source_target_pairs={{0,2},{1,3},{2,4},{3,5},{4,6},{5,7},{6,0},{7,1},{8,10},{9,11},{10,... | collective-permute-start | bytes 3145736 | tf_op jit(solution)/shard_map/ppermute | solution.py:33
  13.1 24.7 %collective-permute-start.4 = (bf16[512,1024]{1,0:T(8,128)(2,1)}, bf16[512,1024]{1,0:T(8,128)(2,1)S(1)}, u32[]{:S(2)}, u32[]{:S(2)}) collective-permute-start(bf16[512,1024]{1,0:T(8,128)(2,1)} %refs_0_.1), channel_id=1, source_target_pairs={{0,6},{1,7},{2,0},{3,1},{4,2},{5,3},{6,4},{7,5},{8,14},{9,15},{10,... | collective-permute-start | bytes 3145736 | tf_op jit(solution)/shard_map/ppermute | solution.py:33
  39.9 27.1 %collective-permute-start.5 = (bf16[4624,128]{1,0:T(8,128)(2,1)S(1)}, bf16[4624,128]{1,0:T(8,128)(2,1)S(1)}, u32[]{:S(2)}, u32[]{:S(2)}) collective-permute-start(bf16[4624,128]{1,0:T(8,128)(2,1)S(1)} %collective-permute-done.1.refs_3_), channel_id=1, source_target_pairs={{0,16},{1,17},{2,18},{3,19},{4,20},{5,21},{6,22},{7,23},{8,24},{9,... | collective-permute-start | bytes 3551240 | tf_op jit(solution)/shard_map/ppermute | solution.py:33
  39.9 28.2 %collective-permute-start.6 = (bf16[4624,128]{1,0:T(8,128)(2,1)}, bf16[4624,128]{1,0:T(8,128)(2,1)}, u32[]{:S(2)}, u32[]{:S(2)}) collective-permute-start(bf16[4624,128]{1,0:T(8,128)(2,1)} %collective-permute-done.2.refs_4_), channel_id=1, source_target_pairs={{0,48},{1,49},{2,50},{3,51},{4,52},{5,53},{6,54},{7,55},{8,56},{9,... | collective-permute-start | bytes 3551240 | tf_op jit(solution)/shard_map/ppermute | solution.py:33
  42.9 23.3 %collective-permute-start.8 = (bf16[512,1024]{1,0:T(8,128)(2,1)S(1)}, bf16[512,1024]{1,0:T(8,128)(2,1)}, u32[]{:S(2)}, u32[]{:S(2)}) collective-permute-start(bf16[512,1024]{1,0:T(8,128)(2,1)S(1)} %collective-permute-done.3.refs_1_), channel_id=1, source_target_pairs={{0,2},{1,3},{2,4},{3,5},{4,6},{5,7},{6,0},{7,1},{8,10},{9,11},{10,... | collective-permute-start | bytes 3145736 | tf_op jit(solution)/shard_map/ppermute | solution.py:33
  68.1 26.4 %collective-permute-start.9 = (bf16[4624,128]{1,0:T(8,128)(2,1)}, bf16[4624,128]{1,0:T(8,128)(2,1)}, u32[]{:S(2)}, u32[]{:S(2)}) collective-permute-start(bf16[4624,128]{1,0:T(8,128)(2,1)} %collective-permute-done.2.refs_4_), channel_id=1, source_target_pairs={{0,16},{1,17},{2,18},{3,19},{4,20},{5,21},{6,22},{7,23},{8,24},{9,... | collective-permute-start | bytes 3551240 | tf_op jit(solution)/shard_map/ppermute | solution.py:33
  68.1 26.4 %collective-permute-start.10 = (bf16[4624,128]{1,0:T(8,128)(2,1)}, bf16[4624,128]{1,0:T(8,128)(2,1)}, u32[]{:S(2)}, u32[]{:S(2)}) collective-permute-start(bf16[4624,128]{1,0:T(8,128)(2,1)} %collective-permute-done.6.refs_5_), channel_id=1, source_target_pairs={{0,48},{1,49},{2,50},{3,51},{4,52},{5,53},{6,54},{7,55},{8,56},{9,... | collective-permute-start | bytes 3551240 | tf_op jit(solution)/shard_map/ppermute | solution.py:33
  125.7 26.3 %collective-permute-start.19 = (bf16[512,1024]{1,0:T(8,128)(2,1)S(1)}, bf16[512,1024]{1,0:T(8,128)(2,1)S(1)}, u32[]{:S(2)}, u32[]{:S(2)}) collective-permute-start(bf16[512,1024]{1,0:T(8,128)(2,1)S(1)} %shard_map.87.refs_0_), channel_id=1, source_target_pairs={{0,64},{1,65},{2,66},{3,67},{4,68},{5,69},{6,70},{7,71},{8,72},{9,... | collective-permute-start | bytes 3145736 | tf_op jit(solution)/shard_map/ppermute | solution.py:33
  125.8 26.2 %collective-permute-start.20 = (bf16[512,1024]{1,0:T(8,128)(2,1)S(1)}, bf16[512,1024]{1,0:T(8,128)(2,1)S(1)}, u32[]{:S(2)}, u32[]{:S(2)}) collective-permute-start(bf16[512,1024]{1,0:T(8,128)(2,1)S(1)} %shard_map.87.refs_0_), channel_id=1, source_target_pairs={{0,16},{1,17},{2,18},{3,19},{4,20},{5,21},{6,22},{7,23},{8,24},{9,... | collective-permute-start | bytes 3145736 | tf_op jit(solution)/shard_map/ppermute | solution.py:33
  125.9 26.1 %collective-permute-start.21 = (bf16[512,1024]{1,0:T(8,128)(2,1)S(1)}, bf16[512,1024]{1,0:T(8,128)(2,1)S(1)}, u32[]{:S(2)}, u32[]{:S(2)}) collective-permute-start(bf16[512,1024]{1,0:T(8,128)(2,1)S(1)} %add_convert_fusion.1.refs_0_), channel_id=1, source_target_pairs={{0,2},{1,3},{2,4},{3,5},{4,6},{5,7},{6,0},{7,1},{8,10},{9,11},{10,... | collective-permute-start | bytes 3145736 | tf_op jit(solution)/shard_map/ppermute | solution.py:33
  126.0 26.1 %collective-permute-start.22 = (bf16[512,1024]{1,0:T(8,128)(2,1)S(1)}, bf16[512,1024]{1,0:T(8,128)(2,1)S(1)}, u32[]{:S(2)}, u32[]{:S(2)}) collective-permute-start(bf16[512,1024]{1,0:T(8,128)(2,1)S(1)} %shard_map.87.refs_0_), channel_id=1, source_target_pairs={{0,48},{1,49},{2,50},{3,51},{4,52},{5,53},{6,54},{7,55},{8,56},{9,... | collective-permute-start | bytes 3145736 | tf_op jit(solution)/shard_map/ppermute | solution.py:33
  128.6 24.2 %collective-permute-start.23 = (bf16[512,1024]{1,0:T(8,128)(2,1)S(1)}, bf16[512,1024]{1,0:T(8,128)(2,1)S(1)}, u32[]{:S(2)}, u32[]{:S(2)}) collective-permute-start(bf16[512,1024]{1,0:T(8,128)(2,1)S(1)} %add_convert_fusion.1.refs_0_), channel_id=1, source_target_pairs={{0,6},{1,7},{2,0},{3,1},{4,2},{5,3},{6,4},{7,5},{8,14},{9,15},{10,... | collective-permute-start | bytes 3145736 | tf_op jit(solution)/shard_map/ppermute | solution.py:33
  154.2 23.3 %collective-permute-start.25 = (bf16[512,1024]{1,0:T(8,128)(2,1)S(1)}, bf16[512,1024]{1,0:T(8,128)(2,1)S(1)}, u32[]{:S(2)}, u32[]{:S(2)}) collective-permute-start(bf16[512,1024]{1,0:T(8,128)(2,1)S(1)} %add_convert_fusion.1.refs_0_), channel_id=1, source_target_pairs={{0,1},{1,0},{2,3},{3,2},{4,5},{5,4},{6,7},{7,6},{8,9},{9,8},{10,11... | collective-permute-start | bytes 3145736 | tf_op jit(solution)/shard_map/ppermute | solution.py:33
  154.2 24.4 %collective-permute-start.26 = (bf16[512,1024]{1,0:T(8,128)(2,1)S(1)}, bf16[512,1024]{1,0:T(8,128)(2,1)S(1)}, u32[]{:S(2)}, u32[]{:S(2)}) collective-permute-start(bf16[512,1024]{1,0:T(8,128)(2,1)S(1)} %collective-permute-done.21.refs_1_), channel_id=1, source_target_pairs={{0,2},{1,3},{2,4},{3,5},{4,6},{5,7},{6,0},{7,1},{8,10},{9,11},{10,... | collective-permute-start | bytes 3145736 | tf_op jit(solution)/shard_map/ppermute | solution.py:33
  154.2 24.4 %collective-permute-start.27 = (bf16[512,1024]{1,0:T(8,128)(2,1)S(1)}, bf16[512,1024]{1,0:T(8,128)(2,1)S(1)}, u32[]{:S(2)}, u32[]{:S(2)}) collective-permute-start(bf16[512,1024]{1,0:T(8,128)(2,1)S(1)} %collective-permute-done.20.refs_1_), channel_id=1, source_target_pairs={{0,16},{1,17},{2,18},{3,19},{4,20},{5,21},{6,22},{7,23},{8,24},{9,... | collective-permute-start | bytes 3145736 | tf_op jit(solution)/shard_map/ppermute | solution.py:33
  178.6 23.5 %collective-permute-start.31 = (bf16[512,1024]{1,0:T(8,128)(2,1)S(1)}, bf16[512,1024]{1,0:T(8,128)(2,1)S(1)}, u32[]{:S(2)}, u32[]{:S(2)}) collective-permute-start(bf16[512,1024]{1,0:T(8,128)(2,1)S(1)} %collective-permute-done.19.refs_3_), channel_id=1, source_target_pairs={{0,16},{1,17},{2,18},{3,19},{4,20},{5,21},{6,22},{7,23},{8,24},{9,... | collective-permute-start | bytes 3145736 | tf_op jit(solution)/shard_map/ppermute | solution.py:33
  179.1 23.0 %collective-permute-start.32 = (bf16[512,1024]{1,0:T(8,128)(2,1)}, bf16[512,1024]{1,0:T(8,128)(2,1)}, u32[]{:S(2)}, u32[]{:S(2)}) collective-permute-start(bf16[512,1024]{1,0:T(8,128)(2,1)} %collective-permute-done.24.refs_5_), channel_id=1, source_target_pairs={{0,48},{1,49},{2,50},{3,51},{4,52},{5,53},{6,54},{7,55},{8,56},{9,... | collective-permute-start | bytes 3145736 | tf_op jit(solution)/shard_map/ppermute | solution.py:33
  181.3 44.5 %collective-permute-start.28 = (bf16[512,1024]{1,0:T(8,128)(2,1)S(1)}, bf16[512,1024]{1,0:T(8,128)(2,1)S(1)}, u32[]{:S(2)}, u32[]{:S(2)}) collective-permute-start(bf16[512,1024]{1,0:T(8,128)(2,1)S(1)} %collective-permute-done.25.refs_3_), channel_id=1, source_target_pairs={{0,2},{1,3},{2,4},{3,5},{4,6},{5,7},{6,0},{7,1},{8,10},{9,11},{10,... | collective-permute-start | bytes 3145736 | tf_op jit(solution)/shard_map/ppermute | solution.py:33
  181.8 43.9 %collective-permute-start.29 = (bf16[512,1024]{1,0:T(8,128)(2,1)S(1)}, bf16[512,1024]{1,0:T(8,128)(2,1)}, u32[]{:S(2)}, u32[]{:S(2)}) collective-permute-start(bf16[512,1024]{1,0:T(8,128)(2,1)S(1)} %collective-permute-done.25.refs_3_), channel_id=1, source_target_pairs={{0,6},{1,7},{2,0},{3,1},{4,2},{5,3},{6,4},{7,5},{8,14},{9,15},{10,... | collective-permute-start | bytes 3145736 | tf_op jit(solution)/shard_map/ppermute | solution.py:33
  183.9 41.8 %collective-permute-start.30 = (bf16[512,1024]{1,0:T(8,128)(2,1)S(1)}, bf16[512,1024]{1,0:T(8,128)(2,1)}, u32[]{:S(2)}, u32[]{:S(2)}) collective-permute-start(bf16[512,1024]{1,0:T(8,128)(2,1)S(1)} %collective-permute-done.26.refs_4_), channel_id=1, source_target_pairs={{0,1},{1,0},{2,3},{3,2},{4,5},{5,4},{6,7},{7,6},{8,9},{9,8},{10,11... | collective-permute-start | bytes 3145736 | tf_op jit(solution)/shard_map/ppermute | solution.py:33
  209.9 25.6 %collective-permute-start.33 = (bf16[512,1024]{1,0:T(8,128)(2,1)S(1)}, bf16[512,1024]{1,0:T(8,128)(2,1)S(1)}, u32[]{:S(2)}, u32[]{:S(2)}) collective-permute-start(bf16[512,1024]{1,0:T(8,128)(2,1)S(1)} %get-tuple-element.57), channel_id=1, source_target_pairs={{0,8},{1,9},{2,10},{3,11},{4,12},{5,13},{6,14},{7,15},{8,0},{9,1},... | collective-permute-start | bytes 3145736 | tf_op jit(solution)/shard_map/ppermute | solution.py:33
  (29 other events, 414.5 us)

commit v3 on v2

v3 whole, which is shorter than its diff:
```python
import functools

import jax
import jax.numpy as jnp
from jax import lax
from jax.experimental import pallas as pl
from jax.experimental.pallas import tpu as pltpu
from jax.sharding import PartitionSpec as P

AXES = ("rows", "inner")
B = 128
BF = jnp.bfloat16
F32 = jnp.float32
MIB = 1024 * 1024
ZC, HC, ZN, HN = 0, 8, 4, 5
PX, PYH, PP, PZ, PYL, PM, PC, PR = range(8)


def places():
    for yh in range(2):
        for x in range(4):
            for p in range(2):
                for z in range(4):
                    for yl in range(2):
                        yield yh, x, p, z, yl


def number(yh, x, p, z, yl):
    return (((yh * 4 + x % 4) * 2 + p) * 4 + z % 4) * 2 + yl


def send(value, to):
    return lax.ppermute(value, AXES, [(number(*at), number(*to(*at))) for at in places()])


def along_x(d):
    return lambda yh, x, p, z, yl: (yh, (x + d) % 4, p, z, yl)


def along_z(d):
    return lambda yh, x, p, z, yl: (yh, x, p, (z + d) % 4, yl)


def other_yh(yh, x, p, z, yl):
    return 1 - yh, x, p, z, yl


def other_yl(yh, x, p, z, yl):
    return yh, x, p, z, 1 - yl


def other_core(yh, x, p, z, yl):
    return yh, x, 1 - p, z, yl


OWN, UP, DOWN, FAR = (0, 0), (-1, 0), (1, 0), (2, 0)
PAIR, PAIR_UP, PAIR_DOWN, PAIR_FAR = (0, 1), (-1, 1), (1, 1), (2, 1)
GATHERED = (OWN, DOWN, FAR, UP, PAIR, PAIR_DOWN, PAIR_FAR, PAIR_UP)
LZ, LH, LN, LETTER = 0, 4096, 4608, 4624


def after(*values):
    return lax.optimization_barrier(values)


def in_hbm(value):
    return pltpu.with_memory_space_constraint(value, pltpu.HBM)


def vmem_call(kernel, scalars, arrays, out_shape, scratch, flops, mib, space=pltpu.VMEM, out_space=pltpu.VMEM):
    spaces = space if isinstance(space, list) else [space] * len(arrays)
    whole_out = pl.BlockSpec(memory_space=out_space)
    many = isinstance(out_shape, (list, tuple))
    outs = list(out_shape) if many else [out_shape]
    size = sum(a.size * a.dtype.itemsize for a in list(arrays) + outs)
    return pl.pallas_call(
        kernel,
        out_shape=out_shape,
        grid_spec=pltpu.PrefetchScalarGridSpec(
            num_scalar_prefetch=len(scalars),
            grid=(),
            in_specs=[pl.BlockSpec(memory_space=v) for v in spaces],
            out_specs=[whole_out] * len(outs) if many else whole_out,
            scratch_shapes=scratch,
        ),
        compiler_params=pltpu.CompilerParams(vmem_limit_bytes=mib * MIB),
        cost_estimate=pl.CostEstimate(flops=flops, bytes_accessed=size, transcendentals=0),
    )(*scalars, *arrays)


def inner_stripe(pos, dz, dyl):
    return lax.rem(pos[PZ] + dz + 4, 4) * 2 + lax.rem(pos[PYL] + dyl, 2)


def chip_of(pos, dx, dyh):
    return lax.rem(pos[PYH] + dyh, 2) * 4 + lax.rem(pos[PX] + dx + 4, 4)


def spot_of(pos, chip):
    return lax.rem(chip // 4 + pos[PYH], 2) * 4 + lax.rem(lax.rem(chip, 4) - pos[PX] + 4, 4)


class Row:
    def __init__(self, table, side, piece, j):
        self.table, self.side, self.piece, self.j = table, side, piece, j

    def z_name(self, t):
        return self.table[self.side, self.piece, self.j, ZC + t]

    def h_name(self, s):
        return self.table[self.side, self.piece, self.j, HC + s]

    def z_live(self, t):
        return t < self.table[self.side, self.piece, ZN, self.j]

    def h_live(self, s):
        return s < self.table[self.side, self.piece, HN, self.j]


def rows_at(start, size=B):
    return pl.ds(pl.multiple_of(start, size), size)


def masked(live, block):
    return jnp.where(live, block, jnp.zeros_like(block))


def pick_kernel(pos, *refs):
    letters, (stripe, slots, names, sems) = refs[:8], refs[8:]
    c = pos[PC]
    copies = []
    for n, v in enumerate(letters):
        copies.append(pltpu.make_async_copy(v.at[rows_at(c * 512, 512)], slots.at[n], sems.at[0, n]))
        copies.append(pltpu.make_async_copy(v.at[pl.ds(LN, 16)], names.at[n], sems.at[1, n]))
    for copy in copies:
        copy.start()
    for v, (dx, dyh) in zip(letters, GATHERED):

        @pl.when(chip_of(pos, dx, dyh) == c)
        def _():
            copy = pltpu.make_async_copy(v.at[pl.ds(0, 4096)], stripe, sems.at[2, 0])
            copy.start()
            copy.wait()

    for copy in copies:
        copy.wait()


def coupled_kernel(pieces, table, pos, *refs):
    xs, (z_own, z_sib, out) = refs[:8], refs[8:]
    c, p = pos[PC], pos[PP]
    stripes = [inner_stripe(pos, dz, dyl) for dz, dyl in pieces]
    for side, (source, core) in enumerate(((z_own, p), (z_sib, 1 - p))):
        for j in range(4):
            row = Row(table, side, spot_of(pos, c), j)
            total = None
            for n in range(0, 8, 2):
                lhs, rhs = [], []
                for ref, t in zip(xs[n : n + 2], stripes[n : n + 2]):
                    lhs.append(ref[:, rows_at((row.z_name(t) - t * 8) * B)])
                    rhs.append(masked(row.z_live(t), source[rows_at(t * 512 + j * B), :]))
                term = lax.dot_general(
                    jnp.concatenate(lhs, axis=1),
                    jnp.concatenate(rhs, axis=1),
                    (((1,), (1,)), ((), ())),
                    preferred_element_type=F32,
                )
                total = term if total is None else total + term
            out[:, rows_at((core * 4 + j) * B)] = total.astype(BF)


def x_out_kernel(pieces, first, last, table, pos, *refs):
    n = len(pieces)
    blocks, rest = refs[:n], refs[n:]
    z_own, z_sib = rest[:2]
    befores = None if first else rest[2:4]
    mine, theirs, z, held, sems = rest[-5:]
    p, m = pos[PP], pos[PM]
    copies = [pltpu.make_async_copy(v, held.at[pl.ds(s * 512, 512)], sems.at[s]) for s, v in enumerate(blocks)]
    for copy in copies:
        copy.start()
    for s, (dx, dyh) in enumerate(pieces):
        t = chip_of(pos, dx, dyh)
        for side, source in enumerate((z_own, z_sib)):
            for i in range(4):
                row = Row(table, side, 0, i)
                q = row.z_name(t) - t * 8 - p * 4
                block = masked(row.z_live(t), source[i, t])
                for k in range(4):
                    at = (side * 4 + i) * B, (s * 4 + k) * B
                    z[at[0] : at[0] + B, at[1] : at[1] + B] = masked(q == k, block)
    for copy in copies:
        copy.wait()
    for side, out in enumerate((mine, theirs)):
        total = jnp.dot(z[side * 512 : side * 512 + 512, :], held[...], preferred_element_type=F32)
        if not first:
            total += befores[side][...].astype(F32)
        out[...] = total.astype(out.dtype)


def w_kernel(spots, first, last, table, pos, *refs):
    n = len(spots)
    letters, rest = refs[:n], refs[n:]
    before = None if first else rest[0]
    z_m, h_c, acc, sems = rest[-4:]
    p, m, c = pos[PP], pos[PM], pos[PC]
    copies = []
    for s, v in enumerate(letters):
        copies.append(pltpu.make_async_copy(v.at[rows_at(m * 512, 512)], z_m.at[s], sems.at[0, s]))
        copies.append(pltpu.make_async_copy(v.at[pl.ds(LH, 512)], h_c.at[s], sems.at[1, s]))
    for copy in copies:
        copy.start()
    acc[...] = jnp.zeros_like(acc) if first else before[...]
    for copy in copies:
        copy.wait()
    for s, spot in enumerate(spots):
        for j in range(4):
            row = Row(table, 0, spot, j)
            i = row.z_name(m) - m * 8
            col = row.h_name(c) - c * 8
            term = lax.dot_general(
                masked(row.z_live(m) & row.h_live(c), z_m[s, j * B : j * B + B, :]),
                h_c[s, j * B : j * B + B, :],
                (((0,), (0,)), ((), ())),
                preferred_element_type=F32,
            )
            acc[rows_at(i * B), rows_at(col * B)] += term

    if last:
        mine, theirs = rest[-6:-4]
        mine[...] = acc[rows_at(p * 512, 512), :]
        theirs[...] = acc[rows_at(512 - p * 512, 512), :].astype(BF)
    else:
        rest[-5][...] = acc[...]


def h_perp_kernel(pieces, first, last, table, pos, *refs):
    n = len(pieces)
    blocks, rest = refs[:n], refs[n:]
    own, sib = rest[:2]
    out, acc = rest[-2:]
    c, p = pos[PC], pos[PP]
    acc[...] = jnp.zeros_like(acc) if first else rest[2][...].astype(F32)
    for ref, (dz, dyl) in zip(blocks, pieces):
        spot = spot_of(pos, inner_stripe(pos, dz, dyl))
        for side, (source, core) in enumerate(((own, p), (sib, 1 - p))):
            for j in range(4):
                row = Row(table, side, spot, j)
                term = jnp.dot(
                    ref[:, rows_at((core * 4 + j) * B)],
                    masked(row.z_live(c), source[spot, j * B : j * B + B, :]),
                    preferred_element_type=F32,
                )
                acc[:, rows_at((row.z_name(c) - c * 8) * B)] += term
    out[...] = acc[...].astype(out.dtype)


def part(kernel, scalars, blocks, fixed, before, last, outs, scratch, mib, space=pltpu.VMEM):
    pieces = tuple(blocks)
    shapes = [jax.ShapeDtypeStruct((512, 1024), t) for t in outs]
    got = vmem_call(
        functools.partial(kernel, pieces, not before, last),
        scalars,
        (*blocks.values(), *fixed, *before),
        shapes,
        scratch,
        2 * 8 * len(pieces) * 512 * B * B,
        mib,
        [space] * len(pieces) + [pltpu.VMEM] * (len(fixed) + len(before)),
    )
    return list(got)


def body(h_blocks, h_cols, h_count, z_blocks, z_cols, z_count, x_perp):
    r, c = lax.axis_index("rows"), lax.axis_index("inner")
    m, p = r // 2, r % 2
    yh, ax, az, yl = m // 4, m % 4, c // 2, c % 2
    pos = jnp.stack([ax, yh, p, az, yl, m, c, r]).astype(jnp.int32)
    up_z, down_z, up_x, down_x = along_z(1), along_z(-1), along_x(1), along_x(-1)

    def at_place(v, row, column):
        return jnp.pad(v, ((row, 16 - row - v.shape[0]), (column, B - column - v.shape[1])))

    names = at_place(z_cols, 0, ZC) + at_place(h_cols, 0, HC)
    names = names + at_place(z_count[None, :], ZN, 0) + at_place(h_count[None, :], HN, 0)
    h_c = lax.dynamic_index_in_dim(h_blocks, c, 1, keepdims=False).reshape(512, B)
    z_slots = z_blocks.transpose(1, 0, 2, 3).reshape(4096, B)
    l = jnp.concatenate([z_slots, h_c, names.astype(BF)], axis=0)

    la, lb, ly = send(l, up_x), send(l, down_x), send(l, other_yh)
    xa, xb = send(x_perp, up_z), send(x_perp, down_z)
    l, la, lb, ly, x, xa, xb, z = after(l, la, lb, ly, x_perp, xa, xb, z_blocks)
    la2, lyb = send(la, up_x), send(ly, down_x)
    xy, xa2 = send(x, other_yl), send(xa, up_z)
    z_sib = send(z, other_core)
    la2, ly, lyb, xy, xa2, z_sib = after(la2, ly, lyb, xy, xa2, z_sib)
    lya, lyb2 = send(ly, up_x), send(lyb, down_x)
    xya, xyb, xya2 = send(xy, up_z), send(xy, down_z), send(xa2, other_yl)

    tile = jax.ShapeDtypeStruct((512, 1024), BF)

    def table_of(letters):
        return jnp.stack([v[LN : LN + 6, :16] for v in letters]).astype(jnp.int32)

    def w_part(letters, names, before, last):
        shapes = [jax.ShapeDtypeStruct((512, 1024), F32), tile] if last else [jax.ShapeDtypeStruct((1024, 1024), F32)]
        n = len(letters)
        scratch = [pltpu.VMEM((n, 512, B), BF)] * 2 + [pltpu.VMEM((1024, 1024), F32), pltpu.SemaphoreType.DMA((2, n))]
        spaces = [pl.ANY] * n + [pltpu.VMEM] * len(before)
        arrays = (*[in_hbm(v) for v in letters.values()], *before)
        kernel = functools.partial(w_kernel, tuple(letters), not before, last)
        return list(vmem_call(kernel, (names, pos), arrays, shapes, scratch, 8 * n * B**3, 22, spaces))

    early = {0: l, 1: lb, 2: la2, 3: la, 4: ly, 5: lyb}
    names_early = table_of([*early.values(), l, l])[None]
    ws = w_part(early, names_early, [], False)
    lya, lyb2, xya, xyb, xya2, *ws = after(lya, lyb2, xya, xyb, xya2, *ws)

    letters = [*early.values(), lyb2, lya]
    z_stripe, slots_zc, names = vmem_call(
        pick_kernel,
        (pos,),
        [in_hbm(v) for v in letters],
        [jax.ShapeDtypeStruct((*n, B), BF) for n in ((4096,), (8, 512), (8, 16))],
        [pltpu.SemaphoreType.DMA((3, 8))],
        0,
        2,
        pl.ANY,
        pl.ANY,
    )
    table = names[:, :6, :16].astype(jnp.int32)
    table = jnp.stack([table, send(table, other_core)])
    at = (table, pos)
    z_stripe_sib = send(z_stripe, other_core)
    w_mine, w_theirs = w_part({6: lyb2, 7: lya}, table, ws, True)
    w = (w_mine + send(w_theirs, other_core).astype(F32)).astype(BF)
    x_all = {OWN: x, UP: xa, DOWN: xb, PAIR: xy, FAR: xa2, PAIR_UP: xya, PAIR_DOWN: xyb, PAIR_FAR: xya2}
    v = vmem_call(
        functools.partial(coupled_kernel, tuple(x_all)),
        at,
        (*x_all.values(), z_stripe, z_stripe_sib),
        tile,
        [],
        2 * 64 * 512 * B * B,
        18,
    )

    v, w = after(v, w)
    va, vb, vy = send(v, up_x), send(v, down_x), send(v, other_yh)
    wa, wb = send(w, up_z), send(w, down_z)
    va, vb, vy, wa, wb, w, slots_zc = after(va, vb, vy, wa, wb, w, slots_zc)
    va2, vyb = send(va, up_x), send(vy, down_x)
    wy, wa2 = send(w, other_yl), send(wa, up_z)
    slots_zc_sib = send(slots_zc, other_core)

    def x_part(blocks, before, last):
        n = len(blocks)
        scratch = [pltpu.VMEM((1024, 512 * n), BF), pltpu.VMEM((512 * n, 1024), BF), pltpu.SemaphoreType.DMA((n,))]
        outs = [F32, BF] if last else [BF, BF]
        return part(x_out_kernel, at, blocks, (z, z_sib), before, last, outs, scratch, 14 + 3 * n, pl.ANY)

    def h_part(blocks, before, last):
        scratch = [pltpu.VMEM((512, 1024), F32)]
        return part(h_perp_kernel, at, blocks, (slots_zc, slots_zc_sib), before, last, [BF], scratch, 12 + len(blocks))

    va2, vy, vyb, wy, wa2, slots_zc_sib = after(va2, vy, vyb, wy, wa2, slots_zc_sib)
    vya, vyb2 = send(vy, up_x), send(vyb, down_x)
    wya, wyb, wya2 = send(wy, up_z), send(wy, down_z), send(wa2, other_yl)
    xs = x_part({OWN: v, UP: va, DOWN: vb, PAIR: vy, FAR: va2, PAIR_DOWN: vyb}, [], False)
    hs = h_part({OWN: w, UP: wa, DOWN: wb, PAIR: wy, FAR: wa2}, [], False)
    vya, vyb2, *hs = after(vya, vyb2, *hs)
    mine, theirs = x_part({PAIR_UP: vya, PAIR_FAR: vyb2}, xs, True)
    x_tile = (mine + send(theirs, other_core).astype(F32)).astype(BF)
    (h_tile,) = h_part({PAIR_UP: wya, PAIR_DOWN: wyb, PAIR_FAR: wya2}, hs, True)
    return h_tile, x_tile


def solution(mesh):
    in_specs = (
        P("rows", None, None, None),
        P("rows", None),
        P("rows"),
        P("rows", None, None, None),
        P("rows", None),
        P("rows"),
        P("rows", "inner"),
    )
    out_specs = (P("rows", "inner"), P("rows", "inner"))
    return jax.shard_map(body, mesh=mesh, in_specs=in_specs, out_specs=out_specs, check_vma=False)
```

time: 238 us -> 209 us (0.88)
  Pallas kernels: 62.2 us -> 40.7 us
  waiting for transfers between devices: 115 us -> 106 us
  starting transfers between devices: 42 us -> 49.1 us
  other arithmetic: 4.68 us -> 1.85 us
    pallas_call x7 -> x8, Pallas kernels: 62.2 us -> 40.7 us  [vmem_call(): pl.pallas_call(kernel, out_shape=out_shape, grid_spec=pltpu.PrefetchScala...]
    ppermute x34, waiting for transfers between devices: 115 us -> 106 us  [send(): lax.ppermute(value, AXES, [(number(*at), number(*to(*at))) for at in plac...]
    ppermute x34, starting transfers between devices: 42 us -> 49.1 us  [send(): lax.ppermute(value, AXES, [(number(*at), number(*to(*at))) for at in plac...]
    slice x7 -> x0, local copies, waits for them, and re-layouts: 3.95 us -> none  [body(): v[LN:LN + 4, :18]]
    unnamed x38 -> x31, local copies, waits for them, and re-layouts: 6.74 us -> 7.97 us
  transfers between devices with their start and end apart: 34 -> 34, of which waited for: 12 -> 17; matrix products, arithmetic and copies ran while one was open for 1% -> 3% of each run, Pallas kernels for 26% -> 18%
where the time goes in v3:
time: 209 us
  waiting for transfers between devices  106 us (51%)
  starting transfers between devices  49.1 us (23%)
  Pallas kernels  40.7 us (19%)
  local copies, waits for them, and re-layouts  10.2 us (5%)
    ppermute x34, waiting for transfers between devices, send(): lax.ppermute(value, AXES, [(number(*at), number(*to(*at))) for at in plac...  106 us
    ppermute x34, starting transfers between devices, send(): lax.ppermute(value, AXES, [(number(*at), number(*to(*at))) for at in plac...  49.1 us
    pallas_call x8, Pallas kernels, vmem_call(): pl.pallas_call(kernel, out_shape=out_shape, grid_spec=pltpu.PrefetchScala...  40.7 us
    unnamed x31, local copies, waits for them, and re-layouts  7.97 us
  transfers between devices with their start and end apart: 34, of which 17 were waited for; matrix products, arithmetic and copies ran while one was open for 3% of the time, Pallas kernels for 18%

profile of v3, /device:TPU:1, one launch (start us, length us, event | category | flops | bytes accessed | tf_op | source)
XLA Modules:
  0.0 208.7 jit_solution(15614951443744605703)
XLA Ops:
  2.4 3.8 %collective-permute-start.2 = (bf16[4624,128]{1,0:T(8,128)(2,1)S(1)}, bf16[4624,128]{1,0:T(8,128)(2,1)}, u32[]{:S(2)}, u32[]{:S(2)}) collective-permute-start(bf16[4624,128]{1,0:T(8,128)(2,1)S(1)} %pad_maximum_fusion.refs_0_), channel_id=1, source_target_pairs={{0,64},{1,65},{2,66},{3,67},{4,68},{5,69},{6,70},{7,71},{8,72},{9,... | collective-permute-start | bytes 3551240 | tf_op jit(solution)/shard_map/ppermute | solution.py:33
  6.2 2.5 %collective-permute-start.1 = (bf16[4624,128]{1,0:T(8,128)(2,1)S(1)}, bf16[4624,128]{1,0:T(8,128)(2,1)S(1)}, u32[]{:S(2)}, u32[]{:S(2)}) collective-permute-start(bf16[4624,128]{1,0:T(8,128)(2,1)S(1)} %pad_maximum_fusion.refs_0_), channel_id=1, source_target_pairs={{0,48},{1,49},{2,50},{3,51},{4,52},{5,53},{6,54},{7,55},{8,56},{9,... | collective-permute-start | bytes 3551240 | tf_op jit(solution)/shard_map/ppermute | solution.py:33
  12.5 22.6 %collective-permute-done.3.refs_1_ = bf16[512,1024]{1,0:T(8,128)(2,1)} collective-permute-done((bf16[512,1024]{1,0:T(8,128)(2,1)}, bf16[512,1024]{1,0:T(8,128)(2,1)}, u32[]{:S(2)}, u32[]{:S(2)}) %collective-permute-start.3) | collective-permute-done | bytes 1048608 | tf_op jit(solution)/shard_map/ppermute | solution.py:33
  39.8 3.3 %collective-permute-start.9 = (bf16[4,8,128,128]{3,2,1,0:T(8,128)(2,1)S(1)}, bf16[4,8,128,128]{3,2,1,0:T(8,128)(2,1)S(1)}, u32[]{:S(2)}, u32[]{:S(2)}) collective-permute-start(bf16[4,8,128,128]{3,2,1,0:T(8,128)(2,1)S(1)} %copy-done.1), channel_id=1, source_target_pairs={{0,8},{1,9},{2,10},{3,11},{4,12},{5,13},{6,14},{7,15},{8,0},{9,1},... | collective-permute-start | bytes 3145736 | tf_op jit(solution)/shard_map/ppermute | solution.py:33
  44.6 16.4 %collective-permute-done.7.refs_3_ = bf16[512,1024]{1,0:T(8,128)(2,1)} collective-permute-done((bf16[512,1024]{1,0:T(8,128)(2,1)}, bf16[512,1024]{1,0:T(8,128)(2,1)}, u32[]{:S(2)}, u32[]{:S(2)}) %collective-permute-start.7) | collective-permute-done | bytes 1048608 | tf_op jit(solution)/shard_map/ppermute | solution.py:33
  67.5 2.7 %collective-permute-start.11 = (bf16[4624,128]{1,0:T(8,128)(2,1)}, bf16[4624,128]{1,0:T(8,128)(2,1)S(1)}, u32[]{:S(2)}, u32[]{:S(2)}) collective-permute-start(bf16[4624,128]{1,0:T(8,128)(2,1)} %collective-permute-done.6.refs_5_), channel_id=1, source_target_pairs={{0,48},{1,49},{2,50},{3,51},{4,52},{5,53},{6,54},{7,55},{8,56},{9,... | collective-permute-start | bytes 3551240 | tf_op jit(solution)/shard_map/ppermute | solution.py:33
  74.3 3.5 %shard_map.86.refs_2_ = f32[1024,1024]{1,0:T(8,128)S(1)} custom-call(s32[1,8,6,16]{3,2,1,0:T(8,128)S(1)} %convert_element_type.29.table, s32[8]{0:T(128)S(1)} %stack.67.pos, bf16[4624,128]{1,0:T(8,128)(2,1)} %copy-done.4, bf16[4624,128]{1,0:T(8,128)(2,1)} %copy-done.5, bf16[4624,128]{1,0:T(8,128)(2,1)} %collective-permute-done.5.refs_2_, ...), custom_call_target="tpu_custom_call" | custom-call | flops 100663296 | bytes 11296768 | tf_op jit(solution)/shard_map/pallas_call | solution.py:76
  77.8 10.3 %collective-permute-done.14.refs_7_ = bf16[512,1024]{1,0:T(8,128)(2,1)S(1)} collective-permute-done((bf16[512,1024]{1,0:T(8,128)(2,1)}, bf16[512,1024]{1,0:T(8,128)(2,1)S(1)}, u32[]{:S(2)}, u32[]{:S(2)}) %collective-permute-start.14) | collective-permute-done | bytes 1048608 | tf_op jit(solution)/shard_map/ppermute | solution.py:33
  89.3 3.0 %collective-permute-done.10.refs_7_.refs_1_ = bf16[4624,128]{1,0:T(8,128)(2,1)S(1)} collective-permute-done((bf16[4624,128]{1,0:T(8,128)(2,1)}, bf16[4624,128]{1,0:T(8,128)(2,1)S(1)}, u32[]{:S(2)}, u32[]{:S(2)}) %collective-permute-start.10) | collective-permute-done | bytes 1183776 | tf_op jit(solution)/shard_map/ppermute | solution.py:33
  96.9 5.2 %collective-permute-start.15 = (s32[8,6,16]{2,1,0:T(8,128)S(1)}, s32[8,6,16]{2,1,0:T(8,128)S(1)}, u32[]{:S(2)}, u32[]{:S(2)}) collective-permute-start(s32[8,6,16]{2,1,0:T(8,128)S(1)} %get-tuple-element.97), channel_id=1, source_target_pairs={{0,8},{1,9},{2,10},{3,11},{4,12},{5,13},{6,14},{7,15},{8,0},{9,1},... | collective-permute-start | bytes 9224 | tf_op jit(solution)/shard_map/ppermute | solution.py:33
  103.0 3.3 %shard_map.89 = (f32[512,1024]{1,0:T(8,128)S(1)}, bf16[512,1024]{1,0:T(8,128)(2,1)S(1)}) custom-call(s32[2,8,6,16]{3,2,1,0:T(8,128)S(1)} %pad_add_fusion.table, s32[8]{0:T(128)S(1)} %stack.67.pos, bf16[4624,128]{1,0:T(8,128)(2,1)} %copy-done.7, bf16[4624,128]{1,0:T(8,128)(2,1)} %copy-done.6, f32[1024,1024]{1,0:T(8,128)S(1)} %shard_map.86.refs_2_), custom_call_target="tpu_custom_call" | custom-call | flops 33554432 | bytes 9707520 | tf_op jit(solution)/shard_map/pallas_call | solution.py:76
  106.7 6.3 %shard_map.88.refs_0_ = bf16[512,1024]{1,0:T(8,128)(2,1)S(1)} custom-call(s32[2,8,6,16]{3,2,1,0:T(8,128)S(1)} %pad_add_fusion.table, s32[8]{0:T(128)S(1)} %stack.67.pos, bf16[512,1024]{1,0:T(8,128)(2,1)} %refs_0_, bf16[512,1024]{1,0:T(8,128)(2,1)} %collective-permute-done.3.refs_1_, bf16[512,1024]{1,0:T(8,128)(2,1)S(1)} %copy-done.3, ...), custom_call_target="tpu_custom_call" | custom-call | flops 1073741824 | bytes 11534336 | tf_op jit(solution)/shard_map/pallas_call | solution.py:76
  113.4 2.9 %collective-permute-start.22 = (bf16[512,1024]{1,0:T(8,128)(2,1)S(1)}, bf16[512,1024]{1,0:T(8,128)(2,1)S(1)}, u32[]{:S(2)}, u32[]{:S(2)}) collective-permute-start(bf16[512,1024]{1,0:T(8,128)(2,1)S(1)} %add_convert_fusion.1.refs_0_), channel_id=1, source_target_pairs={{0,6},{1,7},{2,0},{3,1},{4,2},{5,3},{6,4},{7,5},{8,14},{9,15},{10,... | collective-permute-start | bytes 3145736 | tf_op jit(solution)/shard_map/ppermute | solution.py:33
  119.7 19.0 %collective-permute-done.22.refs_2_ = bf16[512,1024]{1,0:T(8,128)(2,1)S(1)} collective-permute-done((bf16[512,1024]{1,0:T(8,128)(2,1)S(1)}, bf16[512,1024]{1,0:T(8,128)(2,1)S(1)}, u32[]{:S(2)}, u32[]{:S(2)}) %collective-permute-start.22) | collective-permute-done | bytes 1048608 | tf_op jit(solution)/shard_map/ppermute | solution.py:33
  138.8 3.1 %collective-permute-done.21.refs_1_ = bf16[512,1024]{1,0:T(8,128)(2,1)S(1)} collective-permute-done((bf16[512,1024]{1,0:T(8,128)(2,1)S(1)}, bf16[512,1024]{1,0:T(8,128)(2,1)S(1)}, u32[]{:S(2)}, u32[]{:S(2)}) %collective-permute-start.21) | collective-permute-done | bytes 1048608 | tf_op jit(solution)/shard_map/ppermute | solution.py:33
  144.6 2.7 %collective-permute-start.24 = (bf16[512,1024]{1,0:T(8,128)(2,1)S(1)}, bf16[512,1024]{1,0:T(8,128)(2,1)S(1)}, u32[]{:S(2)}, u32[]{:S(2)}) collective-permute-start(bf16[512,1024]{1,0:T(8,128)(2,1)S(1)} %collective-permute-done.20.refs_3_), channel_id=1, source_target_pairs={{0,48},{1,49},{2,50},{3,51},{4,52},{5,53},{6,54},{7,55},{8,56},{9,... | collective-permute-start | bytes 3145736 | tf_op jit(solution)/shard_map/ppermute | solution.py:33
  147.3 2.5 %collective-permute-start.27 = (bf16[8,512,128]{2,1,0:T(8,128)(2,1)S(1)}, bf16[8,512,128]{2,1,0:T(8,128)(2,1)S(1)}, u32[]{:S(2)}, u32[]{:S(2)}) collective-permute-start(bf16[8,512,128]{2,1,0:T(8,128)(2,1)S(1)} %get-tuple-element.79.refs_5_.refs_3_), channel_id=1, source_target_pairs={{0,8},{1,9},{2,10},{3,11},{4,12},{5,13},{6,14},{7,15},{8,0},{9,1},... | collective-permute-start | bytes 3145736 | tf_op jit(solution)/shard_map/ppermute | solution.py:33
  149.8 18.8 %collective-permute-done.23.refs_4_ = bf16[512,1024]{1,0:T(8,128)(2,1)S(1)} collective-permute-done((bf16[512,1024]{1,0:T(8,128)(2,1)S(1)}, bf16[512,1024]{1,0:T(8,128)(2,1)S(1)}, u32[]{:S(2)}, u32[]{:S(2)}) %collective-permute-start.23) | collective-permute-done | bytes 1048608 | tf_op jit(solution)/shard_map/ppermute | solution.py:33
  170.7 2.7 %collective-permute-start.32 = (bf16[512,1024]{1,0:T(8,128)(2,1)S(1)}, bf16[512,1024]{1,0:T(8,128)(2,1)S(1)}, u32[]{:S(2)}, u32[]{:S(2)}) collective-permute-start(bf16[512,1024]{1,0:T(8,128)(2,1)S(1)} %collective-permute-done.24.refs_5_), channel_id=1, source_target_pairs={{0,48},{1,49},{2,50},{3,51},{4,52},{5,53},{6,54},{7,55},{8,56},{9,... | collective-permute-start | bytes 3145736 | tf_op jit(solution)/shard_map/ppermute | solution.py:33
  176.0 10.3 %shard_map.92 = (bf16[512,1024]{1,0:T(8,128)(2,1)S(1)}, bf16[512,1024]{1,0:T(8,128)(2,1)S(1)}) custom-call(s32[2,8,6,16]{3,2,1,0:T(8,128)S(1)} %pad_add_fusion.table, s32[8]{0:T(128)S(1)} %stack.67.pos, bf16[512,1024]{1,0:T(8,128)(2,1)S(1)} %shard_map.88.refs_0_, bf16[512,1024]{1,0:T(8,128)(2,1)S(1)} %collective-permute-done.18.refs_1_, ...), custom_call_target="tpu_custom_call" | custom-call | flops 805306368 | bytes 10485760 | tf_op jit(solution)/shard_map/pallas_call | solution.py:76
  186.3 5.3 %shard_map.90.refs_5_ = bf16[512,1024]{1,0:T(8,128)(2,1)S(1)} custom-call(s32[2,8,6,16]{3,2,1,0:T(8,128)S(1)} %pad_add_fusion.table, s32[8]{0:T(128)S(1)} %stack.67.pos, bf16[512,1024]{1,0:T(8,128)(2,1)S(1)} %add_convert_fusion.1.refs_0_, bf16[512,1024]{1,0:T(8,128)(2,1)S(1)} %collective-permute-done.21.refs_1_, ...), custom_call_target="tpu_custom_call" | custom-call | flops 671088640 | bytes 8388608 | tf_op jit(solution)/shard_map/pallas_call | solution.py:76
  193.1 4.6 %shard_map.93 = (f32[512,1024]{1,0:T(8,128)S(1)}, bf16[512,1024]{1,0:T(8,128)(2,1)S(1)}) custom-call(s32[2,8,6,16]{3,2,1,0:T(8,128)S(1)} %pad_add_fusion.table, s32[8]{0:T(128)S(1)} %stack.67.pos, bf16[512,1024]{1,0:T(8,128)(2,1)S(1)} %collective-permute-done.31.refs_0_, bf16[512,1024]{1,0:T(8,128)(2,1)S(1)} %collective-permute-done.32.refs_1_, ...), custom_call_target="tpu_custom_call" | custom-call | flops 268435456 | bytes 9437184 | tf_op jit(solution)/shard_map/pallas_call | solution.py:76
  197.8 4.7 %collective-permute-start.33 = (bf16[512,1024]{1,0:T(8,128)(2,1)S(1)}, bf16[512,1024]{1,0:T(8,128)(2,1)S(1)}, u32[]{:S(2)}, u32[]{:S(2)}) collective-permute-start(bf16[512,1024]{1,0:T(8,128)(2,1)S(1)} %get-tuple-element.95), channel_id=1, source_target_pairs={{0,8},{1,9},{2,10},{3,11},{4,12},{5,13},{6,14},{7,15},{8,0},{9,1},... | collective-permute-start | bytes 3145736 | tf_op jit(solution)/shard_map/ppermute | solution.py:33
  202.4 5.0 %shard_map.91 = bf16[512,1024]{1,0:T(8,128)(2,1)} custom-call(s32[2,8,6,16]{3,2,1,0:T(8,128)S(1)} %pad_add_fusion.table, s32[8]{0:T(128)S(1)} %stack.67.pos, bf16[512,1024]{1,0:T(8,128)(2,1)S(1)} %collective-permute-done.28.refs_0_, bf16[512,1024]{1,0:T(8,128)(2,1)S(1)} %collective-permute-done.29.refs_1_, ...), custom_call_target="tpu_custom_call" | custom-call | flops 402653184 | bytes 7340032 | tf_op jit(solution)/shard_map/pallas_call | solution.py:76
  (94 shorter events, 43.5 us)
Async XLA Ops:
  2.4 33.6 %collective-permute-start.2 = (bf16[4624,128]{1,0:T(8,128)(2,1)S(1)}, bf16[4624,128]{1,0:T(8,128)(2,1)}, u32[]{:S(2)}, u32[]{:S(2)}) collective-permute-start(bf16[4624,128]{1,0:T(8,128)(2,1)S(1)} %pad_maximum_fusion.refs_0_), channel_id=1, source_target_pairs={{0,64},{1,65},{2,66},{3,67},{4,68},{5,69},{6,70},{7,71},{8,72},{9,... | collective-permute-start | bytes 3551240 | tf_op jit(solution)/shard_map/ppermute | solution.py:33
  6.2 29.8 %collective-permute-start.1 = (bf16[4624,128]{1,0:T(8,128)(2,1)S(1)}, bf16[4624,128]{1,0:T(8,128)(2,1)S(1)}, u32[]{:S(2)}, u32[]{:S(2)}) collective-permute-start(bf16[4624,128]{1,0:T(8,128)(2,1)S(1)} %pad_maximum_fusion.refs_0_), channel_id=1, source_target_pairs={{0,48},{1,49},{2,50},{3,51},{4,52},{5,53},{6,54},{7,55},{8,56},{9,... | collective-permute-start | bytes 3551240 | tf_op jit(solution)/shard_map/ppermute | solution.py:33
  8.7 27.6 %collective-permute-start = (bf16[4624,128]{1,0:T(8,128)(2,1)S(1)}, bf16[4624,128]{1,0:T(8,128)(2,1)}, u32[]{:S(2)}, u32[]{:S(2)}) collective-permute-start(bf16[4624,128]{1,0:T(8,128)(2,1)S(1)} %pad_maximum_fusion.refs_0_), channel_id=1, source_target_pairs={{0,16},{1,17},{2,18},{3,19},{4,20},{5,21},{6,22},{7,23},{8,24},{9,... | collective-permute-start | bytes 3551240 | tf_op jit(solution)/shard_map/ppermute | solution.py:33
  8.7 26.3 %collective-permute-start.3 = (bf16[512,1024]{1,0:T(8,128)(2,1)}, bf16[512,1024]{1,0:T(8,128)(2,1)}, u32[]{:S(2)}, u32[]{:S(2)}) collective-permute-start(bf16[512,1024]{1,0:T(8,128)(2,1)} %refs_0_), channel_id=1, source_target_pairs={{0,2},{1,3},{2,4},{3,5},{4,6},{5,7},{6,0},{7,1},{8,10},{9,11},{10,... | collective-permute-start | bytes 3145736 | tf_op jit(solution)/shard_map/ppermute | solution.py:33
  10.3 24.7 %collective-permute-start.4 = (bf16[512,1024]{1,0:T(8,128)(2,1)}, bf16[512,1024]{1,0:T(8,128)(2,1)S(1)}, u32[]{:S(2)}, u32[]{:S(2)}) collective-permute-start(bf16[512,1024]{1,0:T(8,128)(2,1)} %refs_0_), channel_id=1, source_target_pairs={{0,6},{1,7},{2,0},{3,1},{4,2},{5,3},{6,4},{7,5},{8,14},{9,15},{10,... | collective-permute-start | bytes 3145736 | tf_op jit(solution)/shard_map/ppermute | solution.py:33
  36.3 26.4 %collective-permute-start.6 = (bf16[4624,128]{1,0:T(8,128)(2,1)}, bf16[4624,128]{1,0:T(8,128)(2,1)}, u32[]{:S(2)}, u32[]{:S(2)}) collective-permute-start(bf16[4624,128]{1,0:T(8,128)(2,1)} %collective-permute-done.2.refs_4_), channel_id=1, source_target_pairs={{0,48},{1,49},{2,50},{3,51},{4,52},{5,53},{6,54},{7,55},{8,56},{9,... | collective-permute-start | bytes 3551240 | tf_op jit(solution)/shard_map/ppermute | solution.py:33
  38.5 26.6 %collective-permute-start.5 = (bf16[4624,128]{1,0:T(8,128)(2,1)}, bf16[4624,128]{1,0:T(8,128)(2,1)}, u32[]{:S(2)}, u32[]{:S(2)}) collective-permute-start(bf16[4624,128]{1,0:T(8,128)(2,1)} %collective-permute-done.refs_3_), channel_id=1, source_target_pairs={{0,16},{1,17},{2,18},{3,19},{4,20},{5,21},{6,22},{7,23},{8,24},{9,... | collective-permute-start | bytes 3551240 | tf_op jit(solution)/shard_map/ppermute | solution.py:33
  38.9 23.9 %collective-permute-start.8 = (bf16[512,1024]{1,0:T(8,128)(2,1)}, bf16[512,1024]{1,0:T(8,128)(2,1)}, u32[]{:S(2)}, u32[]{:S(2)}) collective-permute-start(bf16[512,1024]{1,0:T(8,128)(2,1)} %collective-permute-done.3.refs_1_), channel_id=1, source_target_pairs={{0,2},{1,3},{2,4},{3,5},{4,6},{5,7},{6,0},{7,1},{8,10},{9,11},{10,... | collective-permute-start | bytes 3145736 | tf_op jit(solution)/shard_map/ppermute | solution.py:33
  39.8 22.9 %collective-permute-start.9 = (bf16[4,8,128,128]{3,2,1,0:T(8,128)(2,1)S(1)}, bf16[4,8,128,128]{3,2,1,0:T(8,128)(2,1)S(1)}, u32[]{:S(2)}, u32[]{:S(2)}) collective-permute-start(bf16[4,8,128,128]{3,2,1,0:T(8,128)(2,1)S(1)} %copy-done.1), channel_id=1, source_target_pairs={{0,8},{1,9},{2,10},{3,11},{4,12},{5,13},{6,14},{7,15},{8,0},{9,1},... | collective-permute-start | bytes 3145736 | tf_op jit(solution)/shard_map/ppermute | solution.py:33
  65.1 23.0 %collective-permute-start.13 = (bf16[512,1024]{1,0:T(8,128)(2,1)}, bf16[512,1024]{1,0:T(8,128)(2,1)S(1)}, u32[]{:S(2)}, u32[]{:S(2)}) collective-permute-start(bf16[512,1024]{1,0:T(8,128)(2,1)} %collective-permute-done.7.refs_3_), channel_id=1, source_target_pairs={{0,6},{1,7},{2,0},{3,1},{4,2},{5,3},{6,4},{7,5},{8,14},{9,15},{10,... | collective-permute-start | bytes 3145736 | tf_op jit(solution)/shard_map/ppermute | solution.py:33
  67.5 24.8 %collective-permute-start.10 = (bf16[4624,128]{1,0:T(8,128)(2,1)}, bf16[4624,128]{1,0:T(8,128)(2,1)S(1)}, u32[]{:S(2)}, u32[]{:S(2)}) collective-permute-start(bf16[4624,128]{1,0:T(8,128)(2,1)} %collective-permute-done.2.refs_4_), channel_id=1, source_target_pairs={{0,16},{1,17},{2,18},{3,19},{4,20},{5,21},{6,22},{7,23},{8,24},{9,... | collective-permute-start | bytes 3551240 | tf_op jit(solution)/shard_map/ppermute | solution.py:33
  67.5 24.8 %collective-permute-start.11 = (bf16[4624,128]{1,0:T(8,128)(2,1)}, bf16[4624,128]{1,0:T(8,128)(2,1)S(1)}, u32[]{:S(2)}, u32[]{:S(2)}) collective-permute-start(bf16[4624,128]{1,0:T(8,128)(2,1)} %collective-permute-done.6.refs_5_), channel_id=1, source_target_pairs={{0,48},{1,49},{2,50},{3,51},{4,52},{5,53},{6,54},{7,55},{8,56},{9,... | collective-permute-start | bytes 3551240 | tf_op jit(solution)/shard_map/ppermute | solution.py:33
  113.4 25.4 %collective-permute-start.22 = (bf16[512,1024]{1,0:T(8,128)(2,1)S(1)}, bf16[512,1024]{1,0:T(8,128)(2,1)S(1)}, u32[]{:S(2)}, u32[]{:S(2)}) collective-permute-start(bf16[512,1024]{1,0:T(8,128)(2,1)S(1)} %add_convert_fusion.1.refs_0_), channel_id=1, source_target_pairs={{0,6},{1,7},{2,0},{3,1},{4,2},{5,3},{6,4},{7,5},{8,14},{9,15},{10,... | collective-permute-start | bytes 3145736 | tf_op jit(solution)/shard_map/ppermute | solution.py:33
  116.4 25.5 %collective-permute-start.21 = (bf16[512,1024]{1,0:T(8,128)(2,1)S(1)}, bf16[512,1024]{1,0:T(8,128)(2,1)S(1)}, u32[]{:S(2)}, u32[]{:S(2)}) collective-permute-start(bf16[512,1024]{1,0:T(8,128)(2,1)S(1)} %add_convert_fusion.1.refs_0_), channel_id=1, source_target_pairs={{0,2},{1,3},{2,4},{3,5},{4,6},{5,7},{6,0},{7,1},{8,10},{9,11},{10,... | collective-permute-start | bytes 3145736 | tf_op jit(solution)/shard_map/ppermute | solution.py:33
  116.4 25.8 %collective-permute-start.20 = (bf16[512,1024]{1,0:T(8,128)(2,1)S(1)}, bf16[512,1024]{1,0:T(8,128)(2,1)S(1)}, u32[]{:S(2)}, u32[]{:S(2)}) collective-permute-start(bf16[512,1024]{1,0:T(8,128)(2,1)S(1)} %shard_map.88.refs_0_), channel_id=1, source_target_pairs={{0,64},{1,65},{2,66},{3,67},{4,68},{5,69},{6,70},{7,71},{8,72},{9,... | collective-permute-start | bytes 3145736 | tf_op jit(solution)/shard_map/ppermute | solution.py:33
  118.1 24.0 %collective-permute-start.19 = (bf16[512,1024]{1,0:T(8,128)(2,1)S(1)}, bf16[512,1024]{1,0:T(8,128)(2,1)S(1)}, u32[]{:S(2)}, u32[]{:S(2)}) collective-permute-start(bf16[512,1024]{1,0:T(8,128)(2,1)S(1)} %shard_map.88.refs_0_), channel_id=1, source_target_pairs={{0,48},{1,49},{2,50},{3,51},{4,52},{5,53},{6,54},{7,55},{8,56},{9,... | collective-permute-start | bytes 3145736 | tf_op jit(solution)/shard_map/ppermute | solution.py:33
  119.7 24.9 %collective-permute-start.18 = (bf16[512,1024]{1,0:T(8,128)(2,1)S(1)}, bf16[512,1024]{1,0:T(8,128)(2,1)S(1)}, u32[]{:S(2)}, u32[]{:S(2)}) collective-permute-start(bf16[512,1024]{1,0:T(8,128)(2,1)S(1)} %shard_map.88.refs_0_), channel_id=1, source_target_pairs={{0,16},{1,17},{2,18},{3,19},{4,20},{5,21},{6,22},{7,23},{8,24},{9,... | collective-permute-start | bytes 3145736 | tf_op jit(solution)/shard_map/ppermute | solution.py:33
  144.6 23.9 %collective-permute-start.23 = (bf16[512,1024]{1,0:T(8,128)(2,1)S(1)}, bf16[512,1024]{1,0:T(8,128)(2,1)S(1)}, u32[]{:S(2)}, u32[]{:S(2)}) collective-permute-start(bf16[512,1024]{1,0:T(8,128)(2,1)S(1)} %collective-permute-done.18.refs_1_), channel_id=1, source_target_pairs={{0,16},{1,17},{2,18},{3,19},{4,20},{5,21},{6,22},{7,23},{8,24},{9,... | collective-permute-start | bytes 3145736 | tf_op jit(solution)/shard_map/ppermute | solution.py:33
  144.6 23.9 %collective-permute-start.24 = (bf16[512,1024]{1,0:T(8,128)(2,1)S(1)}, bf16[512,1024]{1,0:T(8,128)(2,1)S(1)}, u32[]{:S(2)}, u32[]{:S(2)}) collective-permute-start(bf16[512,1024]{1,0:T(8,128)(2,1)S(1)} %collective-permute-done.20.refs_3_), channel_id=1, source_target_pairs={{0,48},{1,49},{2,50},{3,51},{4,52},{5,53},{6,54},{7,55},{8,56},{9,... | collective-permute-start | bytes 3145736 | tf_op jit(solution)/shard_map/ppermute | solution.py:33
  147.3 23.4 %collective-permute-start.26 = (bf16[512,1024]{1,0:T(8,128)(2,1)S(1)}, bf16[512,1024]{1,0:T(8,128)(2,1)S(1)}, u32[]{:S(2)}, u32[]{:S(2)}) collective-permute-start(bf16[512,1024]{1,0:T(8,128)(2,1)S(1)} %collective-permute-done.21.refs_1_), channel_id=1, source_target_pairs={{0,2},{1,3},{2,4},{3,5},{4,6},{5,7},{6,0},{7,1},{8,10},{9,11},{10,... | collective-permute-start | bytes 3145736 | tf_op jit(solution)/shard_map/ppermute | solution.py:33
  147.3 23.4 %collective-permute-start.27 = (bf16[8,512,128]{2,1,0:T(8,128)(2,1)S(1)}, bf16[8,512,128]{2,1,0:T(8,128)(2,1)S(1)}, u32[]{:S(2)}, u32[]{:S(2)}) collective-permute-start(bf16[8,512,128]{2,1,0:T(8,128)(2,1)S(1)} %get-tuple-element.79.refs_5_.refs_3_), channel_id=1, source_target_pairs={{0,8},{1,9},{2,10},{3,11},{4,12},{5,13},{6,14},{7,15},{8,0},{9,1},... | collective-permute-start | bytes 3145736 | tf_op jit(solution)/shard_map/ppermute | solution.py:33
  173.3 29.1 %collective-permute-start.29 = (bf16[512,1024]{1,0:T(8,128)(2,1)S(1)}, bf16[512,1024]{1,0:T(8,128)(2,1)S(1)}, u32[]{:S(2)}, u32[]{:S(2)}) collective-permute-start(bf16[512,1024]{1,0:T(8,128)(2,1)S(1)} %collective-permute-done.25.refs_3_), channel_id=1, source_target_pairs={{0,6},{1,7},{2,0},{3,1},{4,2},{5,3},{6,4},{7,5},{8,14},{9,15},{10,... | collective-permute-start | bytes 3145736 | tf_op jit(solution)/shard_map/ppermute | solution.py:33
  174.2 28.2 %collective-permute-start.28 = (bf16[512,1024]{1,0:T(8,128)(2,1)S(1)}, bf16[512,1024]{1,0:T(8,128)(2,1)S(1)}, u32[]{:S(2)}, u32[]{:S(2)}) collective-permute-start(bf16[512,1024]{1,0:T(8,128)(2,1)S(1)} %collective-permute-done.25.refs_3_), channel_id=1, source_target_pairs={{0,2},{1,3},{2,4},{3,5},{4,6},{5,7},{6,0},{7,1},{8,10},{9,11},{10,... | collective-permute-start | bytes 3145736 | tf_op jit(solution)/shard_map/ppermute | solution.py:33
  174.8 27.6 %collective-permute-start.30 = (bf16[512,1024]{1,0:T(8,128)(2,1)S(1)}, bf16[512,1024]{1,0:T(8,128)(2,1)S(1)}, u32[]{:S(2)}, u32[]{:S(2)}) collective-permute-start(bf16[512,1024]{1,0:T(8,128)(2,1)S(1)} %collective-permute-done.26.refs_4_), channel_id=1, source_target_pairs={{0,1},{1,0},{2,3},{3,2},{4,5},{5,4},{6,7},{7,6},{8,9},{9,8},{10,11... | collective-permute-start | bytes 3145736 | tf_op jit(solution)/shard_map/ppermute | solution.py:33
  (22 other events, 252.2 us)

commit v4 on v3

--- a/solution.py
+++ b/solution.py
@@ -289,11 +289,13 @@
 
     la, lb, ly = send(l, up_x), send(l, down_x), send(l, other_yh)
     xa, xb = send(x_perp, up_z), send(x_perp, down_z)
-    l, la, lb, ly, x, xa, xb, z = after(l, la, lb, ly, x_perp, xa, xb, z_blocks)
+    l, la, lb, ly, z = after(l, la, lb, ly, z_blocks)
+    x, xa, xb = after(x_perp, xa, xb)
     la2, lyb = send(la, up_x), send(ly, down_x)
     xy, xa2 = send(x, other_yl), send(xa, up_z)
     z_sib = send(z, other_core)
-    la2, ly, lyb, xy, xa2, z_sib = after(la2, ly, lyb, xy, xa2, z_sib)
+    la2, ly, lyb, z_sib = after(la2, ly, lyb, z_sib)
+    xy, xa2 = after(xy, xa2)
     lya, lyb2 = send(ly, up_x), send(lyb, down_x)
     xya, xyb, xya2 = send(xy, up_z), send(xy, down_z), send(xa2, other_yl)
 
@@ -307,7 +309,7 @@
         n = len(letters)
         scratch = [pltpu.VMEM((n, 512, B), BF)] * 2 + [pltpu.VMEM((1024, 1024), F32), pltpu.SemaphoreType.DMA((2, n))]
         spaces = [pl.ANY] * n + [pltpu.VMEM] * len(before)
-        arrays = (*[in_hbm(v) for v in letters.values()], *before)
+        arrays = (*[v if last else in_hbm(v) for v in letters.values()], *before)
         kernel = functools.partial(w_kernel, tuple(letters), not before, last)
         return list(vmem_call(kernel, (names, pos), arrays, shapes, scratch, 8 * n * B**3, 22, spaces))
 
@@ -320,7 +322,7 @@
     z_stripe, slots_zc, names = vmem_call(
         pick_kernel,
         (pos,),
-        [in_hbm(v) for v in letters],
+        [*[in_hbm(v) for v in early.values()], lyb2, lya],
         [jax.ShapeDtypeStruct((*n, B), BF) for n in ((4096,), (8, 512), (8, 16))],
         [pltpu.SemaphoreType.DMA((3, 8))],
         0,
@@ -348,7 +350,8 @@
     v, w = after(v, w)
     va, vb, vy = send(v, up_x), send(v, down_x), send(v, other_yh)
     wa, wb = send(w, up_z), send(w, down_z)
-    va, vb, vy, wa, wb, w, slots_zc = after(va, vb, vy, wa, wb, w, slots_zc)
+    va, vb, vy = after(va, vb, vy)
+    wa, wb, w, slots_zc = after(wa, wb, w, slots_zc)
     va2, vyb = send(va, up_x), send(vy, down_x)
     wy, wa2 = send(w, other_yl), send(wa, up_z)
     slots_zc_sib = send(slots_zc, other_core)
@@ -363,7 +366,8 @@
         scratch = [pltpu.VMEM((512, 1024), F32)]
         return part(h_perp_kernel, at, blocks, (slots_zc, slots_zc_sib), before, last, [BF], scratch, 12 + len(blocks))
 
-    va2, vy, vyb, wy, wa2, slots_zc_sib = after(va2, vy, vyb, wy, wa2, slots_zc_sib)
+    va2, vy, vyb = after(va2, vy, vyb)
+    wy, wa2, slots_zc_sib = after(wy, wa2, slots_zc_sib)
     vya, vyb2 = send(vy, up_x), send(vyb, down_x)
     wya, wyb, wya2 = send(wy, up_z), send(wy, down_z), send(wa2, other_yl)
     xs = x_part({OWN: v, UP: va, DOWN: vb, PAIR: vy, FAR: va2, PAIR_DOWN: vyb}, [], False)

time: 209 us -> 202 us (0.967)
  waiting for transfers between devices: 106 us -> 100 us
  local copies, waits for them, and re-layouts: 10.2 us -> 8 us
    ppermute x34, waiting for transfers between devices: 106 us -> 100 us  [send(): lax.ppermute(value, AXES, [(number(*at), number(*to(*at))) for at in plac...]
    unnamed x31 -> x27, local copies, waits for them, and re-layouts: 7.97 us -> 5.83 us
  transfers between devices with their start and end apart: 34 -> 34, of which waited for: 17 -> 13; matrix products, arithmetic and copies ran while one was open for 3% -> 3% of each run, Pallas kernels for 18% -> 19%
where the time goes in v4:
time: 202 us; the launch traced here: 201 us
  waiting for transfers between devices  100 us (50%)
  starting transfers between devices  49.6 us (25%)
  Pallas kernels  40.6 us (20%)
  local copies, waits for them, and re-layouts  8 us (4%)
    ppermute x34, waiting for transfers between devices, send(): lax.ppermute(value, AXES, [(number(*at), number(*to(*at))) for at in plac...  100 us
    ppermute x34, starting transfers between devices, send(): lax.ppermute(value, AXES, [(number(*at), number(*to(*at))) for at in plac...  49.6 us
    pallas_call x8, Pallas kernels, vmem_call(): pl.pallas_call(kernel, out_shape=out_shape, grid_spec=pltpu.PrefetchScala...  40.6 us
    unnamed x27, local copies, waits for them, and re-layouts  5.83 us
  transfers between devices with their start and end apart: 34, of which 13 were waited for; matrix products, arithmetic and copies ran while one was open for 3% of the time, Pallas kernels for 19%

profile of v4, /device:TPU:1, one launch (start us, length us, event | category | flops | bytes accessed | tf_op | source)
XLA Modules:
  0.0 201.3 jit_solution(15150344045967730290)
XLA Ops:
  2.4 3.8 %collective-permute-start.2 = (bf16[4624,128]{1,0:T(8,128)(2,1)S(1)}, bf16[4624,128]{1,0:T(8,128)(2,1)}, u32[]{:S(2)}, u32[]{:S(2)}) collective-permute-start(bf16[4624,128]{1,0:T(8,128)(2,1)S(1)} %pad_maximum_fusion.refs_0_), channel_id=1, source_target_pairs={{0,64},{1,65},{2,66},{3,67},{4,68},{5,69},{6,70},{7,71},{8,72},{9,... | collective-permute-start | bytes 3551240 | tf_op jit(solution)/shard_map/ppermute | solution.py:33
  12.5 19.4 %collective-permute-done.2.refs_4_ = bf16[4624,128]{1,0:T(8,128)(2,1)} collective-permute-done((bf16[4624,128]{1,0:T(8,128)(2,1)S(1)}, bf16[4624,128]{1,0:T(8,128)(2,1)}, u32[]{:S(2)}, u32[]{:S(2)}) %collective-permute-start.2) | collective-permute-done | bytes 1183776 | tf_op jit(solution)/shard_map/ppermute | solution.py:33
  33.1 3.2 %collective-permute-done.refs_3_ = bf16[4624,128]{1,0:T(8,128)(2,1)} collective-permute-done((bf16[4624,128]{1,0:T(8,128)(2,1)S(1)}, bf16[4624,128]{1,0:T(8,128)(2,1)}, u32[]{:S(2)}, u32[]{:S(2)}) %collective-permute-start) | collective-permute-done | bytes 1183776 | tf_op jit(solution)/shard_map/ppermute | solution.py:33
  40.8 3.3 %collective-permute-start.5 = (bf16[4,8,128,128]{3,2,1,0:T(8,128)(2,1)S(1)}, bf16[4,8,128,128]{3,2,1,0:T(8,128)(2,1)S(1)}, u32[]{:S(2)}, u32[]{:S(2)}) collective-permute-start(bf16[4,8,128,128]{3,2,1,0:T(8,128)(2,1)S(1)} %copy-done.1), channel_id=1, source_target_pairs={{0,8},{1,9},{2,10},{3,11},{4,12},{5,13},{6,14},{7,15},{8,0},{9,1},... | collective-permute-start | bytes 3145736 | tf_op jit(solution)/shard_map/ppermute | solution.py:33
  45.5 15.5 %collective-permute-done.10.refs_3_ = bf16[512,1024]{1,0:T(8,128)(2,1)} collective-permute-done((bf16[512,1024]{1,0:T(8,128)(2,1)}, bf16[512,1024]{1,0:T(8,128)(2,1)}, u32[]{:S(2)}, u32[]{:S(2)}) %collective-permute-start.10) | collective-permute-done | bytes 1048608 | tf_op jit(solution)/shard_map/ppermute | solution.py:33
  61.0 2.7 %collective-permute-done.11.refs_4_ = bf16[512,1024]{1,0:T(8,128)(2,1)} collective-permute-done((bf16[512,1024]{1,0:T(8,128)(2,1)}, bf16[512,1024]{1,0:T(8,128)(2,1)}, u32[]{:S(2)}, u32[]{:S(2)}) %collective-permute-start.11) | collective-permute-done | bytes 1048608 | tf_op jit(solution)/shard_map/ppermute | solution.py:33
  73.0 3.5 %shard_map.86.refs_2_ = f32[1024,1024]{1,0:T(8,128)S(1)} custom-call(s32[1,8,6,16]{3,2,1,0:T(8,128)S(1)} %convert_element_type.29.table, s32[8]{0:T(128)S(1)} %stack.67.pos, bf16[4624,128]{1,0:T(8,128)(2,1)} %copy-done.4, bf16[4624,128]{1,0:T(8,128)(2,1)} %copy-done.5, bf16[4624,128]{1,0:T(8,128)(2,1)} %collective-permute-done.3.refs_2_, ...), custom_call_target="tpu_custom_call" | custom-call | flops 100663296 | bytes 11296768 | tf_op jit(solution)/shard_map/pallas_call | solution.py:76
  76.5 9.3 %collective-permute-done.14.refs_7_ = bf16[512,1024]{1,0:T(8,128)(2,1)S(1)} collective-permute-done((bf16[512,1024]{1,0:T(8,128)(2,1)}, bf16[512,1024]{1,0:T(8,128)(2,1)S(1)}, u32[]{:S(2)}, u32[]{:S(2)}) %collective-permute-start.14) | collective-permute-done | bytes 1048608 | tf_op jit(solution)/shard_map/ppermute | solution.py:33
  86.5 4.3 %collective-permute-done.6.refs_7_.refs_1_ = bf16[4624,128]{1,0:T(8,128)(2,1)S(1)} collective-permute-done((bf16[4624,128]{1,0:T(8,128)(2,1)}, bf16[4624,128]{1,0:T(8,128)(2,1)S(1)}, u32[]{:S(2)}, u32[]{:S(2)}) %collective-permute-start.6) | collective-permute-done | bytes 1183776 | tf_op jit(solution)/shard_map/ppermute | solution.py:33
  93.2 5.5 %collective-permute-start.15 = (s32[8,6,16]{2,1,0:T(8,128)S(1)}, s32[8,6,16]{2,1,0:T(8,128)S(1)}, u32[]{:S(2)}, u32[]{:S(2)}) collective-permute-start(s32[8,6,16]{2,1,0:T(8,128)S(1)} %get-tuple-element.97), channel_id=1, source_target_pairs={{0,8},{1,9},{2,10},{3,11},{4,12},{5,13},{6,14},{7,15},{8,0},{9,1},... | collective-permute-start | bytes 9224 | tf_op jit(solution)/shard_map/ppermute | solution.py:33
  99.6 3.2 %shard_map.89 = (f32[512,1024]{1,0:T(8,128)S(1)}, bf16[512,1024]{1,0:T(8,128)(2,1)S(1)}) custom-call(s32[2,8,6,16]{3,2,1,0:T(8,128)S(1)} %pad_add_fusion.table, s32[8]{0:T(128)S(1)} %stack.67.pos, bf16[4624,128]{1,0:T(8,128)(2,1)S(1)} %collective-permute-done.7.refs_6_.refs_0_, bf16[4624,128]{1,0:T(8,128)(2,1)S(1)} %collective-permute-done.6.refs_7_.refs_1_, ...), custom_call_target="tpu_custom_call" | custom-call | flops 33554432 | bytes 9707520 | tf_op jit(solution)/shard_map/pallas_call | solution.py:76
  103.2 6.4 %shard_map.88.refs_0_ = bf16[512,1024]{1,0:T(8,128)(2,1)S(1)} custom-call(s32[2,8,6,16]{3,2,1,0:T(8,128)S(1)} %pad_add_fusion.table, s32[8]{0:T(128)S(1)} %stack.67.pos, bf16[512,1024]{1,0:T(8,128)(2,1)} %refs_0_, bf16[512,1024]{1,0:T(8,128)(2,1)} %collective-permute-done.8.refs_1_, bf16[512,1024]{1,0:T(8,128)(2,1)S(1)} %copy-done.3, ...), custom_call_target="tpu_custom_call" | custom-call | flops 1073741824 | bytes 11534336 | tf_op jit(solution)/shard_map/pallas_call | solution.py:76
  111.0 2.7 %collective-permute-start.27 = (bf16[512,1024]{1,0:T(8,128)(2,1)S(1)}, bf16[512,1024]{1,0:T(8,128)(2,1)S(1)}, u32[]{:S(2)}, u32[]{:S(2)}) collective-permute-start(bf16[512,1024]{1,0:T(8,128)(2,1)S(1)} %shard_map.88.refs_0_), channel_id=1, source_target_pairs={{0,48},{1,49},{2,50},{3,51},{4,52},{5,53},{6,54},{7,55},{8,56},{9,... | collective-permute-start | bytes 3145736 | tf_op jit(solution)/shard_map/ppermute | solution.py:33
  116.1 20.2 %collective-permute-done.28.refs_3_ = bf16[512,1024]{1,0:T(8,128)(2,1)S(1)} collective-permute-done((bf16[512,1024]{1,0:T(8,128)(2,1)S(1)}, bf16[512,1024]{1,0:T(8,128)(2,1)S(1)}, u32[]{:S(2)}, u32[]{:S(2)}) %collective-permute-start.28) | collective-permute-done | bytes 1048608 | tf_op jit(solution)/shard_map/ppermute | solution.py:33
  136.3 2.6 %collective-permute-done.26.refs_1_ = bf16[512,1024]{1,0:T(8,128)(2,1)S(1)} collective-permute-done((bf16[512,1024]{1,0:T(8,128)(2,1)S(1)}, bf16[512,1024]{1,0:T(8,128)(2,1)S(1)}, u32[]{:S(2)}, u32[]{:S(2)}) %collective-permute-start.26) | collective-permute-done | bytes 1048608 | tf_op jit(solution)/shard_map/ppermute | solution.py:33
  138.9 2.7 %collective-permute-start.30 = (bf16[512,1024]{1,0:T(8,128)(2,1)S(1)}, bf16[512,1024]{1,0:T(8,128)(2,1)S(1)}, u32[]{:S(2)}, u32[]{:S(2)}) collective-permute-start(bf16[512,1024]{1,0:T(8,128)(2,1)S(1)} %collective-permute-done.28.refs_3_), channel_id=1, source_target_pairs={{0,48},{1,49},{2,50},{3,51},{4,52},{5,53},{6,54},{7,55},{8,56},{9,... | collective-permute-start | bytes 3145736 | tf_op jit(solution)/shard_map/ppermute | solution.py:33
  142.1 2.7 %collective-permute-start.22 = (bf16[8,512,128]{2,1,0:T(8,128)(2,1)S(1)}, bf16[8,512,128]{2,1,0:T(8,128)(2,1)S(1)}, u32[]{:S(2)}, u32[]{:S(2)}) collective-permute-start(bf16[8,512,128]{2,1,0:T(8,128)(2,1)S(1)} %get-tuple-element.76.refs_5_.refs_3_), channel_id=1, source_target_pairs={{0,8},{1,9},{2,10},{3,11},{4,12},{5,13},{6,14},{7,15},{8,0},{9,1},... | collective-permute-start | bytes 3145736 | tf_op jit(solution)/shard_map/ppermute | solution.py:33
  144.9 18.3 %collective-permute-done.29.refs_4_ = bf16[512,1024]{1,0:T(8,128)(2,1)S(1)} collective-permute-done((bf16[512,1024]{1,0:T(8,128)(2,1)S(1)}, bf16[512,1024]{1,0:T(8,128)(2,1)S(1)}, u32[]{:S(2)}, u32[]{:S(2)}) %collective-permute-start.29) | collective-permute-done | bytes 1048608 | tf_op jit(solution)/shard_map/ppermute | solution.py:33
  163.2 2.7 %collective-permute-start.32 = (bf16[512,1024]{1,0:T(8,128)(2,1)S(1)}, bf16[512,1024]{1,0:T(8,128)(2,1)S(1)}, u32[]{:S(2)}, u32[]{:S(2)}) collective-permute-start(bf16[512,1024]{1,0:T(8,128)(2,1)S(1)} %collective-permute-done.30.refs_5_), channel_id=1, source_target_pairs={{0,48},{1,49},{2,50},{3,51},{4,52},{5,53},{6,54},{7,55},{8,56},{9,... | collective-permute-start | bytes 3145736 | tf_op jit(solution)/shard_map/ppermute | solution.py:33
  168.9 10.3 %shard_map.92 = (bf16[512,1024]{1,0:T(8,128)(2,1)S(1)}, bf16[512,1024]{1,0:T(8,128)(2,1)S(1)}) custom-call(s32[2,8,6,16]{3,2,1,0:T(8,128)S(1)} %pad_add_fusion.table, s32[8]{0:T(128)S(1)} %stack.67.pos, bf16[512,1024]{1,0:T(8,128)(2,1)S(1)} %shard_map.88.refs_0_, bf16[512,1024]{1,0:T(8,128)(2,1)S(1)} %collective-permute-done.26.refs_1_, ...), custom_call_target="tpu_custom_call" | custom-call | flops 805306368 | bytes 10485760 | tf_op jit(solution)/shard_map/pallas_call | solution.py:76
  179.1 5.3 %shard_map.90.refs_5_ = bf16[512,1024]{1,0:T(8,128)(2,1)S(1)} custom-call(s32[2,8,6,16]{3,2,1,0:T(8,128)S(1)} %pad_add_fusion.table, s32[8]{0:T(128)S(1)} %stack.67.pos, bf16[512,1024]{1,0:T(8,128)(2,1)S(1)} %add_convert_fusion.1.refs_0_, bf16[512,1024]{1,0:T(8,128)(2,1)S(1)} %collective-permute-done.18.refs_1_, ...), custom_call_target="tpu_custom_call" | custom-call | flops 671088640 | bytes 8388608 | tf_op jit(solution)/shard_map/pallas_call | solution.py:76
  186.6 4.6 %shard_map.93 = (f32[512,1024]{1,0:T(8,128)S(1)}, bf16[512,1024]{1,0:T(8,128)(2,1)S(1)}) custom-call(s32[2,8,6,16]{3,2,1,0:T(8,128)S(1)} %pad_add_fusion.table, s32[8]{0:T(128)S(1)} %stack.67.pos, bf16[512,1024]{1,0:T(8,128)(2,1)S(1)} %collective-permute-done.31.refs_0_, bf16[512,1024]{1,0:T(8,128)(2,1)S(1)} %collective-permute-done.32.refs_1_, ...), custom_call_target="tpu_custom_call" | custom-call | flops 268435456 | bytes 9437184 | tf_op jit(solution)/shard_map/pallas_call | solution.py:76
  191.2 3.8 %collective-permute-start.33 = (bf16[512,1024]{1,0:T(8,128)(2,1)S(1)}, bf16[512,1024]{1,0:T(8,128)(2,1)S(1)}, u32[]{:S(2)}, u32[]{:S(2)}) collective-permute-start(bf16[512,1024]{1,0:T(8,128)(2,1)S(1)} %get-tuple-element.95), channel_id=1, source_target_pairs={{0,8},{1,9},{2,10},{3,11},{4,12},{5,13},{6,14},{7,15},{8,0},{9,1},... | collective-permute-start | bytes 3145736 | tf_op jit(solution)/shard_map/ppermute | solution.py:33
  195.0 5.0 %shard_map.91 = bf16[512,1024]{1,0:T(8,128)(2,1)} custom-call(s32[2,8,6,16]{3,2,1,0:T(8,128)S(1)} %pad_add_fusion.table, s32[8]{0:T(128)S(1)} %stack.67.pos, bf16[512,1024]{1,0:T(8,128)(2,1)S(1)} %collective-permute-done.23.refs_0_, bf16[512,1024]{1,0:T(8,128)(2,1)S(1)} %collective-permute-done.24.refs_1_, ...), custom_call_target="tpu_custom_call" | custom-call | flops 402653184 | bytes 7340032 | tf_op jit(solution)/shard_map/pallas_call | solution.py:76
  (90 shorter events, 39.5 us)
Async XLA Ops:
  2.4 29.4 %collective-permute-start.2 = (bf16[4624,128]{1,0:T(8,128)(2,1)S(1)}, bf16[4624,128]{1,0:T(8,128)(2,1)}, u32[]{:S(2)}, u32[]{:S(2)}) collective-permute-start(bf16[4624,128]{1,0:T(8,128)(2,1)S(1)} %pad_maximum_fusion.refs_0_), channel_id=1, source_target_pairs={{0,64},{1,65},{2,66},{3,67},{4,68},{5,69},{6,70},{7,71},{8,72},{9,... | collective-permute-start | bytes 3551240 | tf_op jit(solution)/shard_map/ppermute | solution.py:33
  6.2 26.9 %collective-permute-start.1 = (bf16[4624,128]{1,0:T(8,128)(2,1)S(1)}, bf16[4624,128]{1,0:T(8,128)(2,1)S(1)}, u32[]{:S(2)}, u32[]{:S(2)}) collective-permute-start(bf16[4624,128]{1,0:T(8,128)(2,1)S(1)} %pad_maximum_fusion.refs_0_), channel_id=1, source_target_pairs={{0,48},{1,49},{2,50},{3,51},{4,52},{5,53},{6,54},{7,55},{8,56},{9,... | collective-permute-start | bytes 3551240 | tf_op jit(solution)/shard_map/ppermute | solution.py:33
  8.7 27.6 %collective-permute-start = (bf16[4624,128]{1,0:T(8,128)(2,1)S(1)}, bf16[4624,128]{1,0:T(8,128)(2,1)}, u32[]{:S(2)}, u32[]{:S(2)}) collective-permute-start(bf16[4624,128]{1,0:T(8,128)(2,1)S(1)} %pad_maximum_fusion.refs_0_), channel_id=1, source_target_pairs={{0,16},{1,17},{2,18},{3,19},{4,20},{5,21},{6,22},{7,23},{8,24},{9,... | collective-permute-start | bytes 3551240 | tf_op jit(solution)/shard_map/ppermute | solution.py:33
  8.7 29.1 %collective-permute-start.8 = (bf16[512,1024]{1,0:T(8,128)(2,1)}, bf16[512,1024]{1,0:T(8,128)(2,1)}, u32[]{:S(2)}, u32[]{:S(2)}) collective-permute-start(bf16[512,1024]{1,0:T(8,128)(2,1)} %refs_0_), channel_id=1, source_target_pairs={{0,2},{1,3},{2,4},{3,5},{4,6},{5,7},{6,0},{7,1},{8,10},{9,11},{10,... | collective-permute-start | bytes 3145736 | tf_op jit(solution)/shard_map/ppermute | solution.py:33
  10.3 27.5 %collective-permute-start.9 = (bf16[512,1024]{1,0:T(8,128)(2,1)}, bf16[512,1024]{1,0:T(8,128)(2,1)S(1)}, u32[]{:S(2)}, u32[]{:S(2)}) collective-permute-start(bf16[512,1024]{1,0:T(8,128)(2,1)} %refs_0_), channel_id=1, source_target_pairs={{0,6},{1,7},{2,0},{3,1},{4,2},{5,3},{6,4},{7,5},{8,14},{9,15},{10,... | collective-permute-start | bytes 3145736 | tf_op jit(solution)/shard_map/ppermute | solution.py:33
  36.3 29.9 %collective-permute-start.4 = (bf16[4624,128]{1,0:T(8,128)(2,1)}, bf16[4624,128]{1,0:T(8,128)(2,1)}, u32[]{:S(2)}, u32[]{:S(2)}) collective-permute-start(bf16[4624,128]{1,0:T(8,128)(2,1)} %collective-permute-done.2.refs_4_), channel_id=1, source_target_pairs={{0,48},{1,49},{2,50},{3,51},{4,52},{5,53},{6,54},{7,55},{8,56},{9,... | collective-permute-start | bytes 3551240 | tf_op jit(solution)/shard_map/ppermute | solution.py:33
  36.6 29.6 %collective-permute-start.3 = (bf16[4624,128]{1,0:T(8,128)(2,1)}, bf16[4624,128]{1,0:T(8,128)(2,1)}, u32[]{:S(2)}, u32[]{:S(2)}) collective-permute-start(bf16[4624,128]{1,0:T(8,128)(2,1)} %collective-permute-done.refs_3_), channel_id=1, source_target_pairs={{0,16},{1,17},{2,18},{3,19},{4,20},{5,21},{6,22},{7,23},{8,24},{9,... | collective-permute-start | bytes 3551240 | tf_op jit(solution)/shard_map/ppermute | solution.py:33
  39.2 24.5 %collective-permute-start.11 = (bf16[512,1024]{1,0:T(8,128)(2,1)}, bf16[512,1024]{1,0:T(8,128)(2,1)}, u32[]{:S(2)}, u32[]{:S(2)}) collective-permute-start(bf16[512,1024]{1,0:T(8,128)(2,1)} %collective-permute-done.8.refs_1_), channel_id=1, source_target_pairs={{0,2},{1,3},{2,4},{3,5},{4,6},{5,7},{6,0},{7,1},{8,10},{9,11},{10,... | collective-permute-start | bytes 3145736 | tf_op jit(solution)/shard_map/ppermute | solution.py:33
  40.8 24.4 %collective-permute-start.5 = (bf16[4,8,128,128]{3,2,1,0:T(8,128)(2,1)S(1)}, bf16[4,8,128,128]{3,2,1,0:T(8,128)(2,1)S(1)}, u32[]{:S(2)}, u32[]{:S(2)}) collective-permute-start(bf16[4,8,128,128]{3,2,1,0:T(8,128)(2,1)S(1)} %copy-done.1), channel_id=1, source_target_pairs={{0,8},{1,9},{2,10},{3,11},{4,12},{5,13},{6,14},{7,15},{8,0},{9,1},... | collective-permute-start | bytes 3145736 | tf_op jit(solution)/shard_map/ppermute | solution.py:33
  66.3 24.5 %collective-permute-start.6 = (bf16[4624,128]{1,0:T(8,128)(2,1)}, bf16[4624,128]{1,0:T(8,128)(2,1)S(1)}, u32[]{:S(2)}, u32[]{:S(2)}) collective-permute-start(bf16[4624,128]{1,0:T(8,128)(2,1)} %collective-permute-done.2.refs_4_), channel_id=1, source_target_pairs={{0,16},{1,17},{2,18},{3,19},{4,20},{5,21},{6,22},{7,23},{8,24},{9,... | collective-permute-start | bytes 3551240 | tf_op jit(solution)/shard_map/ppermute | solution.py:33
  66.6 24.2 %collective-permute-start.7 = (bf16[4624,128]{1,0:T(8,128)(2,1)}, bf16[4624,128]{1,0:T(8,128)(2,1)S(1)}, u32[]{:S(2)}, u32[]{:S(2)}) collective-permute-start(bf16[4624,128]{1,0:T(8,128)(2,1)} %collective-permute-done.4.refs_5_), channel_id=1, source_target_pairs={{0,48},{1,49},{2,50},{3,51},{4,52},{5,53},{6,54},{7,55},{8,56},{9,... | collective-permute-start | bytes 3551240 | tf_op jit(solution)/shard_map/ppermute | solution.py:33
  109.9 26.4 %collective-permute-start.28 = (bf16[512,1024]{1,0:T(8,128)(2,1)S(1)}, bf16[512,1024]{1,0:T(8,128)(2,1)S(1)}, u32[]{:S(2)}, u32[]{:S(2)}) collective-permute-start(bf16[512,1024]{1,0:T(8,128)(2,1)S(1)} %shard_map.88.refs_0_), channel_id=1, source_target_pairs={{0,64},{1,65},{2,66},{3,67},{4,68},{5,69},{6,70},{7,71},{8,72},{9,... | collective-permute-start | bytes 3145736 | tf_op jit(solution)/shard_map/ppermute | solution.py:33
  111.0 25.3 %collective-permute-start.27 = (bf16[512,1024]{1,0:T(8,128)(2,1)S(1)}, bf16[512,1024]{1,0:T(8,128)(2,1)S(1)}, u32[]{:S(2)}, u32[]{:S(2)}) collective-permute-start(bf16[512,1024]{1,0:T(8,128)(2,1)S(1)} %shard_map.88.refs_0_), channel_id=1, source_target_pairs={{0,48},{1,49},{2,50},{3,51},{4,52},{5,53},{6,54},{7,55},{8,56},{9,... | collective-permute-start | bytes 3145736 | tf_op jit(solution)/shard_map/ppermute | solution.py:33
  113.7 25.2 %collective-permute-start.26 = (bf16[512,1024]{1,0:T(8,128)(2,1)S(1)}, bf16[512,1024]{1,0:T(8,128)(2,1)S(1)}, u32[]{:S(2)}, u32[]{:S(2)}) collective-permute-start(bf16[512,1024]{1,0:T(8,128)(2,1)S(1)} %shard_map.88.refs_0_), channel_id=1, source_target_pairs={{0,16},{1,17},{2,18},{3,19},{4,20},{5,21},{6,22},{7,23},{8,24},{9,... | collective-permute-start | bytes 3145736 | tf_op jit(solution)/shard_map/ppermute | solution.py:33
  113.7 27.9 %collective-permute-start.19 = (bf16[512,1024]{1,0:T(8,128)(2,1)S(1)}, bf16[512,1024]{1,0:T(8,128)(2,1)S(1)}, u32[]{:S(2)}, u32[]{:S(2)}) collective-permute-start(bf16[512,1024]{1,0:T(8,128)(2,1)S(1)} %add_convert_fusion.1.refs_0_), channel_id=1, source_target_pairs={{0,6},{1,7},{2,0},{3,1},{4,2},{5,3},{6,4},{7,5},{8,14},{9,15},{10,... | collective-permute-start | bytes 3145736 | tf_op jit(solution)/shard_map/ppermute | solution.py:33
  116.1 25.5 %collective-permute-start.18 = (bf16[512,1024]{1,0:T(8,128)(2,1)S(1)}, bf16[512,1024]{1,0:T(8,128)(2,1)S(1)}, u32[]{:S(2)}, u32[]{:S(2)}) collective-permute-start(bf16[512,1024]{1,0:T(8,128)(2,1)S(1)} %add_convert_fusion.1.refs_0_), channel_id=1, source_target_pairs={{0,2},{1,3},{2,4},{3,5},{4,6},{5,7},{6,0},{7,1},{8,10},{9,11},{10,... | collective-permute-start | bytes 3145736 | tf_op jit(solution)/shard_map/ppermute | solution.py:33
  138.9 24.3 %collective-permute-start.29 = (bf16[512,1024]{1,0:T(8,128)(2,1)S(1)}, bf16[512,1024]{1,0:T(8,128)(2,1)S(1)}, u32[]{:S(2)}, u32[]{:S(2)}) collective-permute-start(bf16[512,1024]{1,0:T(8,128)(2,1)S(1)} %collective-permute-done.26.refs_1_), channel_id=1, source_target_pairs={{0,16},{1,17},{2,18},{3,19},{4,20},{5,21},{6,22},{7,23},{8,24},{9,... | collective-permute-start | bytes 3145736 | tf_op jit(solution)/shard_map/ppermute | solution.py:33
  138.9 24.3 %collective-permute-start.30 = (bf16[512,1024]{1,0:T(8,128)(2,1)S(1)}, bf16[512,1024]{1,0:T(8,128)(2,1)S(1)}, u32[]{:S(2)}, u32[]{:S(2)}) collective-permute-start(bf16[512,1024]{1,0:T(8,128)(2,1)S(1)} %collective-permute-done.28.refs_3_), channel_id=1, source_target_pairs={{0,48},{1,49},{2,50},{3,51},{4,52},{5,53},{6,54},{7,55},{8,56},{9,... | collective-permute-start | bytes 3145736 | tf_op jit(solution)/shard_map/ppermute | solution.py:33
  141.6 24.3 %collective-permute-start.20 = (bf16[512,1024]{1,0:T(8,128)(2,1)S(1)}, bf16[512,1024]{1,0:T(8,128)(2,1)S(1)}, u32[]{:S(2)}, u32[]{:S(2)}) collective-permute-start(bf16[512,1024]{1,0:T(8,128)(2,1)S(1)} %add_convert_fusion.1.refs_0_), channel_id=1, source_target_pairs={{0,1},{1,0},{2,3},{3,2},{4,5},{5,4},{6,7},{7,6},{8,9},{9,8},{10,11... | collective-permute-start | bytes 3145736 | tf_op jit(solution)/shard_map/ppermute | solution.py:33
  141.6 24.3 %collective-permute-start.21 = (bf16[512,1024]{1,0:T(8,128)(2,1)S(1)}, bf16[512,1024]{1,0:T(8,128)(2,1)S(1)}, u32[]{:S(2)}, u32[]{:S(2)}) collective-permute-start(bf16[512,1024]{1,0:T(8,128)(2,1)S(1)} %collective-permute-done.18.refs_1_), channel_id=1, source_target_pairs={{0,2},{1,3},{2,4},{3,5},{4,6},{5,7},{6,0},{7,1},{8,10},{9,11},{10,... | collective-permute-start | bytes 3145736 | tf_op jit(solution)/shard_map/ppermute | solution.py:33
  142.1 23.7 %collective-permute-start.22 = (bf16[8,512,128]{2,1,0:T(8,128)(2,1)S(1)}, bf16[8,512,128]{2,1,0:T(8,128)(2,1)S(1)}, u32[]{:S(2)}, u32[]{:S(2)}) collective-permute-start(bf16[8,512,128]{2,1,0:T(8,128)(2,1)S(1)} %get-tuple-element.76.refs_5_.refs_3_), channel_id=1, source_target_pairs={{0,8},{1,9},{2,10},{3,11},{4,12},{5,13},{6,14},{7,15},{8,0},{9,1},... | collective-permute-start | bytes 3145736 | tf_op jit(solution)/shard_map/ppermute | solution.py:33
  165.9 29.1 %collective-permute-start.24 = (bf16[512,1024]{1,0:T(8,128)(2,1)S(1)}, bf16[512,1024]{1,0:T(8,128)(2,1)S(1)}, u32[]{:S(2)}, u32[]{:S(2)}) collective-permute-start(bf16[512,1024]{1,0:T(8,128)(2,1)S(1)} %collective-permute-done.20.refs_3_), channel_id=1, source_target_pairs={{0,6},{1,7},{2,0},{3,1},{4,2},{5,3},{6,4},{7,5},{8,14},{9,15},{10,... | collective-permute-start | bytes 3145736 | tf_op jit(solution)/shard_map/ppermute | solution.py:33
  168.3 26.7 %collective-permute-start.23 = (bf16[512,1024]{1,0:T(8,128)(2,1)S(1)}, bf16[512,1024]{1,0:T(8,128)(2,1)S(1)}, u32[]{:S(2)}, u32[]{:S(2)}) collective-permute-start(bf16[512,1024]{1,0:T(8,128)(2,1)S(1)} %collective-permute-done.20.refs_3_), channel_id=1, source_target_pairs={{0,2},{1,3},{2,4},{3,5},{4,6},{5,7},{6,0},{7,1},{8,10},{9,11},{10,... | collective-permute-start | bytes 3145736 | tf_op jit(solution)/shard_map/ppermute | solution.py:33
  168.3 26.7 %collective-permute-start.25 = (bf16[512,1024]{1,0:T(8,128)(2,1)S(1)}, bf16[512,1024]{1,0:T(8,128)(2,1)S(1)}, u32[]{:S(2)}, u32[]{:S(2)}) collective-permute-start(bf16[512,1024]{1,0:T(8,128)(2,1)S(1)} %collective-permute-done.21.refs_4_), channel_id=1, source_target_pairs={{0,1},{1,0},{2,3},{3,2},{4,5},{5,4},{6,7},{7,6},{8,9},{9,8},{10,11... | collective-permute-start | bytes 3145736 | tf_op jit(solution)/shard_map/ppermute | solution.py:33
  (20 other events, 254.9 us)

commit v5 on v4

--- a/solution.py
+++ b/solution.py
@@ -350,8 +350,8 @@
     v, w = after(v, w)
     va, vb, vy = send(v, up_x), send(v, down_x), send(v, other_yh)
     wa, wb = send(w, up_z), send(w, down_z)
-    va, vb, vy = after(va, vb, vy)
-    wa, wb, w, slots_zc = after(wa, wb, w, slots_zc)
+    va, vy = after(va, vy)
+    vb, wa, wb, w, slots_zc = after(vb, wa, wb, w, slots_zc)
     va2, vyb = send(va, up_x), send(vy, down_x)
     wy, wa2 = send(w, other_yl), send(wa, up_z)
     slots_zc_sib = send(slots_zc, other_core)

time: 202 us -> 200 us (0.990)
  no operation moved by 1% of the time
where the time goes in v5:
time: 200 us; the launch traced here: 199 us
  waiting for transfers between devices  98.7 us (49%)
  starting transfers between devices  49.1 us (25%)
  Pallas kernels  40.6 us (20%)
  local copies, waits for them, and re-layouts  8 us (4%)
    ppermute x34, waiting for transfers between devices, send(): lax.ppermute(value, AXES, [(number(*at), number(*to(*at))) for at in plac...  98.7 us
    ppermute x34, starting transfers between devices, send(): lax.ppermute(value, AXES, [(number(*at), number(*to(*at))) for at in plac...  49.1 us
    pallas_call x8, Pallas kernels, vmem_call(): pl.pallas_call(kernel, out_shape=out_shape, grid_spec=pltpu.PrefetchScala...  40.6 us
    unnamed x27, local copies, waits for them, and re-layouts  5.83 us
  transfers between devices with their start and end apart: 34, of which 13 were waited for; matrix products, arithmetic and copies ran while one was open for 3% of the time, Pallas kernels for 19%

profile of v5, /device:TPU:1, one launch (start us, length us, event | category | flops | bytes accessed | tf_op | source)
XLA Modules:
  0.0 199.1 jit_solution(13825370351165532357)
XLA Ops:
  2.4 3.8 %collective-permute-start.2 = (bf16[4624,128]{1,0:T(8,128)(2,1)S(1)}, bf16[4624,128]{1,0:T(8,128)(2,1)}, u32[]{:S(2)}, u32[]{:S(2)}) collective-permute-start(bf16[4624,128]{1,0:T(8,128)(2,1)S(1)} %pad_maximum_fusion.refs_0_), channel_id=1, source_target_pairs={{0,64},{1,65},{2,66},{3,67},{4,68},{5,69},{6,70},{7,71},{8,72},{9,... | collective-permute-start | bytes 3551240 | tf_op jit(solution)/shard_map/ppermute | solution.py:33
  6.2 2.5 %collective-permute-start.1 = (bf16[4624,128]{1,0:T(8,128)(2,1)S(1)}, bf16[4624,128]{1,0:T(8,128)(2,1)S(1)}, u32[]{:S(2)}, u32[]{:S(2)}) collective-permute-start(bf16[4624,128]{1,0:T(8,128)(2,1)S(1)} %pad_maximum_fusion.refs_0_), channel_id=1, source_target_pairs={{0,48},{1,49},{2,50},{3,51},{4,52},{5,53},{6,54},{7,55},{8,56},{9,... | collective-permute-start | bytes 3551240 | tf_op jit(solution)/shard_map/ppermute | solution.py:33
  12.5 19.4 %collective-permute-done.2.refs_4_ = bf16[4624,128]{1,0:T(8,128)(2,1)} collective-permute-done((bf16[4624,128]{1,0:T(8,128)(2,1)S(1)}, bf16[4624,128]{1,0:T(8,128)(2,1)}, u32[]{:S(2)}, u32[]{:S(2)}) %collective-permute-start.2) | collective-permute-done | bytes 1183776 | tf_op jit(solution)/shard_map/ppermute | solution.py:33
  33.1 3.2 %collective-permute-done.refs_3_ = bf16[4624,128]{1,0:T(8,128)(2,1)} collective-permute-done((bf16[4624,128]{1,0:T(8,128)(2,1)S(1)}, bf16[4624,128]{1,0:T(8,128)(2,1)}, u32[]{:S(2)}, u32[]{:S(2)}) %collective-permute-start) | collective-permute-done | bytes 1183776 | tf_op jit(solution)/shard_map/ppermute | solution.py:33
  40.8 3.3 %collective-permute-start.5 = (bf16[4,8,128,128]{3,2,1,0:T(8,128)(2,1)S(1)}, bf16[4,8,128,128]{3,2,1,0:T(8,128)(2,1)S(1)}, u32[]{:S(2)}, u32[]{:S(2)}) collective-permute-start(bf16[4,8,128,128]{3,2,1,0:T(8,128)(2,1)S(1)} %copy-done.1), channel_id=1, source_target_pairs={{0,8},{1,9},{2,10},{3,11},{4,12},{5,13},{6,14},{7,15},{8,0},{9,1},... | collective-permute-start | bytes 3145736 | tf_op jit(solution)/shard_map/ppermute | solution.py:33
  45.5 15.5 %collective-permute-done.10.refs_3_ = bf16[512,1024]{1,0:T(8,128)(2,1)} collective-permute-done((bf16[512,1024]{1,0:T(8,128)(2,1)}, bf16[512,1024]{1,0:T(8,128)(2,1)}, u32[]{:S(2)}, u32[]{:S(2)}) %collective-permute-start.10) | collective-permute-done | bytes 1048608 | tf_op jit(solution)/shard_map/ppermute | solution.py:33
  61.0 2.7 %collective-permute-done.11.refs_4_ = bf16[512,1024]{1,0:T(8,128)(2,1)} collective-permute-done((bf16[512,1024]{1,0:T(8,128)(2,1)}, bf16[512,1024]{1,0:T(8,128)(2,1)}, u32[]{:S(2)}, u32[]{:S(2)}) %collective-permute-start.11) | collective-permute-done | bytes 1048608 | tf_op jit(solution)/shard_map/ppermute | solution.py:33
  73.0 3.5 %shard_map.86.refs_2_ = f32[1024,1024]{1,0:T(8,128)S(1)} custom-call(s32[1,8,6,16]{3,2,1,0:T(8,128)S(1)} %convert_element_type.29.table, s32[8]{0:T(128)S(1)} %stack.67.pos, bf16[4624,128]{1,0:T(8,128)(2,1)} %copy-done.4, bf16[4624,128]{1,0:T(8,128)(2,1)} %copy-done.5, bf16[4624,128]{1,0:T(8,128)(2,1)} %collective-permute-done.3.refs_2_, ...), custom_call_target="tpu_custom_call" | custom-call | flops 100663296 | bytes 11296768 | tf_op jit(solution)/shard_map/pallas_call | solution.py:76
  76.5 9.3 %collective-permute-done.14.refs_7_ = bf16[512,1024]{1,0:T(8,128)(2,1)S(1)} collective-permute-done((bf16[512,1024]{1,0:T(8,128)(2,1)}, bf16[512,1024]{1,0:T(8,128)(2,1)S(1)}, u32[]{:S(2)}, u32[]{:S(2)}) %collective-permute-start.14) | collective-permute-done | bytes 1048608 | tf_op jit(solution)/shard_map/ppermute | solution.py:33
  86.5 4.3 %collective-permute-done.6.refs_7_.refs_1_ = bf16[4624,128]{1,0:T(8,128)(2,1)S(1)} collective-permute-done((bf16[4624,128]{1,0:T(8,128)(2,1)}, bf16[4624,128]{1,0:T(8,128)(2,1)S(1)}, u32[]{:S(2)}, u32[]{:S(2)}) %collective-permute-start.6) | collective-permute-done | bytes 1183776 | tf_op jit(solution)/shard_map/ppermute | solution.py:33
  90.7 2.5 %shard_map.87 = (bf16[4096,128]{1,0:T(8,128)(2,1)S(1)}, bf16[8,512,128]{2,1,0:T(8,128)(2,1)S(1)}, bf16[8,16,128]{2,1,0:T(8,128)(2,1)S(1)}) custom-call(s32[8]{0:T(128)S(1)} %stack.67.pos, bf16[4624,128]{1,0:T(8,128)(2,1)} %copy-done.4, bf16[4624,128]{1,0:T(8,128)(2,1)} %copy-done.5, bf16[4624,128]{1,0:T(8,128)(2,1)} %collective-permute-done.3.refs_2_, ...), custom_call_target="tpu_custom_call" | custom-call | bytes 11599872 | tf_op jit(solution)/shard_map/pallas_call | solution.py:76
  93.2 5.5 %collective-permute-start.15 = (s32[8,6,16]{2,1,0:T(8,128)S(1)}, s32[8,6,16]{2,1,0:T(8,128)S(1)}, u32[]{:S(2)}, u32[]{:S(2)}) collective-permute-start(s32[8,6,16]{2,1,0:T(8,128)S(1)} %get-tuple-element.97), channel_id=1, source_target_pairs={{0,8},{1,9},{2,10},{3,11},{4,12},{5,13},{6,14},{7,15},{8,0},{9,1},... | collective-permute-start | bytes 9224 | tf_op jit(solution)/shard_map/ppermute | solution.py:33
  99.6 3.1 %shard_map.89 = (f32[512,1024]{1,0:T(8,128)S(1)}, bf16[512,1024]{1,0:T(8,128)(2,1)S(1)}) custom-call(s32[2,8,6,16]{3,2,1,0:T(8,128)S(1)} %pad_add_fusion.table, s32[8]{0:T(128)S(1)} %stack.67.pos, bf16[4624,128]{1,0:T(8,128)(2,1)S(1)} %collective-permute-done.7.refs_6_.refs_0_, bf16[4624,128]{1,0:T(8,128)(2,1)S(1)} %collective-permute-done.6.refs_7_.refs_1_, ...), custom_call_target="tpu_custom_call" | custom-call | flops 33554432 | bytes 9707520 | tf_op jit(solution)/shard_map/pallas_call | solution.py:76
  103.2 6.4 %shard_map.88.refs_0_ = bf16[512,1024]{1,0:T(8,128)(2,1)S(1)} custom-call(s32[2,8,6,16]{3,2,1,0:T(8,128)S(1)} %pad_add_fusion.table, s32[8]{0:T(128)S(1)} %stack.67.pos, bf16[512,1024]{1,0:T(8,128)(2,1)} %refs_0_, bf16[512,1024]{1,0:T(8,128)(2,1)} %collective-permute-done.8.refs_1_, bf16[512,1024]{1,0:T(8,128)(2,1)S(1)} %copy-done.3, ...), custom_call_target="tpu_custom_call" | custom-call | flops 1073741824 | bytes 11534336 | tf_op jit(solution)/shard_map/pallas_call | solution.py:76
  111.0 2.6 %collective-permute-start.20 = (bf16[512,1024]{1,0:T(8,128)(2,1)S(1)}, bf16[512,1024]{1,0:T(8,128)(2,1)S(1)}, u32[]{:S(2)}, u32[]{:S(2)}) collective-permute-start(bf16[512,1024]{1,0:T(8,128)(2,1)S(1)} %add_convert_fusion.1.refs_0_), channel_id=1, source_target_pairs={{0,6},{1,7},{2,0},{3,1},{4,2},{5,3},{6,4},{7,5},{8,14},{9,15},{10,... | collective-permute-start | bytes 3145736 | tf_op jit(solution)/shard_map/ppermute | solution.py:33
  113.6 2.5 %collective-permute-start.18 = (bf16[512,1024]{1,0:T(8,128)(2,1)S(1)}, bf16[512,1024]{1,0:T(8,128)(2,1)S(1)}, u32[]{:S(2)}, u32[]{:S(2)}) collective-permute-start(bf16[512,1024]{1,0:T(8,128)(2,1)S(1)} %shard_map.88.refs_0_), channel_id=1, source_target_pairs={{0,48},{1,49},{2,50},{3,51},{4,52},{5,53},{6,54},{7,55},{8,56},{9,... | collective-permute-start | bytes 3145736 | tf_op jit(solution)/shard_map/ppermute | solution.py:33
  116.1 20.2 %collective-permute-done.28.refs_3_ = bf16[512,1024]{1,0:T(8,128)(2,1)S(1)} collective-permute-done((bf16[512,1024]{1,0:T(8,128)(2,1)S(1)}, bf16[512,1024]{1,0:T(8,128)(2,1)S(1)}, u32[]{:S(2)}, u32[]{:S(2)}) %collective-permute-start.28) | collective-permute-done | bytes 1048608 | tf_op jit(solution)/shard_map/ppermute | solution.py:33
  136.5 2.7 %collective-permute-start.30 = (bf16[512,1024]{1,0:T(8,128)(2,1)S(1)}, bf16[512,1024]{1,0:T(8,128)(2,1)S(1)}, u32[]{:S(2)}, u32[]{:S(2)}) collective-permute-start(bf16[512,1024]{1,0:T(8,128)(2,1)S(1)} %collective-permute-done.28.refs_3_), channel_id=1, source_target_pairs={{0,48},{1,49},{2,50},{3,51},{4,52},{5,53},{6,54},{7,55},{8,56},{9,... | collective-permute-start | bytes 3145736 | tf_op jit(solution)/shard_map/ppermute | solution.py:33
  142.3 18.8 %collective-permute-done.29.refs_4_ = bf16[512,1024]{1,0:T(8,128)(2,1)S(1)} collective-permute-done((bf16[512,1024]{1,0:T(8,128)(2,1)S(1)}, bf16[512,1024]{1,0:T(8,128)(2,1)S(1)}, u32[]{:S(2)}, u32[]{:S(2)}) %collective-permute-start.29) | collective-permute-done | bytes 1048608 | tf_op jit(solution)/shard_map/ppermute | solution.py:33
  166.8 10.3 %shard_map.92 = (bf16[512,1024]{1,0:T(8,128)(2,1)S(1)}, bf16[512,1024]{1,0:T(8,128)(2,1)S(1)}) custom-call(s32[2,8,6,16]{3,2,1,0:T(8,128)S(1)} %pad_add_fusion.table, s32[8]{0:T(128)S(1)} %stack.67.pos, bf16[512,1024]{1,0:T(8,128)(2,1)S(1)} %shard_map.88.refs_0_, bf16[512,1024]{1,0:T(8,128)(2,1)S(1)} %collective-permute-done.27.refs_1_, ...), custom_call_target="tpu_custom_call" | custom-call | flops 805306368 | bytes 10485760 | tf_op jit(solution)/shard_map/pallas_call | solution.py:76
  177.1 5.3 %shard_map.90.refs_5_ = bf16[512,1024]{1,0:T(8,128)(2,1)S(1)} custom-call(s32[2,8,6,16]{3,2,1,0:T(8,128)S(1)} %pad_add_fusion.table, s32[8]{0:T(128)S(1)} %stack.67.pos, bf16[512,1024]{1,0:T(8,128)(2,1)S(1)} %add_convert_fusion.1.refs_0_, bf16[512,1024]{1,0:T(8,128)(2,1)S(1)} %collective-permute-done.19.refs_1_, ...), custom_call_target="tpu_custom_call" | custom-call | flops 671088640 | bytes 8388608 | tf_op jit(solution)/shard_map/pallas_call | solution.py:76
  184.8 4.6 %shard_map.93 = (f32[512,1024]{1,0:T(8,128)S(1)}, bf16[512,1024]{1,0:T(8,128)(2,1)S(1)}) custom-call(s32[2,8,6,16]{3,2,1,0:T(8,128)S(1)} %pad_add_fusion.table, s32[8]{0:T(128)S(1)} %stack.67.pos, bf16[512,1024]{1,0:T(8,128)(2,1)S(1)} %collective-permute-done.31.refs_0_, bf16[512,1024]{1,0:T(8,128)(2,1)S(1)} %collective-permute-done.32.refs_1_, ...), custom_call_target="tpu_custom_call" | custom-call | flops 268435456 | bytes 9437184 | tf_op jit(solution)/shard_map/pallas_call | solution.py:76
  189.4 3.5 %collective-permute-start.33 = (bf16[512,1024]{1,0:T(8,128)(2,1)S(1)}, bf16[512,1024]{1,0:T(8,128)(2,1)S(1)}, u32[]{:S(2)}, u32[]{:S(2)}) collective-permute-start(bf16[512,1024]{1,0:T(8,128)(2,1)S(1)} %get-tuple-element.95), channel_id=1, source_target_pairs={{0,8},{1,9},{2,10},{3,11},{4,12},{5,13},{6,14},{7,15},{8,0},{9,1},... | collective-permute-start | bytes 3145736 | tf_op jit(solution)/shard_map/ppermute | solution.py:33
  192.9 4.9 %shard_map.91 = bf16[512,1024]{1,0:T(8,128)(2,1)} custom-call(s32[2,8,6,16]{3,2,1,0:T(8,128)S(1)} %pad_add_fusion.table, s32[8]{0:T(128)S(1)} %stack.67.pos, bf16[512,1024]{1,0:T(8,128)(2,1)S(1)} %collective-permute-done.24.refs_0_, bf16[512,1024]{1,0:T(8,128)(2,1)S(1)} %collective-permute-done.25.refs_1_, ...), custom_call_target="tpu_custom_call" | custom-call | flops 402653184 | bytes 7340032 | tf_op jit(solution)/shard_map/pallas_call | solution.py:76
  (90 shorter events, 38.0 us)
Async XLA Ops:
  2.4 29.4 %collective-permute-start.2 = (bf16[4624,128]{1,0:T(8,128)(2,1)S(1)}, bf16[4624,128]{1,0:T(8,128)(2,1)}, u32[]{:S(2)}, u32[]{:S(2)}) collective-permute-start(bf16[4624,128]{1,0:T(8,128)(2,1)S(1)} %pad_maximum_fusion.refs_0_), channel_id=1, source_target_pairs={{0,64},{1,65},{2,66},{3,67},{4,68},{5,69},{6,70},{7,71},{8,72},{9,... | collective-permute-start | bytes 3551240 | tf_op jit(solution)/shard_map/ppermute | solution.py:33
  6.2 26.9 %collective-permute-start.1 = (bf16[4624,128]{1,0:T(8,128)(2,1)S(1)}, bf16[4624,128]{1,0:T(8,128)(2,1)S(1)}, u32[]{:S(2)}, u32[]{:S(2)}) collective-permute-start(bf16[4624,128]{1,0:T(8,128)(2,1)S(1)} %pad_maximum_fusion.refs_0_), channel_id=1, source_target_pairs={{0,48},{1,49},{2,50},{3,51},{4,52},{5,53},{6,54},{7,55},{8,56},{9,... | collective-permute-start | bytes 3551240 | tf_op jit(solution)/shard_map/ppermute | solution.py:33
  8.7 27.6 %collective-permute-start = (bf16[4624,128]{1,0:T(8,128)(2,1)S(1)}, bf16[4624,128]{1,0:T(8,128)(2,1)}, u32[]{:S(2)}, u32[]{:S(2)}) collective-permute-start(bf16[4624,128]{1,0:T(8,128)(2,1)S(1)} %pad_maximum_fusion.refs_0_), channel_id=1, source_target_pairs={{0,16},{1,17},{2,18},{3,19},{4,20},{5,21},{6,22},{7,23},{8,24},{9,... | collective-permute-start | bytes 3551240 | tf_op jit(solution)/shard_map/ppermute | solution.py:33
  8.7 29.1 %collective-permute-start.8 = (bf16[512,1024]{1,0:T(8,128)(2,1)}, bf16[512,1024]{1,0:T(8,128)(2,1)}, u32[]{:S(2)}, u32[]{:S(2)}) collective-permute-start(bf16[512,1024]{1,0:T(8,128)(2,1)} %refs_0_), channel_id=1, source_target_pairs={{0,2},{1,3},{2,4},{3,5},{4,6},{5,7},{6,0},{7,1},{8,10},{9,11},{10,... | collective-permute-start | bytes 3145736 | tf_op jit(solution)/shard_map/ppermute | solution.py:33
  10.3 27.5 %collective-permute-start.9 = (bf16[512,1024]{1,0:T(8,128)(2,1)}, bf16[512,1024]{1,0:T(8,128)(2,1)S(1)}, u32[]{:S(2)}, u32[]{:S(2)}) collective-permute-start(bf16[512,1024]{1,0:T(8,128)(2,1)} %refs_0_), channel_id=1, source_target_pairs={{0,6},{1,7},{2,0},{3,1},{4,2},{5,3},{6,4},{7,5},{8,14},{9,15},{10,... | collective-permute-start | bytes 3145736 | tf_op jit(solution)/shard_map/ppermute | solution.py:33
  36.3 29.9 %collective-permute-start.4 = (bf16[4624,128]{1,0:T(8,128)(2,1)}, bf16[4624,128]{1,0:T(8,128)(2,1)}, u32[]{:S(2)}, u32[]{:S(2)}) collective-permute-start(bf16[4624,128]{1,0:T(8,128)(2,1)} %collective-permute-done.2.refs_4_), channel_id=1, source_target_pairs={{0,48},{1,49},{2,50},{3,51},{4,52},{5,53},{6,54},{7,55},{8,56},{9,... | collective-permute-start | bytes 3551240 | tf_op jit(solution)/shard_map/ppermute | solution.py:33
  36.6 29.6 %collective-permute-start.3 = (bf16[4624,128]{1,0:T(8,128)(2,1)}, bf16[4624,128]{1,0:T(8,128)(2,1)}, u32[]{:S(2)}, u32[]{:S(2)}) collective-permute-start(bf16[4624,128]{1,0:T(8,128)(2,1)} %collective-permute-done.refs_3_), channel_id=1, source_target_pairs={{0,16},{1,17},{2,18},{3,19},{4,20},{5,21},{6,22},{7,23},{8,24},{9,... | collective-permute-start | bytes 3551240 | tf_op jit(solution)/shard_map/ppermute | solution.py:33
  39.2 24.5 %collective-permute-start.11 = (bf16[512,1024]{1,0:T(8,128)(2,1)}, bf16[512,1024]{1,0:T(8,128)(2,1)}, u32[]{:S(2)}, u32[]{:S(2)}) collective-permute-start(bf16[512,1024]{1,0:T(8,128)(2,1)} %collective-permute-done.8.refs_1_), channel_id=1, source_target_pairs={{0,2},{1,3},{2,4},{3,5},{4,6},{5,7},{6,0},{7,1},{8,10},{9,11},{10,... | collective-permute-start | bytes 3145736 | tf_op jit(solution)/shard_map/ppermute | solution.py:33
  40.8 24.4 %collective-permute-start.5 = (bf16[4,8,128,128]{3,2,1,0:T(8,128)(2,1)S(1)}, bf16[4,8,128,128]{3,2,1,0:T(8,128)(2,1)S(1)}, u32[]{:S(2)}, u32[]{:S(2)}) collective-permute-start(bf16[4,8,128,128]{3,2,1,0:T(8,128)(2,1)S(1)} %copy-done.1), channel_id=1, source_target_pairs={{0,8},{1,9},{2,10},{3,11},{4,12},{5,13},{6,14},{7,15},{8,0},{9,1},... | collective-permute-start | bytes 3145736 | tf_op jit(solution)/shard_map/ppermute | solution.py:33
  66.3 24.5 %collective-permute-start.6 = (bf16[4624,128]{1,0:T(8,128)(2,1)}, bf16[4624,128]{1,0:T(8,128)(2,1)S(1)}, u32[]{:S(2)}, u32[]{:S(2)}) collective-permute-start(bf16[4624,128]{1,0:T(8,128)(2,1)} %collective-permute-done.2.refs_4_), channel_id=1, source_target_pairs={{0,16},{1,17},{2,18},{3,19},{4,20},{5,21},{6,22},{7,23},{8,24},{9,... | collective-permute-start | bytes 3551240 | tf_op jit(solution)/shard_map/ppermute | solution.py:33
  66.6 24.2 %collective-permute-start.7 = (bf16[4624,128]{1,0:T(8,128)(2,1)}, bf16[4624,128]{1,0:T(8,128)(2,1)S(1)}, u32[]{:S(2)}, u32[]{:S(2)}) collective-permute-start(bf16[4624,128]{1,0:T(8,128)(2,1)} %collective-permute-done.4.refs_5_), channel_id=1, source_target_pairs={{0,48},{1,49},{2,50},{3,51},{4,52},{5,53},{6,54},{7,55},{8,56},{9,... | collective-permute-start | bytes 3551240 | tf_op jit(solution)/shard_map/ppermute | solution.py:33
  109.9 26.4 %collective-permute-start.28 = (bf16[512,1024]{1,0:T(8,128)(2,1)S(1)}, bf16[512,1024]{1,0:T(8,128)(2,1)S(1)}, u32[]{:S(2)}, u32[]{:S(2)}) collective-permute-start(bf16[512,1024]{1,0:T(8,128)(2,1)S(1)} %shard_map.88.refs_0_), channel_id=1, source_target_pairs={{0,64},{1,65},{2,66},{3,67},{4,68},{5,69},{6,70},{7,71},{8,72},{9,... | collective-permute-start | bytes 3145736 | tf_op jit(solution)/shard_map/ppermute | solution.py:33
  111.0 25.5 %collective-permute-start.27 = (bf16[512,1024]{1,0:T(8,128)(2,1)S(1)}, bf16[512,1024]{1,0:T(8,128)(2,1)S(1)}, u32[]{:S(2)}, u32[]{:S(2)}) collective-permute-start(bf16[512,1024]{1,0:T(8,128)(2,1)S(1)} %shard_map.88.refs_0_), channel_id=1, source_target_pairs={{0,16},{1,17},{2,18},{3,19},{4,20},{5,21},{6,22},{7,23},{8,24},{9,... | collective-permute-start | bytes 3145736 | tf_op jit(solution)/shard_map/ppermute | solution.py:33
  111.0 28.2 %collective-permute-start.20 = (bf16[512,1024]{1,0:T(8,128)(2,1)S(1)}, bf16[512,1024]{1,0:T(8,128)(2,1)S(1)}, u32[]{:S(2)}, u32[]{:S(2)}) collective-permute-start(bf16[512,1024]{1,0:T(8,128)(2,1)S(1)} %add_convert_fusion.1.refs_0_), channel_id=1, source_target_pairs={{0,6},{1,7},{2,0},{3,1},{4,2},{5,3},{6,4},{7,5},{8,14},{9,15},{10,... | collective-permute-start | bytes 3145736 | tf_op jit(solution)/shard_map/ppermute | solution.py:33
  113.6 25.6 %collective-permute-start.19 = (bf16[512,1024]{1,0:T(8,128)(2,1)S(1)}, bf16[512,1024]{1,0:T(8,128)(2,1)S(1)}, u32[]{:S(2)}, u32[]{:S(2)}) collective-permute-start(bf16[512,1024]{1,0:T(8,128)(2,1)S(1)} %add_convert_fusion.1.refs_0_), channel_id=1, source_target_pairs={{0,2},{1,3},{2,4},{3,5},{4,6},{5,7},{6,0},{7,1},{8,10},{9,11},{10,... | collective-permute-start | bytes 3145736 | tf_op jit(solution)/shard_map/ppermute | solution.py:33
  113.6 25.6 %collective-permute-start.18 = (bf16[512,1024]{1,0:T(8,128)(2,1)S(1)}, bf16[512,1024]{1,0:T(8,128)(2,1)S(1)}, u32[]{:S(2)}, u32[]{:S(2)}) collective-permute-start(bf16[512,1024]{1,0:T(8,128)(2,1)S(1)} %shard_map.88.refs_0_), channel_id=1, source_target_pairs={{0,48},{1,49},{2,50},{3,51},{4,52},{5,53},{6,54},{7,55},{8,56},{9,... | collective-permute-start | bytes 3145736 | tf_op jit(solution)/shard_map/ppermute | solution.py:33
  136.5 24.6 %collective-permute-start.29 = (bf16[512,1024]{1,0:T(8,128)(2,1)S(1)}, bf16[512,1024]{1,0:T(8,128)(2,1)S(1)}, u32[]{:S(2)}, u32[]{:S(2)}) collective-permute-start(bf16[512,1024]{1,0:T(8,128)(2,1)S(1)} %collective-permute-done.27.refs_1_), channel_id=1, source_target_pairs={{0,16},{1,17},{2,18},{3,19},{4,20},{5,21},{6,22},{7,23},{8,24},{9,... | collective-permute-start | bytes 3145736 | tf_op jit(solution)/shard_map/ppermute | solution.py:33
  136.5 24.6 %collective-permute-start.30 = (bf16[512,1024]{1,0:T(8,128)(2,1)S(1)}, bf16[512,1024]{1,0:T(8,128)(2,1)S(1)}, u32[]{:S(2)}, u32[]{:S(2)}) collective-permute-start(bf16[512,1024]{1,0:T(8,128)(2,1)S(1)} %collective-permute-done.28.refs_3_), channel_id=1, source_target_pairs={{0,48},{1,49},{2,50},{3,51},{4,52},{5,53},{6,54},{7,55},{8,56},{9,... | collective-permute-start | bytes 3145736 | tf_op jit(solution)/shard_map/ppermute | solution.py:33
  139.2 24.6 %collective-permute-start.21 = (bf16[512,1024]{1,0:T(8,128)(2,1)S(1)}, bf16[512,1024]{1,0:T(8,128)(2,1)S(1)}, u32[]{:S(2)}, u32[]{:S(2)}) collective-permute-start(bf16[512,1024]{1,0:T(8,128)(2,1)S(1)} %add_convert_fusion.1.refs_0_), channel_id=1, source_target_pairs={{0,1},{1,0},{2,3},{3,2},{4,5},{5,4},{6,7},{7,6},{8,9},{9,8},{10,11... | collective-permute-start | bytes 3145736 | tf_op jit(solution)/shard_map/ppermute | solution.py:33
  139.9 23.9 %collective-permute-start.22 = (bf16[512,1024]{1,0:T(8,128)(2,1)S(1)}, bf16[512,1024]{1,0:T(8,128)(2,1)S(1)}, u32[]{:S(2)}, u32[]{:S(2)}) collective-permute-start(bf16[512,1024]{1,0:T(8,128)(2,1)S(1)} %collective-permute-done.19.refs_1_), channel_id=1, source_target_pairs={{0,2},{1,3},{2,4},{3,5},{4,6},{5,7},{6,0},{7,1},{8,10},{9,11},{10,... | collective-permute-start | bytes 3145736 | tf_op jit(solution)/shard_map/ppermute | solution.py:33
  161.1 23.7 %collective-permute-start.31 = (bf16[512,1024]{1,0:T(8,128)(2,1)S(1)}, bf16[512,1024]{1,0:T(8,128)(2,1)S(1)}, u32[]{:S(2)}, u32[]{:S(2)}) collective-permute-start(bf16[512,1024]{1,0:T(8,128)(2,1)S(1)} %collective-permute-done.28.refs_3_), channel_id=1, source_target_pairs={{0,16},{1,17},{2,18},{3,19},{4,20},{5,21},{6,22},{7,23},{8,24},{9,... | collective-permute-start | bytes 3145736 | tf_op jit(solution)/shard_map/ppermute | solution.py:33
  163.8 29.1 %collective-permute-start.25 = (bf16[512,1024]{1,0:T(8,128)(2,1)S(1)}, bf16[512,1024]{1,0:T(8,128)(2,1)S(1)}, u32[]{:S(2)}, u32[]{:S(2)}) collective-permute-start(bf16[512,1024]{1,0:T(8,128)(2,1)S(1)} %collective-permute-done.21.refs_3_), channel_id=1, source_target_pairs={{0,6},{1,7},{2,0},{3,1},{4,2},{5,3},{6,4},{7,5},{8,14},{9,15},{10,... | collective-permute-start | bytes 3145736 | tf_op jit(solution)/shard_map/ppermute | solution.py:33
  166.2 26.6 %collective-permute-start.24 = (bf16[512,1024]{1,0:T(8,128)(2,1)S(1)}, bf16[512,1024]{1,0:T(8,128)(2,1)S(1)}, u32[]{:S(2)}, u32[]{:S(2)}) collective-permute-start(bf16[512,1024]{1,0:T(8,128)(2,1)S(1)} %collective-permute-done.21.refs_3_), channel_id=1, source_target_pairs={{0,2},{1,3},{2,4},{3,5},{4,6},{5,7},{6,0},{7,1},{8,10},{9,11},{10,... | collective-permute-start | bytes 3145736 | tf_op jit(solution)/shard_map/ppermute | solution.py:33
  166.2 26.6 %collective-permute-start.26 = (bf16[512,1024]{1,0:T(8,128)(2,1)S(1)}, bf16[512,1024]{1,0:T(8,128)(2,1)S(1)}, u32[]{:S(2)}, u32[]{:S(2)}) collective-permute-start(bf16[512,1024]{1,0:T(8,128)(2,1)S(1)} %collective-permute-done.22.refs_4_), channel_id=1, source_target_pairs={{0,1},{1,0},{2,3},{3,2},{4,5},{5,4},{6,7},{7,6},{8,9},{9,8},{10,11... | collective-permute-start | bytes 3145736 | tf_op jit(solution)/shard_map/ppermute | solution.py:33
  (20 other events, 254.2 us)

commit v6 on v5

--- a/solution.py
+++ b/solution.py
@@ -294,8 +294,8 @@
     la2, lyb = send(la, up_x), send(ly, down_x)
     xy, xa2 = send(x, other_yl), send(xa, up_z)
     z_sib = send(z, other_core)
-    la2, ly, lyb, z_sib = after(la2, ly, lyb, z_sib)
-    xy, xa2 = after(xy, xa2)
+    ly, lyb = after(ly, lyb)
+    la2, z_sib, xy, xa2 = after(la2, z_sib, xy, xa2)
     lya, lyb2 = send(ly, up_x), send(lyb, down_x)
     xya, xyb, xya2 = send(xy, up_z), send(xy, down_z), send(xa2, other_yl)
 
@@ -366,8 +366,8 @@
         scratch = [pltpu.VMEM((512, 1024), F32)]
         return part(h_perp_kernel, at, blocks, (slots_zc, slots_zc_sib), before, last, [BF], scratch, 12 + len(blocks))
 
-    va2, vy, vyb = after(va2, vy, vyb)
-    wy, wa2, slots_zc_sib = after(wy, wa2, slots_zc_sib)
+    vy, vyb = after(vy, vyb)
+    va2, wy, wa2, slots_zc_sib = after(va2, wy, wa2, slots_zc_sib)
     vya, vyb2 = send(vy, up_x), send(vyb, down_x)
     wya, wyb, wya2 = send(wy, up_z), send(wy, down_z), send(wa2, other_yl)
     xs = x_part({OWN: v, UP: va, DOWN: vb, PAIR: vy, FAR: va2, PAIR_DOWN: vyb}, [], False)

time: 200 us -> 204 us (1.020)
  waiting for transfers between devices: 98.7 us -> 102 us
    ppermute x34, waiting for transfers between devices: 98.7 us -> 102 us  [send(): lax.ppermute(value, AXES, [(number(*at), number(*to(*at))) for at in plac...]
  transfers between devices with their start and end apart: 34 -> 34, of which waited for: 13 -> 14; matrix products, arithmetic and copies ran while one was open for 3% -> 3% of each run, Pallas kernels for 19% -> 19%
where the time goes in v6:
time: 204 us; the launch traced here: 203 us
  waiting for transfers between devices  102 us (50%)
  starting transfers between devices  49.2 us (24%)
  Pallas kernels  40.6 us (20%)
  local copies, waits for them, and re-layouts  8 us (4%)
    ppermute x34, waiting for transfers between devices, send(): lax.ppermute(value, AXES, [(number(*at), number(*to(*at))) for at in plac...  102 us
    ppermute x34, starting transfers between devices, send(): lax.ppermute(value, AXES, [(number(*at), number(*to(*at))) for at in plac...  49.2 us
    pallas_call x8, Pallas kernels, vmem_call(): pl.pallas_call(kernel, out_shape=out_shape, grid_spec=pltpu.PrefetchScala...  40.6 us
    unnamed x27, local copies, waits for them, and re-layouts  5.83 us
  transfers between devices with their start and end apart: 34, of which 14 were waited for; matrix products, arithmetic and copies ran while one was open for 3% of the time, Pallas kernels for 19%

profile of v6, /device:TPU:1, one launch (start us, length us, event | category | flops | bytes accessed | tf_op | source)
XLA Modules:
  0.0 202.6 jit_solution(15872239696126811242)
XLA Ops:
  2.4 3.8 %collective-permute-start.2 = (bf16[4624,128]{1,0:T(8,128)(2,1)S(1)}, bf16[4624,128]{1,0:T(8,128)(2,1)}, u32[]{:S(2)}, u32[]{:S(2)}) collective-permute-start(bf16[4624,128]{1,0:T(8,128)(2,1)S(1)} %pad_maximum_fusion.refs_0_), channel_id=1, source_target_pairs={{0,64},{1,65},{2,66},{3,67},{4,68},{5,69},{6,70},{7,71},{8,72},{9,... | collective-permute-start | bytes 3551240 | tf_op jit(solution)/shard_map/ppermute | solution.py:33
  6.2 2.5 %collective-permute-start.1 = (bf16[4624,128]{1,0:T(8,128)(2,1)S(1)}, bf16[4624,128]{1,0:T(8,128)(2,1)S(1)}, u32[]{:S(2)}, u32[]{:S(2)}) collective-permute-start(bf16[4624,128]{1,0:T(8,128)(2,1)S(1)} %pad_maximum_fusion.refs_0_), channel_id=1, source_target_pairs={{0,48},{1,49},{2,50},{3,51},{4,52},{5,53},{6,54},{7,55},{8,56},{9,... | collective-permute-start | bytes 3551240 | tf_op jit(solution)/shard_map/ppermute | solution.py:33
  12.5 19.4 %collective-permute-done.2.refs_4_ = bf16[4624,128]{1,0:T(8,128)(2,1)} collective-permute-done((bf16[4624,128]{1,0:T(8,128)(2,1)S(1)}, bf16[4624,128]{1,0:T(8,128)(2,1)}, u32[]{:S(2)}, u32[]{:S(2)}) %collective-permute-start.2) | collective-permute-done | bytes 1183776 | tf_op jit(solution)/shard_map/ppermute | solution.py:33
  33.1 3.2 %collective-permute-done.refs_3_ = bf16[4624,128]{1,0:T(8,128)(2,1)} collective-permute-done((bf16[4624,128]{1,0:T(8,128)(2,1)S(1)}, bf16[4624,128]{1,0:T(8,128)(2,1)}, u32[]{:S(2)}, u32[]{:S(2)}) %collective-permute-start) | collective-permute-done | bytes 1183776 | tf_op jit(solution)/shard_map/ppermute | solution.py:33
  36.3 2.7 %collective-permute-start.9 = (bf16[4624,128]{1,0:T(8,128)(2,1)}, bf16[4624,128]{1,0:T(8,128)(2,1)}, u32[]{:S(2)}, u32[]{:S(2)}) collective-permute-start(bf16[4624,128]{1,0:T(8,128)(2,1)} %collective-permute-done.2.refs_4_), channel_id=1, source_target_pairs={{0,48},{1,49},{2,50},{3,51},{4,52},{5,53},{6,54},{7,55},{8,56},{9,... | collective-permute-start | bytes 3551240 | tf_op jit(solution)/shard_map/ppermute | solution.py:33
  42.0 3.3 %collective-permute-start.4 = (bf16[4,8,128,128]{3,2,1,0:T(8,128)(2,1)S(1)}, bf16[4,8,128,128]{3,2,1,0:T(8,128)(2,1)S(1)}, u32[]{:S(2)}, u32[]{:S(2)}) collective-permute-start(bf16[4,8,128,128]{3,2,1,0:T(8,128)(2,1)S(1)} %copy-done.1), channel_id=1, source_target_pairs={{0,8},{1,9},{2,10},{3,11},{4,12},{5,13},{6,14},{7,15},{8,0},{9,1},... | collective-permute-start | bytes 3145736 | tf_op jit(solution)/shard_map/ppermute | solution.py:33
  46.8 15.5 %collective-permute-done.7.refs_3_ = bf16[512,1024]{1,0:T(8,128)(2,1)} collective-permute-done((bf16[512,1024]{1,0:T(8,128)(2,1)}, bf16[512,1024]{1,0:T(8,128)(2,1)}, u32[]{:S(2)}, u32[]{:S(2)}) %collective-permute-start.7) | collective-permute-done | bytes 1048608 | tf_op jit(solution)/shard_map/ppermute | solution.py:33
  62.2 2.7 %collective-permute-done.8.refs_4_ = bf16[512,1024]{1,0:T(8,128)(2,1)} collective-permute-done((bf16[512,1024]{1,0:T(8,128)(2,1)}, bf16[512,1024]{1,0:T(8,128)(2,1)}, u32[]{:S(2)}, u32[]{:S(2)}) %collective-permute-start.8) | collective-permute-done | bytes 1048608 | tf_op jit(solution)/shard_map/ppermute | solution.py:33
  67.0 2.7 %collective-permute-start.11 = (bf16[4624,128]{1,0:T(8,128)(2,1)}, bf16[4624,128]{1,0:T(8,128)(2,1)S(1)}, u32[]{:S(2)}, u32[]{:S(2)}) collective-permute-start(bf16[4624,128]{1,0:T(8,128)(2,1)} %collective-permute-done.9.refs_5_), channel_id=1, source_target_pairs={{0,48},{1,49},{2,50},{3,51},{4,52},{5,53},{6,54},{7,55},{8,56},{9,... | collective-permute-start | bytes 3551240 | tf_op jit(solution)/shard_map/ppermute | solution.py:33
  74.2 3.5 %shard_map.86.refs_2_ = f32[1024,1024]{1,0:T(8,128)S(1)} custom-call(s32[1,8,6,16]{3,2,1,0:T(8,128)S(1)} %convert_element_type.29.table, s32[8]{0:T(128)S(1)} %stack.67.pos, bf16[4624,128]{1,0:T(8,128)(2,1)} %copy-done.4, bf16[4624,128]{1,0:T(8,128)(2,1)} %copy-done.5, bf16[4624,128]{1,0:T(8,128)(2,1)} %collective-permute-done.3.refs_2_, ...), custom_call_target="tpu_custom_call" | custom-call | flops 100663296 | bytes 11296768 | tf_op jit(solution)/shard_map/pallas_call | solution.py:76
  77.7 12.7 %collective-permute-done.14.refs_7_ = bf16[512,1024]{1,0:T(8,128)(2,1)S(1)} collective-permute-done((bf16[512,1024]{1,0:T(8,128)(2,1)}, bf16[512,1024]{1,0:T(8,128)(2,1)S(1)}, u32[]{:S(2)}, u32[]{:S(2)}) %collective-permute-start.14) | collective-permute-done | bytes 1048608 | tf_op jit(solution)/shard_map/ppermute | solution.py:33
  94.9 4.6 %collective-permute-start.15 = (s32[8,6,16]{2,1,0:T(8,128)S(1)}, s32[8,6,16]{2,1,0:T(8,128)S(1)}, u32[]{:S(2)}, u32[]{:S(2)}) collective-permute-start(s32[8,6,16]{2,1,0:T(8,128)S(1)} %get-tuple-element.97), channel_id=1, source_target_pairs={{0,8},{1,9},{2,10},{3,11},{4,12},{5,13},{6,14},{7,15},{8,0},{9,1},... | collective-permute-start | bytes 9224 | tf_op jit(solution)/shard_map/ppermute | solution.py:33
  100.4 3.1 %shard_map.89 = (f32[512,1024]{1,0:T(8,128)S(1)}, bf16[512,1024]{1,0:T(8,128)(2,1)S(1)}) custom-call(s32[2,8,6,16]{3,2,1,0:T(8,128)S(1)} %pad_add_fusion.table, s32[8]{0:T(128)S(1)} %stack.67.pos, bf16[4624,128]{1,0:T(8,128)(2,1)S(1)} %collective-permute-done.11.refs_6_.refs_0_, bf16[4624,128]{1,0:T(8,128)(2,1)S(1)} %collective-permute-done.10.refs_7_.refs_1_, ...), custom_call_target="tpu_custom_call" | custom-call | flops 33554432 | bytes 9707520 | tf_op jit(solution)/shard_map/pallas_call | solution.py:76
  104.0 6.3 %shard_map.88.refs_0_ = bf16[512,1024]{1,0:T(8,128)(2,1)S(1)} custom-call(s32[2,8,6,16]{3,2,1,0:T(8,128)S(1)} %pad_add_fusion.table, s32[8]{0:T(128)S(1)} %stack.67.pos, bf16[512,1024]{1,0:T(8,128)(2,1)} %refs_0_, bf16[512,1024]{1,0:T(8,128)(2,1)} %collective-permute-done.5.refs_1_, bf16[512,1024]{1,0:T(8,128)(2,1)S(1)} %copy-done.3, ...), custom_call_target="tpu_custom_call" | custom-call | flops 1073741824 | bytes 11534336 | tf_op jit(solution)/shard_map/pallas_call | solution.py:76
  114.3 2.7 %collective-permute-start.21 = (bf16[512,1024]{1,0:T(8,128)(2,1)S(1)}, bf16[512,1024]{1,0:T(8,128)(2,1)S(1)}, u32[]{:S(2)}, u32[]{:S(2)}) collective-permute-start(bf16[512,1024]{1,0:T(8,128)(2,1)S(1)} %shard_map.88.refs_0_), channel_id=1, source_target_pairs={{0,48},{1,49},{2,50},{3,51},{4,52},{5,53},{6,54},{7,55},{8,56},{9,... | collective-permute-start | bytes 3145736 | tf_op jit(solution)/shard_map/ppermute | solution.py:33
  117.0 20.1 %collective-permute-done.19.refs_3_ = bf16[512,1024]{1,0:T(8,128)(2,1)S(1)} collective-permute-done((bf16[512,1024]{1,0:T(8,128)(2,1)S(1)}, bf16[512,1024]{1,0:T(8,128)(2,1)S(1)}, u32[]{:S(2)}, u32[]{:S(2)}) %collective-permute-start.19) | collective-permute-done | bytes 1048608 | tf_op jit(solution)/shard_map/ppermute | solution.py:33
  144.1 17.1 %collective-permute-done.30.refs_5_ = bf16[512,1024]{1,0:T(8,128)(2,1)S(1)} collective-permute-done((bf16[512,1024]{1,0:T(8,128)(2,1)S(1)}, bf16[512,1024]{1,0:T(8,128)(2,1)S(1)}, u32[]{:S(2)}, u32[]{:S(2)}) %collective-permute-start.30) | collective-permute-done | bytes 1048608 | tf_op jit(solution)/shard_map/ppermute | solution.py:33
  164.7 3.4 %collective-permute-done.20.refs_4_ = bf16[512,1024]{1,0:T(8,128)(2,1)S(1)} collective-permute-done((bf16[512,1024]{1,0:T(8,128)(2,1)S(1)}, bf16[512,1024]{1,0:T(8,128)(2,1)S(1)}, u32[]{:S(2)}, u32[]{:S(2)}) %collective-permute-start.20) | collective-permute-done | bytes 1048608 | tf_op jit(solution)/shard_map/ppermute | solution.py:33
  168.1 2.9 %collective-permute-start.28 = (bf16[512,1024]{1,0:T(8,128)(2,1)S(1)}, bf16[512,1024]{1,0:T(8,128)(2,1)S(1)}, u32[]{:S(2)}, u32[]{:S(2)}) collective-permute-start(bf16[512,1024]{1,0:T(8,128)(2,1)S(1)} %collective-permute-done.24.refs_3_), channel_id=1, source_target_pairs={{0,6},{1,7},{2,0},{3,1},{4,2},{5,3},{6,4},{7,5},{8,14},{9,15},{10,... | collective-permute-start | bytes 3145736 | tf_op jit(solution)/shard_map/ppermute | solution.py:33
  171.8 10.3 %shard_map.92 = (bf16[512,1024]{1,0:T(8,128)(2,1)S(1)}, bf16[512,1024]{1,0:T(8,128)(2,1)S(1)}) custom-call(s32[2,8,6,16]{3,2,1,0:T(8,128)S(1)} %pad_add_fusion.table, s32[8]{0:T(128)S(1)} %stack.67.pos, bf16[512,1024]{1,0:T(8,128)(2,1)S(1)} %shard_map.88.refs_0_, bf16[512,1024]{1,0:T(8,128)(2,1)S(1)} %collective-permute-done.18.refs_1_, ...), custom_call_target="tpu_custom_call" | custom-call | flops 805306368 | bytes 10485760 | tf_op jit(solution)/shard_map/pallas_call | solution.py:76
  182.1 5.3 %shard_map.90.refs_5_ = bf16[512,1024]{1,0:T(8,128)(2,1)S(1)} custom-call(s32[2,8,6,16]{3,2,1,0:T(8,128)S(1)} %pad_add_fusion.table, s32[8]{0:T(128)S(1)} %stack.67.pos, bf16[512,1024]{1,0:T(8,128)(2,1)S(1)} %add_convert_fusion.1.refs_0_, bf16[512,1024]{1,0:T(8,128)(2,1)S(1)} %collective-permute-done.22.refs_1_, ...), custom_call_target="tpu_custom_call" | custom-call | flops 671088640 | bytes 8388608 | tf_op jit(solution)/shard_map/pallas_call | solution.py:76
  187.4 3.1 %collective-permute-done.31.refs_0_ = bf16[512,1024]{1,0:T(8,128)(2,1)S(1)} collective-permute-done((bf16[512,1024]{1,0:T(8,128)(2,1)S(1)}, bf16[512,1024]{1,0:T(8,128)(2,1)S(1)}, u32[]{:S(2)}, u32[]{:S(2)}) %collective-permute-start.31) | collective-permute-done | bytes 1048608 | tf_op jit(solution)/shard_map/ppermute | solution.py:33
  190.6 4.6 %shard_map.93 = (f32[512,1024]{1,0:T(8,128)S(1)}, bf16[512,1024]{1,0:T(8,128)(2,1)S(1)}) custom-call(s32[2,8,6,16]{3,2,1,0:T(8,128)S(1)} %pad_add_fusion.table, s32[8]{0:T(128)S(1)} %stack.67.pos, bf16[512,1024]{1,0:T(8,128)(2,1)S(1)} %collective-permute-done.31.refs_0_, bf16[512,1024]{1,0:T(8,128)(2,1)S(1)} %collective-permute-done.32.refs_1_, ...), custom_call_target="tpu_custom_call" | custom-call | flops 268435456 | bytes 9437184 | tf_op jit(solution)/shard_map/pallas_call | solution.py:76
  196.3 5.0 %shard_map.91 = bf16[512,1024]{1,0:T(8,128)(2,1)} custom-call(s32[2,8,6,16]{3,2,1,0:T(8,128)S(1)} %pad_add_fusion.table, s32[8]{0:T(128)S(1)} %stack.67.pos, bf16[512,1024]{1,0:T(8,128)(2,1)S(1)} %collective-permute-done.27.refs_0_, bf16[512,1024]{1,0:T(8,128)(2,1)S(1)} %collective-permute-done.28.refs_1_, ...), custom_call_target="tpu_custom_call" | custom-call | flops 402653184 | bytes 7340032 | tf_op jit(solution)/shard_map/pallas_call | solution.py:76
  (90 shorter events, 41.3 us)
Async XLA Ops:
  2.4 29.4 %collective-permute-start.2 = (bf16[4624,128]{1,0:T(8,128)(2,1)S(1)}, bf16[4624,128]{1,0:T(8,128)(2,1)}, u32[]{:S(2)}, u32[]{:S(2)}) collective-permute-start(bf16[4624,128]{1,0:T(8,128)(2,1)S(1)} %pad_maximum_fusion.refs_0_), channel_id=1, source_target_pairs={{0,64},{1,65},{2,66},{3,67},{4,68},{5,69},{6,70},{7,71},{8,72},{9,... | collective-permute-start | bytes 3551240 | tf_op jit(solution)/shard_map/ppermute | solution.py:33
  6.2 26.9 %collective-permute-start.1 = (bf16[4624,128]{1,0:T(8,128)(2,1)S(1)}, bf16[4624,128]{1,0:T(8,128)(2,1)S(1)}, u32[]{:S(2)}, u32[]{:S(2)}) collective-permute-start(bf16[4624,128]{1,0:T(8,128)(2,1)S(1)} %pad_maximum_fusion.refs_0_), channel_id=1, source_target_pairs={{0,48},{1,49},{2,50},{3,51},{4,52},{5,53},{6,54},{7,55},{8,56},{9,... | collective-permute-start | bytes 3551240 | tf_op jit(solution)/shard_map/ppermute | solution.py:33
  8.7 27.6 %collective-permute-start = (bf16[4624,128]{1,0:T(8,128)(2,1)S(1)}, bf16[4624,128]{1,0:T(8,128)(2,1)}, u32[]{:S(2)}, u32[]{:S(2)}) collective-permute-start(bf16[4624,128]{1,0:T(8,128)(2,1)S(1)} %pad_maximum_fusion.refs_0_), channel_id=1, source_target_pairs={{0,16},{1,17},{2,18},{3,19},{4,20},{5,21},{6,22},{7,23},{8,24},{9,... | collective-permute-start | bytes 3551240 | tf_op jit(solution)/shard_map/ppermute | solution.py:33
  8.7 30.3 %collective-permute-start.5 = (bf16[512,1024]{1,0:T(8,128)(2,1)}, bf16[512,1024]{1,0:T(8,128)(2,1)}, u32[]{:S(2)}, u32[]{:S(2)}) collective-permute-start(bf16[512,1024]{1,0:T(8,128)(2,1)} %refs_0_), channel_id=1, source_target_pairs={{0,2},{1,3},{2,4},{3,5},{4,6},{5,7},{6,0},{7,1},{8,10},{9,11},{10,... | collective-permute-start | bytes 3145736 | tf_op jit(solution)/shard_map/ppermute | solution.py:33
  10.3 28.7 %collective-permute-start.6 = (bf16[512,1024]{1,0:T(8,128)(2,1)}, bf16[512,1024]{1,0:T(8,128)(2,1)S(1)}, u32[]{:S(2)}, u32[]{:S(2)}) collective-permute-start(bf16[512,1024]{1,0:T(8,128)(2,1)} %refs_0_), channel_id=1, source_target_pairs={{0,6},{1,7},{2,0},{3,1},{4,2},{5,3},{6,4},{7,5},{8,14},{9,15},{10,... | collective-permute-start | bytes 3145736 | tf_op jit(solution)/shard_map/ppermute | solution.py:33
  36.3 28.6 %collective-permute-start.3 = (bf16[4624,128]{1,0:T(8,128)(2,1)}, bf16[4624,128]{1,0:T(8,128)(2,1)}, u32[]{:S(2)}, u32[]{:S(2)}) collective-permute-start(bf16[4624,128]{1,0:T(8,128)(2,1)} %collective-permute-done.refs_3_), channel_id=1, source_target_pairs={{0,16},{1,17},{2,18},{3,19},{4,20},{5,21},{6,22},{7,23},{8,24},{9,... | collective-permute-start | bytes 3551240 | tf_op jit(solution)/shard_map/ppermute | solution.py:33
  36.3 30.7 %collective-permute-start.9 = (bf16[4624,128]{1,0:T(8,128)(2,1)}, bf16[4624,128]{1,0:T(8,128)(2,1)}, u32[]{:S(2)}, u32[]{:S(2)}) collective-permute-start(bf16[4624,128]{1,0:T(8,128)(2,1)} %collective-permute-done.2.refs_4_), channel_id=1, source_target_pairs={{0,48},{1,49},{2,50},{3,51},{4,52},{5,53},{6,54},{7,55},{8,56},{9,... | collective-permute-start | bytes 3551240 | tf_op jit(solution)/shard_map/ppermute | solution.py:33
  40.4 24.5 %collective-permute-start.8 = (bf16[512,1024]{1,0:T(8,128)(2,1)}, bf16[512,1024]{1,0:T(8,128)(2,1)}, u32[]{:S(2)}, u32[]{:S(2)}) collective-permute-start(bf16[512,1024]{1,0:T(8,128)(2,1)} %collective-permute-done.5.refs_1_), channel_id=1, source_target_pairs={{0,2},{1,3},{2,4},{3,5},{4,6},{5,7},{6,0},{7,1},{8,10},{9,11},{10,... | collective-permute-start | bytes 3145736 | tf_op jit(solution)/shard_map/ppermute | solution.py:33
  64.9 25.5 %collective-permute-start.13 = (bf16[512,1024]{1,0:T(8,128)(2,1)}, bf16[512,1024]{1,0:T(8,128)(2,1)S(1)}, u32[]{:S(2)}, u32[]{:S(2)}) collective-permute-start(bf16[512,1024]{1,0:T(8,128)(2,1)} %collective-permute-done.7.refs_3_), channel_id=1, source_target_pairs={{0,6},{1,7},{2,0},{3,1},{4,2},{5,3},{6,4},{7,5},{8,14},{9,15},{10,... | collective-permute-start | bytes 3145736 | tf_op jit(solution)/shard_map/ppermute | solution.py:33
  67.0 25.4 %collective-permute-start.10 = (bf16[4624,128]{1,0:T(8,128)(2,1)}, bf16[4624,128]{1,0:T(8,128)(2,1)S(1)}, u32[]{:S(2)}, u32[]{:S(2)}) collective-permute-start(bf16[4624,128]{1,0:T(8,128)(2,1)} %collective-permute-done.2.refs_4_), channel_id=1, source_target_pairs={{0,16},{1,17},{2,18},{3,19},{4,20},{5,21},{6,22},{7,23},{8,24},{9,... | collective-permute-start | bytes 3551240 | tf_op jit(solution)/shard_map/ppermute | solution.py:33
  67.0 25.4 %collective-permute-start.11 = (bf16[4624,128]{1,0:T(8,128)(2,1)}, bf16[4624,128]{1,0:T(8,128)(2,1)S(1)}, u32[]{:S(2)}, u32[]{:S(2)}) collective-permute-start(bf16[4624,128]{1,0:T(8,128)(2,1)} %collective-permute-done.9.refs_5_), channel_id=1, source_target_pairs={{0,48},{1,49},{2,50},{3,51},{4,52},{5,53},{6,54},{7,55},{8,56},{9,... | collective-permute-start | bytes 3551240 | tf_op jit(solution)/shard_map/ppermute | solution.py:33
  110.7 26.4 %collective-permute-start.19 = (bf16[512,1024]{1,0:T(8,128)(2,1)S(1)}, bf16[512,1024]{1,0:T(8,128)(2,1)S(1)}, u32[]{:S(2)}, u32[]{:S(2)}) collective-permute-start(bf16[512,1024]{1,0:T(8,128)(2,1)S(1)} %shard_map.88.refs_0_), channel_id=1, source_target_pairs={{0,64},{1,65},{2,66},{3,67},{4,68},{5,69},{6,70},{7,71},{8,72},{9,... | collective-permute-start | bytes 3145736 | tf_op jit(solution)/shard_map/ppermute | solution.py:33
  111.9 25.5 %collective-permute-start.18 = (bf16[512,1024]{1,0:T(8,128)(2,1)S(1)}, bf16[512,1024]{1,0:T(8,128)(2,1)S(1)}, u32[]{:S(2)}, u32[]{:S(2)}) collective-permute-start(bf16[512,1024]{1,0:T(8,128)(2,1)S(1)} %shard_map.88.refs_0_), channel_id=1, source_target_pairs={{0,16},{1,17},{2,18},{3,19},{4,20},{5,21},{6,22},{7,23},{8,24},{9,... | collective-permute-start | bytes 3145736 | tf_op jit(solution)/shard_map/ppermute | solution.py:33
  111.9 27.8 %collective-permute-start.23 = (bf16[512,1024]{1,0:T(8,128)(2,1)S(1)}, bf16[512,1024]{1,0:T(8,128)(2,1)S(1)}, u32[]{:S(2)}, u32[]{:S(2)}) collective-permute-start(bf16[512,1024]{1,0:T(8,128)(2,1)S(1)} %add_convert_fusion.1.refs_0_), channel_id=1, source_target_pairs={{0,6},{1,7},{2,0},{3,1},{4,2},{5,3},{6,4},{7,5},{8,14},{9,15},{10,... | collective-permute-start | bytes 3145736 | tf_op jit(solution)/shard_map/ppermute | solution.py:33
  114.3 25.4 %collective-permute-start.22 = (bf16[512,1024]{1,0:T(8,128)(2,1)S(1)}, bf16[512,1024]{1,0:T(8,128)(2,1)S(1)}, u32[]{:S(2)}, u32[]{:S(2)}) collective-permute-start(bf16[512,1024]{1,0:T(8,128)(2,1)S(1)} %add_convert_fusion.1.refs_0_), channel_id=1, source_target_pairs={{0,2},{1,3},{2,4},{3,5},{4,6},{5,7},{6,0},{7,1},{8,10},{9,11},{10,... | collective-permute-start | bytes 3145736 | tf_op jit(solution)/shard_map/ppermute | solution.py:33
  114.3 25.4 %collective-permute-start.21 = (bf16[512,1024]{1,0:T(8,128)(2,1)S(1)}, bf16[512,1024]{1,0:T(8,128)(2,1)S(1)}, u32[]{:S(2)}, u32[]{:S(2)}) collective-permute-start(bf16[512,1024]{1,0:T(8,128)(2,1)S(1)} %shard_map.88.refs_0_), channel_id=1, source_target_pairs={{0,48},{1,49},{2,50},{3,51},{4,52},{5,53},{6,54},{7,55},{8,56},{9,... | collective-permute-start | bytes 3145736 | tf_op jit(solution)/shard_map/ppermute | solution.py:33
  140.3 24.3 %collective-permute-start.25 = (bf16[512,1024]{1,0:T(8,128)(2,1)S(1)}, bf16[512,1024]{1,0:T(8,128)(2,1)S(1)}, u32[]{:S(2)}, u32[]{:S(2)}) collective-permute-start(bf16[512,1024]{1,0:T(8,128)(2,1)S(1)} %collective-permute-done.22.refs_1_), channel_id=1, source_target_pairs={{0,2},{1,3},{2,4},{3,5},{4,6},{5,7},{6,0},{7,1},{8,10},{9,11},{10,... | collective-permute-start | bytes 3145736 | tf_op jit(solution)/shard_map/ppermute | solution.py:33
  140.3 24.3 %collective-permute-start.26 = (bf16[8,512,128]{2,1,0:T(8,128)(2,1)S(1)}, bf16[8,512,128]{2,1,0:T(8,128)(2,1)S(1)}, u32[]{:S(2)}, u32[]{:S(2)}) collective-permute-start(bf16[8,512,128]{2,1,0:T(8,128)(2,1)S(1)} %get-tuple-element.78.refs_5_.refs_3_), channel_id=1, source_target_pairs={{0,8},{1,9},{2,10},{3,11},{4,12},{5,13},{6,14},{7,15},{8,0},{9,1},... | collective-permute-start | bytes 3145736 | tf_op jit(solution)/shard_map/ppermute | solution.py:33
  142.1 26.0 %collective-permute-start.20 = (bf16[512,1024]{1,0:T(8,128)(2,1)S(1)}, bf16[512,1024]{1,0:T(8,128)(2,1)S(1)}, u32[]{:S(2)}, u32[]{:S(2)}) collective-permute-start(bf16[512,1024]{1,0:T(8,128)(2,1)S(1)} %collective-permute-done.18.refs_1_), channel_id=1, source_target_pairs={{0,16},{1,17},{2,18},{3,19},{4,20},{5,21},{6,22},{7,23},{8,24},{9,... | collective-permute-start | bytes 3145736 | tf_op jit(solution)/shard_map/ppermute | solution.py:33
  161.2 29.3 %collective-permute-start.31 = (bf16[512,1024]{1,0:T(8,128)(2,1)S(1)}, bf16[512,1024]{1,0:T(8,128)(2,1)S(1)}, u32[]{:S(2)}, u32[]{:S(2)}) collective-permute-start(bf16[512,1024]{1,0:T(8,128)(2,1)S(1)} %collective-permute-done.19.refs_3_), channel_id=1, source_target_pairs={{0,16},{1,17},{2,18},{3,19},{4,20},{5,21},{6,22},{7,23},{8,24},{9,... | collective-permute-start | bytes 3145736 | tf_op jit(solution)/shard_map/ppermute | solution.py:33
  163.2 27.4 %collective-permute-start.32 = (bf16[512,1024]{1,0:T(8,128)(2,1)S(1)}, bf16[512,1024]{1,0:T(8,128)(2,1)S(1)}, u32[]{:S(2)}, u32[]{:S(2)}) collective-permute-start(bf16[512,1024]{1,0:T(8,128)(2,1)S(1)} %collective-permute-done.30.refs_5_), channel_id=1, source_target_pairs={{0,48},{1,49},{2,50},{3,51},{4,52},{5,53},{6,54},{7,55},{8,56},{9,... | collective-permute-start | bytes 3145736 | tf_op jit(solution)/shard_map/ppermute | solution.py:33
  168.1 28.2 %collective-permute-start.28 = (bf16[512,1024]{1,0:T(8,128)(2,1)S(1)}, bf16[512,1024]{1,0:T(8,128)(2,1)S(1)}, u32[]{:S(2)}, u32[]{:S(2)}) collective-permute-start(bf16[512,1024]{1,0:T(8,128)(2,1)S(1)} %collective-permute-done.24.refs_3_), channel_id=1, source_target_pairs={{0,6},{1,7},{2,0},{3,1},{4,2},{5,3},{6,4},{7,5},{8,14},{9,15},{10,... | collective-permute-start | bytes 3145736 | tf_op jit(solution)/shard_map/ppermute | solution.py:33
  171.0 25.3 %collective-permute-start.27 = (bf16[512,1024]{1,0:T(8,128)(2,1)S(1)}, bf16[512,1024]{1,0:T(8,128)(2,1)S(1)}, u32[]{:S(2)}, u32[]{:S(2)}) collective-permute-start(bf16[512,1024]{1,0:T(8,128)(2,1)S(1)} %collective-permute-done.24.refs_3_), channel_id=1, source_target_pairs={{0,2},{1,3},{2,4},{3,5},{4,6},{5,7},{6,0},{7,1},{8,10},{9,11},{10,... | collective-permute-start | bytes 3145736 | tf_op jit(solution)/shard_map/ppermute | solution.py:33
  171.0 25.3 %collective-permute-start.29 = (bf16[512,1024]{1,0:T(8,128)(2,1)S(1)}, bf16[512,1024]{1,0:T(8,128)(2,1)S(1)}, u32[]{:S(2)}, u32[]{:S(2)}) collective-permute-start(bf16[512,1024]{1,0:T(8,128)(2,1)S(1)} %collective-permute-done.25.refs_4_), channel_id=1, source_target_pairs={{0,1},{1,0},{2,3},{3,2},{4,5},{5,4},{6,7},{7,6},{8,9},{9,8},{10,11... | collective-permute-start | bytes 3145736 | tf_op jit(solution)/shard_map/ppermute | solution.py:33
  (20 other events, 258.3 us)
